TPU v7x, 32 devices: a whole 2x2x4 slice. The times are simulated.
32 devices in a mesh: sec: 8 (over y, x, core), lane: 4 (over z).
Axes of the slice: x: 2, y: 2, z: 4, core: 2. Of those that a mesh axis runs over, the one named last changes fastest.
Arguments:
- queries: bfloat16 [8, 384, 5120], P('sec', None, 'lane'), may hold values from -40 to 40
- key_value: bfloat16 [2048, 2, 1024], P('sec', None, 'lane'), may hold values from -6 to 6
- grad_out: bfloat16 [8, 384, 5120], P('sec', None, 'lane'), may hold values from -12 to 12
- inputs: bfloat16 [2048, 5120], P('sec'), may hold values from -6 to 6
- w_kv: bfloat16 [5120, 2, 1024], P('sec'), may hold values from -0.078125 to 0.078125
Outputs:
- grad_queries: bfloat16 [8, 384, 5120], P('sec', None, 'lane')
- grad_inputs: bfloat16 [2048, 5120], P(('sec', 'lane'))
- grad_w_kv: float32 [5120, 2, 1024], P('sec', None, 'lane')
All inputs are finite; a program needn't handle non-finite values.
Results may differ from a plain program's by a relative error of at most 0.0058.
Values may be sent and summed in bfloat16 or wider, within the bound.
No kernel may reach another device: no remote copies, remote signals or barrier semaphores. Data moves between devices by JAX's collectives and lax.ppermute only.
A program may use at most 128 MiB of HBM per device.

v0:
```python
import math

import jax
import jax.numpy as jnp
from jax import lax
from jax.sharding import PartitionSpec as P

NQH = 40
KVH = 8
HD = 128


def attend(q_rows, do_rows, k_head, v_head, last_key, block_count, softmax_scale):
    block_size = k_head.shape[0] // block_count
    k_blocks = k_head.reshape(block_count, block_size, k_head.shape[1])
    v_blocks = v_head.reshape(block_count, block_size, v_head.shape[1])
    offsets = jnp.arange(block_count, dtype=jnp.int32) * block_size
    row_count = q_rows.shape[0]

    def scores(k_block, offset):
        raw = jnp.dot(q_rows, k_block.T, preferred_element_type=jnp.float32) * softmax_scale
        visible = (offset + jnp.arange(block_size, dtype=jnp.int32))[None, :] <= last_key[:, None]
        return (raw, visible)

    def stats_step(carry, items):
        run_max, run_sum, run_dot = carry
        k_block, v_block, offset = items
        raw, visible = scores(k_block, offset)
        dprobs = jnp.dot(do_rows, v_block.T, preferred_element_type=jnp.float32)
        masked = jnp.where(visible, raw, -jnp.inf)
        new_max = jnp.maximum(run_max, jnp.max(masked, axis=1))
        factor = jnp.exp(run_max - new_max)
        weights = jnp.exp(masked - new_max[:, None])
        run_sum = run_sum * factor + jnp.sum(weights, axis=1)
        run_dot = run_dot * factor + jnp.sum(weights * dprobs, axis=1)
        return ((new_max, run_sum, run_dot), None)

    start_max = jnp.full((row_count,), -1e30, jnp.float32)
    start_zero = jnp.zeros((row_count,), jnp.float32)
    (run_max, run_sum, run_dot), _ = lax.scan(
        stats_step, (start_max, start_zero, start_zero), (k_blocks, v_blocks, offsets)
    )
    lse = run_max + jnp.log(run_sum)
    row_delta = run_dot / run_sum

    def grad_step(carry, items):
        k_block, v_block, offset = items
        raw, visible = scores(k_block, offset)
        probs = jnp.where(visible, jnp.exp(raw - lse[:, None]), 0.0)
        dprobs = jnp.dot(do_rows, v_block.T, preferred_element_type=jnp.float32)
        dscores = (probs * (dprobs - row_delta[:, None])).astype(jnp.bfloat16)
        probs_low = probs.astype(jnp.bfloat16)
        contract_rows = (((0,), (0,)), ((), ()))
        dk_block = (
            lax.dot_general(dscores, q_rows, contract_rows, preferred_element_type=jnp.float32)
            * softmax_scale
        )
        dv_block = lax.dot_general(
            probs_low, do_rows, contract_rows, preferred_element_type=jnp.float32
        )
        carry = carry + jnp.dot(dscores, k_block, preferred_element_type=jnp.float32)
        return (carry, (dk_block, dv_block))

    start_dq = jnp.zeros((row_count, k_head.shape[1]), jnp.float32)
    dq_sum, (dk_blocks, dv_blocks) = lax.scan(grad_step, start_dq, (k_blocks, v_blocks, offsets))
    head_dim = k_head.shape[1]
    return (
        dq_sum * softmax_scale,
        dk_blocks.reshape(-1, head_dim),
        dv_blocks.reshape(-1, head_dim),
    )


def local(queries, key_value, grad_out, inputs, w_kv):
    head_dim = HD
    group_size = NQH // KVH
    softmax_scale = head_dim ** (-0.5)
    gathered = lax.all_gather(key_value, "sec", axis=0, tiled=True)
    key_count = gathered.shape[0]
    heads_here = gathered.shape[2] // head_dim
    query_local = queries[0]
    grad_local = grad_out[0]
    query_count = query_local.shape[0]
    block_count = math.gcd(key_count, max(1, key_count // 512))
    last_key = (
        key_count
        - query_count
        + jnp.arange(query_count * group_size, dtype=jnp.int32) // group_size
    )
    dq_list = []
    dk_list = []
    dv_list = []
    for kv_head in range(heads_here):
        low = kv_head * group_size * head_dim
        high = (kv_head + 1) * group_size * head_dim
        q_rows = query_local[:, low:high].reshape(query_count * group_size, head_dim)
        do_rows = grad_local[:, low:high].reshape(query_count * group_size, head_dim)
        k_head = gathered[:, 0, kv_head * head_dim : (kv_head + 1) * head_dim]
        v_head = gathered[:, 1, kv_head * head_dim : (kv_head + 1) * head_dim]
        dq_head, dk_head, dv_head = attend(
            q_rows, do_rows, k_head, v_head, last_key, block_count, softmax_scale
        )
        dq_list.append(dq_head.reshape(query_count, group_size * head_dim))
        dk_list.append(dk_head)
        dv_list.append(dv_head)
    grad_queries = jnp.concatenate(dq_list, axis=1).astype(jnp.bfloat16)[None]
    dkv_part = jnp.stack(
        [jnp.concatenate(dk_list, axis=1), jnp.concatenate(dv_list, axis=1)], axis=1
    )
    summed = lax.psum_scatter(dkv_part, "sec", scatter_dimension=0, tiled=True)
    dkv = summed.astype(jnp.bfloat16)
    contract_first = (((0,), (0,)), ((), ()))
    contract_last = (((1,), (1,)), ((), ()))
    owned_cols = inputs.shape[1] // lax.axis_size("sec")
    input_rows = lax.all_to_all(inputs, "sec", split_axis=1, concat_axis=0, tiled=True)
    grad_piece = lax.all_gather(dkv, "sec", axis=0, tiled=True)
    piece_rows = grad_piece.shape[0]
    grad_flat = grad_piece.reshape(piece_rows, -1)
    folded = lax.dot_general(
        input_rows, grad_flat, contract_first, preferred_element_type=jnp.float32
    )
    grad_w_kv = folded.reshape(owned_cols, 2, dkv.shape[2])
    regrouped = lax.all_to_all(dkv, "lane", split_axis=0, concat_axis=2, tiled=True)
    local_flat = regrouped.reshape(regrouped.shape[0], -1)
    w_piece = lax.all_gather(w_kv, "sec", axis=0, tiled=True)
    piece_flat = w_piece.reshape(w_piece.shape[0], -1)
    grad_inputs = lax.dot_general(
        local_flat, piece_flat, contract_last, preferred_element_type=jnp.float32
    ).astype(jnp.bfloat16)
    return (grad_queries, grad_inputs, grad_w_kv)


def solution(mesh):
    in_specs = (
        P("sec", None, "lane"),
        P("sec", None, "lane"),
        P("sec", None, "lane"),
        P("sec", None),
        P("sec", None, None),
    )
    out_specs = (P("sec", None, "lane"), P(("sec", "lane"), None), P("sec", None, "lane"))
    return jax.shard_map(local, mesh=mesh, in_specs=in_specs, out_specs=out_specs, check_vma=False)
```

profile of v0, /device:TPU:0, one launch (start us, length us, event | category | flops | bytes accessed | tf_op | source)
XLA Modules:
  0.0 424.0 jit_solution(11351361141699881077)
XLA Ops:
  7.2 1.7 copy.22
  11.8 2.0 fusion.87
  15.6 25.5 %all-gather.4.cloned.1.call-done = bf16[2048,2,256]{2,0,1:T(8,128)(2,1)} async-done(((bf16[256,2,256]{2,0,1:T(8,128)(2,1)}), bf16[2048,2,256]{2,0,1:T(8,128)(2,1)}) %all-gather.4.cloned.1.call-update) | async-done | bytes 2097168 | tf_op jit(solution)/shard_map/all_gather | solution.py:78
  41.1 2.9 fusion.86
  44.0 21.2 %while.60 = (s32[]{:T(128)}, f32[1920]{0:T(1024)S(1)}, f32[1920]{0:T(1024)S(1)}, f32[1920]{0:T(1024)S(1)}, s32[4]{0:T(128)S(1)}, /*index=5*/bf16[4,512,128]{2,1,...) while((s32[]{:T(128)}, f32[1920]{0:T(1024)S(1)}, ...), condition=%wide.region_4.5_spmd.clone, body=%wide.region_0.4_spmd.clone.sunk | while | flops 512195072 | bytes 13199512 | solution.py:40
  46.9 1.8 fusion.161
  52.2 1.8 fusion.161
  57.5 1.8 fusion.161
  62.8 1.8 fusion.161
  65.2 22.2 %while.62 = (s32[]{:T(128)}, f32[1920]{0:T(1024)S(1)}, f32[1920]{0:T(1024)S(1)}, f32[1920]{0:T(1024)S(1)}, s32[4]{0:T(128)S(1)}, /*index=5*/bf16[4,512,128]{2,1,...) while((s32[]{:T(128)}, f32[1920]{0:T(1024)S(1)}, ...), condition=%wide.region_11.12_spmd.clone, body=%wide.region_7.11_spmd.clone.sunk | while | flops 512195072 | bytes 13199512 | solution.py:40
  66.5 1.8 fusion.182
  68.4 1.8 fusion.183
  72.1 1.8 fusion.182
  73.9 1.8 fusion.183
  77.6 1.8 fusion.182
  79.4 1.8 fusion.183
  83.1 1.8 fusion.182
  85.0 1.8 fusion.183
  89.5 39.6 %while.63 = (s32[]{:T(128)}, f32[1920,128]{1,0:T(8,128)S(1)}, f32[4,512,128]{2,1,0:T(8,128)}, f32[4,512,128]{2,1,0:T(8,128)}, s32[4]{0:T(128)S(1)}, /*index=5*/b...) while((s32[]{:T(128)}, f32[1920,128]{1,0:T(8,128)S(1)}, ...), condition=%wide.region_13.14_spmd.clone, body=%wide.region_12.13_spmd.clone.sunk | while | flops 1266730368 | bytes 24545488 | solution.py:65
  90.8 2.1 bitcast_select_fusion.7
  96.0 2.0 convolution_add_fusion.5
  100.7 2.1 bitcast_select_fusion.7
  105.8 2.0 convolution_add_fusion.5
  110.6 2.1 bitcast_select_fusion.7
  115.7 2.0 convolution_add_fusion.5
  120.5 2.1 bitcast_select_fusion.7
  124.0 1.7 fusion.197
  125.7 2.0 convolution_add_fusion.5
  129.1 2.6 copy.36
  131.7 2.6 copy.34
  136.3 31.1 %while.61 = (s32[]{:T(128)}, f32[1920,128]{1,0:T(8,128)S(1)}, f32[4,512,128]{2,1,0:T(8,128)}, f32[4,512,128]{2,1,0:T(8,128)}, s32[4]{0:T(128)S(1)}, /*index=5*/b...) while((s32[]{:T(128)}, f32[1920,128]{1,0:T(8,128)S(1)}, ...), condition=%wide.region_6.7_spmd.clone, body=%wide.region_5.6_spmd.clone.sunk | while | flops 1266730368 | bytes 22580404 | solution.py:65
  167.4 2.6 copy.35
  170.1 2.5 copy.33
  172.6 2.3 maximum_bitcast_fusion
  174.9 2.5 pad_maximum_fusion
  177.4 51.5 %reduce-scatter.2.cloned.1.call-done = f32[256,2,256]{0,2,1:T(8,128)} async-done(((f32[2048,2,256]{0,2,1:T(8,128)}), f32[256,2,256]{0,2,1:T(8,128)}) %reduce-scatter.2.cloned.1.call-update) | async-done | bytes 524304 | tf_op jit(solution)/shard_map/reduce_scatter | solution.py:110
  228.8 1.8 convert_element_type.26
  231.2 4.4 %copy.30 = bf16[256,5120]{0,1:T(8,128)(2,1)} copy(bf16[256,5120]{1,0:T(8,128)(2,1)} %param.16) | data formatting | bytes 5242880 | tf_op args[3]
  235.6 43.5 %all_to_all.34 = bf16[256,8,640]{0,2,1:T(8,128)(2,1)} all-to-all(bf16[256,8,640]{0,2,1:T(8,128)(2,1)} %bitcast.205), channel_id=1, replica_groups=mesh['sec'=8,'lane'=4] {'sec'}, dimensions={1} | all-to-all | bytes 5242880 | tf_op jit(solution)/shard_map/all_to_all | solution.py:115
  279.1 4.4 %copy.31 = bf16[8,256,640]{2,1,0:T(8,128)(2,1)} copy(bf16[8,256,640]{1,2,0:T(8,128)(2,1)} %bitcast.204) | data formatting | bytes 5242880 | tf_op jit(solution)/shard_map/all_to_all | solution.py:115
  284.5 4.6 %all-to-all-start = ((bf16[256,2,256]{2,1,0:T(2,128)(2,1)}), bf16[256,2,256]{2,1,0:T(2,128)(2,1)}, u32[]{:S(2)}, u32[]{:S(2)}) async-start(bf16[256,2,256]{2,1,0:T(2,128)(2,1)} %copy.27), calls=%async_computation.1 | async-start | bytes 524288 | tf_op jit(solution)/shard_map/all_to_all | solution.py:123
  292.5 2.0 pad_maximum_fusion.1
  294.5 2.5 all-to-all-done
  298.5 4.5 %fusion.91 = f32[512,640]{1,0:T(8,128)} fusion(bf16[2048,512]{0,1:T(8,128)(2,1)} %bitcast.219, bf16[2048,640]{1,0:T(8,128)(2,1)S(1)} %bitcast.214), kind=kOutput, calls=%fused_computation.131 | convolution fusion | flops 1342177280 | bytes 6029312 | tf_op jit(solution)/shard_map/dot_general | solution.py:119
  303.0 3.3 copy.32
  306.3 78.6 %all-gather.6.cloned.1.call-done = bf16[5120,2,1024]{2,1,0:T(2,128)(2,1)} async-done(((bf16[640,2,1024]{2,1,0:T(2,128)(2,1)}), bf16[5120,2,1024]{2,1,0:T(2,128)(2,1)}) %all-gather.6.cloned.1.call-update) | async-done | bytes 20971536 | tf_op jit(solution)/shard_map/all_gather | solution.py:125
  384.9 21.2 %copy.37 = bf16[640,8,2,1024]{3,1,2,0:T(8,128)(2,1)} copy(bf16[640,8,2,1024]{3,2,1,0:T(2,128)(2,1)} %bitcast.203) | data formatting | bytes 41943040
  406.0 11.5 %convolution_convert_fusion = bf16[64,5120]{1,0:T(8,128)(2,1)} fusion(bf16[64,2048]{1,0:T(8,128)(2,1)S(1)} %reshape.115, bf16[5120,2048]{1,0:T(8,128)(2,1)} %bitcast.202), kind=kOutput, calls=%fused_computation.114 | convolution fusion | flops 1342504960 | bytes 21889024 | tf_op jit(solution)/shard_map/dot_general | solution.py:127
  (168 shorter events, 88.9 us)
Async XLA Ops:
  7.2 33.9 %all-gather.4.cloned.1.call-start = ((), (), s32[]{:S(2)}) async-start(), calls=%async_computation.3 | async-start | bytes 2359296 | tf_op jit(solution)/shard_map/all_gather | solution.py:78
  8.9 219.9 %reduce-scatter.2.cloned.1.call-start = ((), (), s32[]{:S(2)}) async-start(), calls=%async_computation.4 | async-start | bytes 4718592 | tf_op jit(solution)/shard_map/reduce_scatter | solution.py:110
  94.3 3.7 copy-start
  104.2 3.7 copy-start
  114.1 3.7 copy-start
  124.0 3.7 copy-start
  129.1 7.3 %copy-start.2 = (bf16[4,512,128]{2,1,0:T(8,128)(2,1)S(1)}, bf16[4,512,128]{2,1,0:T(8,128)(2,1)}, u32[]{:S(2)}) copy-start(bf16[4,512,128]{2,1,0:T(8,128)(2,1)} %get-tuple-element.922) | copy-start | bytes 1572868
  167.4 5.2 %copy-start.1 = (f32[2048,128]{0,1:T(8,128)S(1)}, f32[2048,128]{0,1:T(8,128)}, u32[]{:S(2)}) copy-start(f32[2048,128]{0,1:T(8,128)} %copy.36) | copy-start | bytes 3145732
  177.3 121.1 %all-gather.8.cloned.1.call-start = ((), (), s32[]{:S(2)}) async-start(), calls=%async_computation.6 | async-start | bytes 2359296 | tf_op jit(solution)/shard_map/all_gather | solution.py:116
  230.6 154.2 %all-gather.6.cloned.1.call-start = ((), (), s32[]{:S(2)}) async-start(), calls=%async_computation.5 | async-start | bytes 23592960 | tf_op jit(solution)/shard_map/all_gather | solution.py:125
  279.1 4.5 %copy-start.4 = (bf16[256,2,256]{0,2,1:T(8,128)(2,1)S(1)}, bf16[256,2,256]{0,2,1:T(8,128)(2,1)}, u32[]{:S(2)}) copy-start(bf16[256,2,256]{0,2,1:T(8,128)(2,1)} %convert_element_type.26) | copy-start | bytes 786436
  284.5 12.6 %all-to-all-start = ((bf16[256,2,256]{2,1,0:T(2,128)(2,1)}), bf16[256,2,256]{2,1,0:T(2,128)(2,1)}, u32[]{:S(2)}, u32[]{:S(2)}) async-start(bf16[256,2,256]{2,1,0:T(2,128)(2,1)} %copy.27), calls=%async_computation.1 | async-start | bytes 524288 | tf_op jit(solution)/shard_map/all_to_all | solution.py:123
  289.9 8.5 %copy-start.3 = (bf16[8,256,640]{2,1,0:T(8,128)(2,1)S(1)}, bf16[8,256,640]{2,1,0:T(8,128)(2,1)}, u32[]{:S(2)}) copy-start(bf16[8,256,640]{2,1,0:T(8,128)(2,1)} %copy.31) | copy-start | bytes 7864324
Sparse Core Ops, SparseCore 0:
  10.5 30.5 all-gather.3
  177.5 51.3 reduce-scatter.1
  231.5 43.8 all-gather.7
  277.2 107.5 all-gather.5
where the time goes:
time: 426 us; the launch traced here: 424 us
  waiting for transfers between devices  159 us (37%)
  matrix products  104 us (24%)
  local copies, waits for them, and re-layouts  73.7 us (17%)
  blocking collectives  43.5 us (10%)
  other arithmetic  24.7 us (6%)
  between operations  13.9 us (3%)
  starting transfers between devices  4.76 us (1%)
    all_gather x1, waiting for transfers between devices, local(): w_piece = lax.all_gather(w_kv, 'sec', axis=0, tiled=True)  78.6 us
    reduce_scatter x1, waiting for transfers between devices, local(): summed = lax.psum_scatter(dkv_part, 'sec', scatter_dimension=0, tiled=True)  51.5 us
    all_to_all x1, blocking collectives, local(): lax.all_to_all(inputs, 'sec', split_axis=1, concat_axis=0, tiled=True)  43.5 us
    unnamed x12, local copies, waits for them, and re-layouts  30.5 us
    dot_general x16, matrix products, scores(): jnp.dot(q_rows, k_block.T, preferred_element_type=jnp.float32)  26 us
    all_gather x1, waiting for transfers between devices, local(): gathered = lax.all_gather(key_value, 'sec', axis=0, tiled=True)  25.5 us
    dot_general x8, matrix products, stats_step(): dprobs = jnp.dot(do_rows, v_block.T, preferred_element_type=jnp.float32)  14.2 us
    dot_general x8, matrix products, grad_step(): dprobs = jnp.dot(do_rows, v_block.T, preferred_element_type=jnp.float32)  13 us
  transfers between devices with their start and end apart: 5, of which 4 were waited for; matrix products, arithmetic and copies ran while one was open for 7% of the time, Pallas kernels for 0%

commit v1 on v0

v1 whole, which is shorter than its diff:
```python
import functools

import jax
import jax.numpy as jnp
from jax import lax
from jax.experimental import pallas as pl
from jax.experimental.pallas import tpu as pltpu
from jax.sharding import PartitionSpec as P

NQH = 40
KVH = 8
HD = 128
LOG2E = 1.4426950408889634
F32 = jnp.float32
BF16 = jnp.bfloat16
NN = (((1,), (0,)), ((), ()))
NT = (((1,), (1,)), ((), ()))
TN = (((0,), (0,)), ((), ()))
VMEM_BYTES = 48 * 1024 * 1024


def dot(a, b, dims):
    return lax.dot_general(a, b, dims, preferred_element_type=F32)


def params():
    return pltpu.CompilerParams(vmem_limit_bytes=VMEM_BYTES)


def exchange(x, offset, axis):
    return lax.ppermute(x, axis, [(i, i ^ offset) for i in range(lax.axis_size(axis))])


def attend_kernel(n, first, last, place, *refs):
    kv = refs[:n]
    refs = refs[n:]
    q_ref, do_ref = refs[:2]
    refs = refs[2:]
    if not first:
        before_ref = refs[0]
        refs = refs[1:]
    if last:
        dq_ref, keep_ref, send_ref, k_s, v_s, s_s, dp_s, acc = refs[-8:]
    else:
        dq_ref, acc, k_s, v_s, s_s, dp_s = refs[-6:]
    blk = kv[0].shape[0]
    qlen = q_ref.shape[0]
    scale = HD**-0.5
    first_query = n * blk - qlen
    step = pl.program_id(0)
    me = place[0]

    @pl.when(step == 0)
    def _():
        for b in range(n):
            g = lax.bitwise_xor(me, b)
            k_s[g] = kv[b][:, :HD]
            v_s[g] = kv[b][:, HD:]
        if first:
            acc[...] = jnp.zeros_like(acc)
        else:
            acc[...] = before_ref[...]

    q = q_ref[...]
    do = do_ref[...]

    def fold(x, op):
        return op(x.reshape(blk // 8, 8, qlen), axis=0)

    top = None
    for g in range(n):
        s = dot(k_s[g], q, NT)
        if (g + 1) * blk - 1 > first_query:
            key = g * blk + lax.broadcasted_iota(jnp.int32, s.shape, 0)
            row = first_query + lax.broadcasted_iota(jnp.int32, s.shape, 1)
            s = jnp.where(key <= row, s, -jnp.inf)
        s_s[g] = s
        high = fold(s, jnp.max)
        top = high if top is None else jnp.maximum(top, high)
    factor = scale * LOG2E
    top = jnp.max(top, axis=0, keepdims=True) * factor
    total = jnp.zeros((8, qlen), F32)
    weighted = jnp.zeros((8, qlen), F32)
    for g in range(n):
        p = jnp.exp2(s_s[g] * factor - top)
        s_s[g] = p
        dp = dot(v_s[g], do, NT)
        dp_s[g] = dp
        total = total + fold(p, jnp.sum)
        weighted = weighted + fold(p * dp, jnp.sum)
    inverse = 1.0 / jnp.sum(total, axis=0, keepdims=True)
    delta = jnp.sum(weighted, axis=0, keepdims=True) * inverse
    dq = None
    for g in range(n):
        p = s_s[g] * inverse
        ds = (p * (dp_s[g] - delta)).astype(BF16)
        acc[g, :, HD:] += dot(p.astype(BF16), do, NN)
        acc[g, :, :HD] += dot(ds, q, NN)
        part = dot(ds, k_s[g], TN)
        dq = part if dq is None else dq + part
    dq_ref[...] = (dq * scale).astype(BF16)

    if last:

        @pl.when(step == pl.num_programs(0) - 1)
        def _():
            for b in range(n):
                g = lax.bitwise_xor(me, b)
                dk = acc[g, :, :HD] * scale
                dv = acc[g, :, HD:]
                if b % 2:
                    send_ref[b // 2, :, :HD] = dk.astype(BF16)
                    send_ref[b // 2, :, HD:] = dv.astype(BF16)
                else:
                    keep_ref[b // 2, :, :HD] = dk
                    keep_ref[b // 2, :, HD:] = dv


def attend(place, kv, q, do, dq, before, low, count, last):
    n = len(kv)
    blk, width = kv[0].shape
    qlen = q.shape[0]
    whole = lambda shape: pl.BlockSpec(shape, lambda h, s: (0,) * len(shape))
    column = pl.BlockSpec((qlen, HD), lambda h, s: (0, low + h))
    first = before is None
    operands = [*kv, q, do]
    in_specs = [whole((blk, width))] * n + [column, column]
    if not first:
        operands.append(before)
        in_specs.append(whole((n, blk, width)))
    aliases = {}
    if dq is not None:
        aliases = {1 + len(operands): 0}
        operands.append(dq)
        in_specs.append(pl.BlockSpec(memory_space=pl.ANY))
    out_shape = [jax.ShapeDtypeStruct(q.shape, BF16)]
    out_specs = [column]
    scratch = [
        pltpu.VMEM((n, blk, HD), BF16),
        pltpu.VMEM((n, blk, HD), BF16),
        pltpu.VMEM((n, blk, qlen), F32),
        pltpu.VMEM((n, blk, qlen), F32),
    ]
    if last:
        out_shape += [
            jax.ShapeDtypeStruct((n // 2, blk, width), F32),
            jax.ShapeDtypeStruct((n // 2, blk, width), BF16),
        ]
        out_specs += [whole((n // 2, blk, width))] * 2
        scratch.append(pltpu.VMEM((n, blk, width), F32))
    else:
        out_shape.append(jax.ShapeDtypeStruct((n, blk, width), F32))
        out_specs.append(whole((n, blk, width)))
    work = count * qlen * n * blk * HD * 2 * 5
    return pl.pallas_call(
        functools.partial(attend_kernel, n, first, last),
        grid_spec=pltpu.PrefetchScalarGridSpec(
            num_scalar_prefetch=1,
            grid=(count,),
            in_specs=in_specs,
            out_specs=out_specs,
            scratch_shapes=scratch,
        ),
        out_shape=out_shape,
        input_output_aliases=aliases,
        compiler_params=params(),
        cost_estimate=pl.CostEstimate(
            flops=work * 2, bytes_accessed=8 * n * blk * width, transcendentals=0
        ),
        name="attend",
    )(place, *operands)


def pair_sum_kernel(keep_ref, got_ref, own_ref, *send_refs):
    own_ref[...] = keep_ref[0] + got_ref[0].astype(F32)
    for k, send_ref in enumerate(send_refs, 1):
        send_ref[...] = (keep_ref[k] + got_ref[k].astype(F32)).astype(BF16)


def pair_sum(keep, got):
    half, blk, width = keep.shape
    out_shape = [jax.ShapeDtypeStruct((blk, width), F32)]
    out_shape += [jax.ShapeDtypeStruct((blk, width), BF16)] * (half - 1)
    return pl.pallas_call(
        pair_sum_kernel, out_shape=out_shape, compiler_params=params(), name="pair_sum"
    )(keep, got)


def owner_sum_kernel(lanes, place, own_ref, *refs):
    got_refs = refs[: -1 - lanes]
    sum_ref, lane_refs = refs[-1 - lanes], refs[-lanes:]
    total = own_ref[...]
    for got_ref in got_refs:
        total = total + got_ref[...].astype(F32)
    sum_ref[...] = total.astype(BF16)
    rows = lane_refs[0].shape[0]
    for b, lane_ref in enumerate(lane_refs):
        start = pl.multiple_of(lax.bitwise_xor(place[1], b) * rows, rows)
        lane_ref[...] = sum_ref[pl.ds(start, rows), :]


def owner_sum(place, own, got, lanes):
    blk, width = own.shape
    out_shape = [jax.ShapeDtypeStruct((blk, width), BF16)]
    out_shape += [jax.ShapeDtypeStruct((blk // lanes, width), BF16)] * lanes
    return pl.pallas_call(
        functools.partial(owner_sum_kernel, lanes),
        in_specs=[pl.BlockSpec(memory_space=pltpu.SMEM)]
        + [pl.BlockSpec(memory_space=pltpu.VMEM)] * (1 + len(got)),
        out_shape=out_shape,
        compiler_params=params(),
        name="owner_sum",
    )(place, own, *got)


def weight_grad_kernel(heads, half, *refs):
    n = 2 * half
    x_refs, refs = refs[:n], refs[n:]
    out_ref = refs[-1]
    for a in range(heads):
        even, odd = refs[a * (half + 1) : a * (half + 1) + half], refs[a * (half + 1) + half]
        total = None
        for b in range(n):
            grads = odd[b // 2] if b % 2 else even[b // 2][...]
            part = dot(x_refs[b][...], grads, TN)
            total = part if total is None else total + part
        out_ref[:, 0, a * HD : (a + 1) * HD] = total[:, :HD]
        out_ref[:, 1, a * HD : (a + 1) * HD] = total[:, HD:]


def weight_grad(columns, gathered):
    half = len(columns) // 2
    heads = len(gathered)
    operands = list(columns)
    for blocks in gathered:
        operands += blocks
    return pl.pallas_call(
        functools.partial(weight_grad_kernel, heads, half),
        out_shape=jax.ShapeDtypeStruct((columns[0].shape[1], 2, heads * HD), F32),
        compiler_params=params(),
        name="weight_grad",
    )(*operands)


def input_grad_kernel(heads, half, lanes, place, *refs):
    block_refs, refs = refs[: heads * half], refs[heads * half :]
    w_refs, out_refs, left = refs[:2], refs[2 : 2 + half], refs[2 + half]
    me, lane = place[0], place[1]
    rows = block_refs[0].shape[1]
    width = w_refs[0].shape[0]
    features = w_refs[0].shape[1] // 2
    for a in range(heads):
        for k in range(half):
            for b in range(lanes):
                head = lax.bitwise_xor(lane, b) * heads + a
                block = block_refs[a * half + k][b]
                for c in range(2):
                    start = pl.multiple_of(c * features + head * HD, HD)
                    left[k * rows : (k + 1) * rows, pl.ds(start, HD)] = block[:, c * HD : (c + 1) * HD]
    mine = lax.rem(me, 2)
    for order, w_ref in enumerate(w_refs):
        start = pl.multiple_of(lax.bitwise_xor(mine, order) * width, HD)
        result = dot(left[...], w_ref[...], NT).astype(BF16)
        for k in range(half):
            out_refs[k][:, pl.ds(start, width)] = result[k * rows : (k + 1) * rows]


def input_grad(place, blocks, own_w, other_w):
    heads, half = len(blocks), len(blocks[0])
    lanes, rows, _ = blocks[0][0].shape
    width, features = own_w.shape
    flat = [block for head in blocks for block in head]
    return pl.pallas_call(
        functools.partial(input_grad_kernel, heads, half, lanes),
        in_specs=[pl.BlockSpec(memory_space=pltpu.SMEM)]
        + [pl.BlockSpec(memory_space=pltpu.VMEM)] * (len(flat) + 2),
        out_shape=[jax.ShapeDtypeStruct((rows, 2 * width), BF16)] * half,
        scratch_shapes=[pltpu.VMEM((half * rows, features), BF16)],
        compiler_params=params(),
        name="input_grad",
    )(place, *flat, own_w, other_w)


def lay_rows_kernel(place, *refs):
    blocks, out_ref = refs[:-1], refs[-1]
    width = blocks[0].shape[1]
    chip = lax.div(place[0], 2)
    for k, block in enumerate(blocks):
        start = pl.multiple_of(lax.bitwise_xor(chip, k) * width, HD)
        out_ref[:, pl.ds(start, width)] = block[...]


def lay_rows(place, blocks):
    rows, width = blocks[0].shape
    return pl.pallas_call(
        lay_rows_kernel,
        in_specs=[pl.BlockSpec(memory_space=pltpu.SMEM)]
        + [pl.BlockSpec(memory_space=pltpu.VMEM)] * len(blocks),
        out_shape=jax.ShapeDtypeStruct((rows, width * len(blocks)), BF16),
        compiler_params=params(),
        name="lay_rows",
    )(place, *blocks)


def local(queries, key_value, grad_out, inputs, w_kv):
    n = lax.axis_size("sec")
    lanes = lax.axis_size("lane")
    me = lax.axis_index("sec")
    place = jnp.stack([me, lax.axis_index("lane")]).astype(jnp.int32)
    heads = key_value.shape[2] // HD
    group = NQH // KVH
    half = n // 2
    q, do = queries[0], grad_out[0]

    kv = []
    for a in range(heads):
        own = jnp.concatenate([key_value[:, c, a * HD : (a + 1) * HD] for c in range(2)], axis=1)
        blocks = [own] + [exchange(own, 2 * k, "sec") for k in range(1, half)]
        kv.append([x for block in blocks for x in (block, exchange(block, 1, "sec"))])

    cols = inputs.shape[1] // n
    columns = []
    for b in range(n):
        part = lax.dynamic_slice_in_dim(inputs, lax.bitwise_xor(me, b) * cols, cols, axis=1)
        columns.append(exchange(part, b, "sec") if b else part)
    own_w = w_kv.reshape(w_kv.shape[0], -1)
    other_w = exchange(own_w, 1, "sec")

    dq = None
    sums = []
    for a in range(heads):
        pieces = [group]
        before = None
        low = a * group
        for i, count in enumerate(pieces):
            last = i == len(pieces) - 1
            out = attend(place, kv[a], q, do, dq, before, low, count, last)
            dq = out[0]
            low += count
            if not last:
                before = out[1]
        sums.append(out[1:])

    gathered, blocks = [], []
    for keep, send in sums:
        own, *sends = pair_sum(keep, exchange(send, 1, "sec"))
        got = [exchange(x, 2 * k, "sec") for k, x in enumerate(sends, 1)]
        mine, *by_lane = owner_sum(place, own, got, lanes)
        even = [mine] + [exchange(mine, 2 * k, "sec") for k in range(1, half)]
        odd = exchange(jnp.stack(even), 1, "sec")
        gathered.append([*even, odd])
        all_lanes = jnp.stack([by_lane[0]] + [exchange(by_lane[b], b, "lane") for b in range(1, lanes)])
        blocks.append([all_lanes] + [exchange(all_lanes, 2 * k, "sec") for k in range(1, half)])

    rows = input_grad(place, blocks, own_w, other_w)
    rows = [rows[0]] + [exchange(rows[k], 2 * k, "sec") for k in range(1, half)]
    grad_inputs = lay_rows(place, rows)
    grad_w_kv = weight_grad(columns, gathered)
    return dq[None], grad_inputs, grad_w_kv


def solution(mesh):
    in_specs = (
        P("sec", None, "lane"),
        P("sec", None, "lane"),
        P("sec", None, "lane"),
        P("sec", None),
        P("sec", None, None),
    )
    out_specs = (P("sec", None, "lane"), P(("sec", "lane"), None), P("sec", None, "lane"))
    return jax.shard_map(local, mesh=mesh, in_specs=in_specs, out_specs=out_specs, check_vma=False)
```

time: 426 us -> 167 us (0.39)
  matrix products: 104 us -> 0 us
  waiting for transfers between devices: 159 us -> 58.4 us
  local copies, waits for them, and re-layouts: 73.7 us -> 7.04 us
  starting transfers between devices: 4.76 us -> 55.7 us
  Pallas kernels: 0 us -> 44.9 us
  blocking collectives: 43.5 us -> 0 us
  other arithmetic: 24.7 us -> 0.29 us
  between operations: 13.9 us -> 0.81 us
    all_gather x3 -> x0, waiting for transfers between devices: 104 us -> none  [the longest x1 78.6 us: local(): w_piece = lax.all_gather(w_kv, 'sec', axis=0, tiled=True)]
    dot_general x58 -> x0, matrix products: 104 us -> none  [the longest x16 26 us: scores(): jnp.dot(q_rows, k_block.T, preferred_element_type=jnp.float32)]
    ppermute x0 -> x53, waiting for transfers between devices: none -> 58.4 us  [exchange(): lax.ppermute(x, axis, [(i, i ^ offset) for i in range(lax.axis_size(axis))])]
    ppermute x0 -> x53, starting transfers between devices: none -> 55.7 us  [exchange(): lax.ppermute(x, axis, [(i, i ^ offset) for i in range(lax.axis_size(axis))])]
    reduce_scatter x1 -> x0, waiting for transfers between devices: 51.5 us -> none  [local(): summed = lax.psum_scatter(dkv_part, 'sec', scatter_dimension=0, tiled=True)]
    pallas_call x0 -> x9, Pallas kernels: none -> 44.9 us  [the longest x2 35.1 us: attend(): pl.pallas_call(functools.partial(attend_kernel, n, first, last), grid_spe...]
    all_to_all x1 -> x0, blocking collectives: 43.5 us -> none  [local(): lax.all_to_all(inputs, 'sec', split_axis=1, concat_axis=0, tiled=True)]
    unnamed x12 -> x9, local copies, waits for them, and re-layouts: 30.5 us -> 2.7 us
  transfers between devices with their start and end apart: 5 -> 53, of which waited for: 4 -> 20; matrix products, arithmetic and copies ran while one was open for 7% -> 3% of each run, Pallas kernels for 0% -> 26%
where the time goes in v1:
time: 167 us
  waiting for transfers between devices  58.4 us (35%)
  starting transfers between devices  55.7 us (33%)
  Pallas kernels  44.9 us (27%)
  local copies, waits for them, and re-layouts  7.04 us (4%)
    ppermute x53, waiting for transfers between devices, exchange(): lax.ppermute(x, axis, [(i, i ^ offset) for i in range(lax.axis_size(axis))])  58.4 us
    ppermute x53, starting transfers between devices, exchange(): lax.ppermute(x, axis, [(i, i ^ offset) for i in range(lax.axis_size(axis))])  55.7 us
    pallas_call x2, Pallas kernels, attend(): pl.pallas_call(functools.partial(attend_kernel, n, first, last), grid_spe...  35.1 us
    pallas_call x1, Pallas kernels, input_grad(): pl.pallas_call(functools.partial(input_grad_kernel, heads, half, lanes),...  3.74 us
  transfers between devices with their start and end apart: 53, of which 20 were waited for; matrix products, arithmetic and copies ran while one was open for 3% of the time, Pallas kernels for 26%

profile of v1, /device:TPU:0, one launch (start us, length us, event | category | flops | bytes accessed | tf_op | source)
XLA Modules:
  0.0 167.2 jit_solution(9201464658792261810)
XLA Ops:
  0.6 1.6 fusion
  2.2 3.0 %collective-permute-start.1 = (bf16[256,256]{1,0:T(8,128)(2,1)S(1)}, bf16[256,256]{1,0:T(8,128)(2,1)S(1)}, u32[]{:S(2)}, u32[]{:S(2)}) collective-permute-start(bf16[256,256]{1,0:T(8,128)(2,1)S(1)} %pad_maximum_fusion.2.refs_0_), channel_id=1, source_target_pairs={{0,8},{4,12},{8,0},{12,4},{16,24},{20,28},{24,16},{28,20},{1,9},{5... | collective-permute-start | bytes 393224 | tf_op jit(solution)/shard_map/ppermute | solution.py:31
  5.2 1.5 collective-permute-start.3
  7.5 2.9 %collective-permute-start.12 = (bf16[256,256]{1,0:T(8,128)(2,1)S(1)}, bf16[256,256]{1,0:T(8,128)(2,1)S(1)}, u32[]{:S(2)}, u32[]{:S(2)}) collective-permute-start(bf16[256,256]{1,0:T(8,128)(2,1)S(1)} %pad_maximum_fusion.3.refs_0_), channel_id=1, source_target_pairs={{0,24},{4,28},{8,16},{12,20},{16,8},{20,12},{24,0},{28,4},{1,25},{... | collective-permute-start | bytes 393224 | tf_op jit(solution)/shard_map/ppermute | solution.py:31
  10.4 2.2 %collective-permute-start.5 = (bf16[256,256]{1,0:T(8,128)(2,1)S(1)}, bf16[256,256]{1,0:T(8,128)(2,1)S(1)}, u32[]{:S(2)}, u32[]{:S(2)}) collective-permute-start(bf16[256,256]{1,0:T(8,128)(2,1)S(1)} %pad_maximum_fusion.2.refs_0_), channel_id=1, source_target_pairs={{0,24},{4,28},{8,16},{12,20},{16,8},{20,12},{24,0},{28,4},{1,25},{... | collective-permute-start | bytes 393224 | tf_op jit(solution)/shard_map/ppermute | solution.py:31
  13.2 5.4 %collective-permute-done.10.refs_4_ = bf16[256,256]{1,0:T(8,128)(2,1)S(1)} collective-permute-done((bf16[256,256]{1,0:T(8,128)(2,1)S(1)}, bf16[256,256]{1,0:T(8,128)(2,1)S(1)}, u32[]{:S(2)}, u32[]{:S(2)}) %collective-permute-start.10) | collective-permute-done | bytes 131104 | tf_op jit(solution)/shard_map/ppermute | solution.py:31
  19.2 2.7 %constant_dynamic-slice_fusion = (bf16[256,640]{1,0:T(8,128)(2,1)S(1)}, bf16[256,640]{1,0:T(8,128)(2,1)S(1)}, bf16[256,640]{1,0:T(8,128)(2,1)S(1)}, bf16[256,640...) fusion(bf16[256,5120]{1,0:T(8,128)(2,1)} %param.8, ...), kind=kLoop, calls=%fused_computation.10 | loop fusion | bytes 5242912 | tf_op jit(solution)/shard_map/dynamic_slice | solution.py:324
  21.9 2.7 %copy.17 = bf16[80,8,2,1024]{3,1,2,0:T(8,128)(2,1)S(1)} copy(bf16[80,8,2,1024]{3,2,1,0:T(2,128)(2,1)} %bitcast.47) | data formatting | bytes 5242880
  25.8 17.6 %attend.2 = (bf16[384,1280]{1,0:T(8,128)(2,1)}, f32[4,256,256]{2,1,0:T(8,128)S(1)}, bf16[4,256,256]{2,1,0:T(8,128)(2,1)S(1)}) custom-call(s32[2]{0:T(128)S(1)} %pad_add_fusion.place, bf16[256,256]{1,0:T(8,128)(2,1)S(1)} %pad_maximum_fusion.3.refs_0_, bf16[256,256]{1,0:T(8,128)(2,1)S(1)} %collective-permute-done.7.refs_1_, ...), custom_call_target="tpu_custom_call" | custom-call | flops 10066329600 | bytes 4194304 | tf_op jit(solution)/shard_map/attend/pallas_call | solution.py:155
  43.9 17.6 %attend.3 = (bf16[384,1280]{1,0:T(8,128)(2,1)}, f32[4,256,256]{2,1,0:T(8,128)S(1)}, bf16[4,256,256]{2,1,0:T(8,128)(2,1)S(1)}) custom-call(s32[2]{0:T(128)S(1)} %pad_add_fusion.place, bf16[256,256]{1,0:T(8,128)(2,1)S(1)} %pad_maximum_fusion.2.refs_0_, bf16[256,256]{1,0:T(8,128)(2,1)S(1)} %collective-permute-done.refs_1_, ...), custom_call_target="tpu_custom_call", output_to_operand_aliasing={{0}: (11, {})} | custom-call | flops 10066329600 | bytes 4194304 | tf_op jit(solution)/shard_map/attend/pallas_call | solution.py:155
  61.9 1.4 collective-permute-start.40
  63.4 1.5 collective-permute-start.41
  65.0 7.5 %collective-permute-done.39.refs_2_ = bf16[256,640]{1,0:T(8,128)(2,1)S(1)} collective-permute-done((bf16[256,640]{1,0:T(8,128)(2,1)S(1)}, bf16[256,640]{1,0:T(8,128)(2,1)S(1)}, u32[]{:S(2)}, u32[]{:S(2)}) %collective-permute-start.39) | collective-permute-done | bytes 327712 | tf_op jit(solution)/shard_map/ppermute | solution.py:31
  72.5 5.3 %collective-permute-done.40.refs_3_ = bf16[256,640]{1,0:T(8,128)(2,1)S(1)} collective-permute-done((bf16[256,640]{1,0:T(8,128)(2,1)S(1)}, bf16[256,640]{1,0:T(8,128)(2,1)S(1)}, u32[]{:S(2)}, u32[]{:S(2)}) %collective-permute-start.40) | collective-permute-done | bytes 327712 | tf_op jit(solution)/shard_map/ppermute | solution.py:31
  77.8 1.5 collective-permute-start.16
  79.3 1.2 collective-permute-start.17
  80.6 0.8 collective-permute-done.15.refs_0_
  81.7 3.6 %collective-permute-done.16.refs_1_ = bf16[256,256]{1,0:T(8,128)(2,1)S(1)} collective-permute-done((bf16[256,256]{1,0:T(8,128)(2,1)S(1)}, bf16[256,256]{1,0:T(8,128)(2,1)S(1)}, u32[]{:S(2)}, u32[]{:S(2)}) %collective-permute-start.16) | collective-permute-done | bytes 131104 | tf_op jit(solution)/shard_map/ppermute | solution.py:31
  85.3 2.6 %collective-permute-start.26 = (bf16[256,256]{1,0:T(8,128)(2,1)S(1)}, bf16[256,256]{1,0:T(8,128)(2,1)S(1)}, u32[]{:S(2)}, u32[]{:S(2)}) collective-permute-start(bf16[256,256]{1,0:T(8,128)(2,1)S(1)} %get-tuple-element.47), channel_id=1, source_target_pairs={{0,16},{4,20},{8,24},{12,28},{16,0},{20,4},{24,8},{28,12},{1,17},{... | collective-permute-start | bytes 393224 | tf_op jit(solution)/shard_map/ppermute | solution.py:31
  87.9 1.4 collective-permute-start.27
  90.3 1.8 %collective-permute-start.46 = (bf16[256,256]{1,0:T(8,128)(2,1)S(1)}, bf16[256,256]{1,0:T(8,128)(2,1)S(1)}, u32[]{:S(2)}, u32[]{:S(2)}) collective-permute-start(bf16[256,256]{1,0:T(8,128)(2,1)S(1)} %get-tuple-element.57.refs_8_), channel_id=1, source_target_pairs={{0,16},{4,20},{8,24},{12,28},{16,0},{20,4},{24,8},{28,12},{1,17},{... | collective-permute-start | bytes 393224 | tf_op jit(solution)/shard_map/ppermute | solution.py:31
  92.1 2.5 %collective-permute-done.26.refs_1_ = bf16[256,256]{1,0:T(8,128)(2,1)S(1)} collective-permute-done((bf16[256,256]{1,0:T(8,128)(2,1)S(1)}, bf16[256,256]{1,0:T(8,128)(2,1)S(1)}, u32[]{:S(2)}, u32[]{:S(2)}) %collective-permute-start.26) | collective-permute-done | bytes 131104 | tf_op jit(solution)/shard_map/ppermute | solution.py:31
  94.6 3.6 %collective-permute-start.20 = (bf16[64,256]{1,0:T(8,128)(2,1)S(1)}, bf16[64,256]{1,0:T(8,128)(2,1)S(1)}, u32[]{:S(2)}, u32[]{:S(2)}) collective-permute-start(bf16[64,256]{1,0:T(8,128)(2,1)S(1)} %get-tuple-element.42), channel_id=1, source_target_pairs={{0,3},{1,2},{2,1},{3,0},{4,7},{5,6},{6,5},{7,4},{8,11},{9,10},{10,... | collective-permute-start | bytes 98312 | tf_op jit(solution)/shard_map/ppermute | solution.py:31
  98.9 1.7 %collective-permute-done.20 = bf16[64,256]{1,0:T(8,128)(2,1)S(1)} collective-permute-done((bf16[64,256]{1,0:T(8,128)(2,1)S(1)}, bf16[64,256]{1,0:T(8,128)(2,1)S(1)}, u32[]{:S(2)}, u32[]{:S(2)}) %collective-permute-start.20) | collective-permute-done | bytes 32800 | tf_op jit(solution)/shard_map/ppermute | solution.py:31
  100.6 2.5 %collective-permute-done.19 = bf16[64,256]{1,0:T(8,128)(2,1)S(1)} collective-permute-done((bf16[64,256]{1,0:T(8,128)(2,1)S(1)}, bf16[64,256]{1,0:T(8,128)(2,1)S(1)}, u32[]{:S(2)}, u32[]{:S(2)}) %collective-permute-start.19) | collective-permute-done | bytes 32800 | tf_op jit(solution)/shard_map/ppermute | solution.py:31
  103.1 2.0 %collective-permute-start.30 = (bf16[64,256]{1,0:T(8,128)(2,1)S(1)}, bf16[64,256]{1,0:T(8,128)(2,1)S(1)}, u32[]{:S(2)}, u32[]{:S(2)}) collective-permute-start(bf16[64,256]{1,0:T(8,128)(2,1)S(1)} %get-tuple-element.52), channel_id=1, source_target_pairs={{0,3},{1,2},{2,1},{3,0},{4,7},{5,6},{6,5},{7,4},{8,11},{9,10},{10,... | collective-permute-start | bytes 98312 | tf_op jit(solution)/shard_map/ppermute | solution.py:31
  105.0 1.8 %collective-permute-start.29 = (bf16[64,256]{1,0:T(8,128)(2,1)S(1)}, bf16[64,256]{1,0:T(8,128)(2,1)S(1)}, u32[]{:S(2)}, u32[]{:S(2)}) collective-permute-start(bf16[64,256]{1,0:T(8,128)(2,1)S(1)} %get-tuple-element.51), channel_id=1, source_target_pairs={{0,2},{1,3},{2,0},{3,1},{4,6},{5,7},{6,4},{7,5},{8,10},{9,11},{10,... | collective-permute-start | bytes 98312 | tf_op jit(solution)/shard_map/ppermute | solution.py:31
  106.9 1.9 %collective-permute-done.30 = bf16[64,256]{1,0:T(8,128)(2,1)S(1)} collective-permute-done((bf16[64,256]{1,0:T(8,128)(2,1)S(1)}, bf16[64,256]{1,0:T(8,128)(2,1)S(1)}, u32[]{:S(2)}, u32[]{:S(2)}) %collective-permute-start.30) | collective-permute-done | bytes 32800 | tf_op jit(solution)/shard_map/ppermute | solution.py:31
  108.9 1.0 collective-permute-done.29
  109.9 3.5 %collective-permute-start.47 = (bf16[256,256]{1,0:T(8,128)(2,1)S(1)}, bf16[256,256]{1,0:T(8,128)(2,1)S(1)}, u32[]{:S(2)}, u32[]{:S(2)}) collective-permute-start(bf16[256,256]{1,0:T(8,128)(2,1)S(1)} %get-tuple-element.57.refs_8_), channel_id=1, source_target_pairs={{0,24},{4,28},{8,16},{12,20},{16,8},{20,12},{24,0},{28,4},{1,25},{... | collective-permute-start | bytes 393224 | tf_op jit(solution)/shard_map/ppermute | solution.py:31
  113.4 0.9 collective-permute-start.49
  114.4 2.5 %collective-permute-start.50 = (bf16[256,256]{1,0:T(8,128)(2,1)S(1)}, bf16[256,256]{1,0:T(8,128)(2,1)S(1)}, u32[]{:S(2)}, u32[]{:S(2)}) collective-permute-start(bf16[256,256]{1,0:T(8,128)(2,1)S(1)} %get-tuple-element.58.refs_13_), channel_id=1, source_target_pairs={{0,16},{4,20},{8,24},{12,28},{16,0},{20,4},{24,8},{28,12},{1,17},{... | collective-permute-start | bytes 393224 | tf_op jit(solution)/shard_map/ppermute | solution.py:31
  116.9 0.9 collective-permute-done.47.refs_11_
  118.5 1.5 collective-permute-done.49.refs_14_
  119.9 1.7 %collective-permute-start.22 = (bf16[4,64,256]{2,1,0:T(8,128)(2,1)S(1)}, bf16[4,64,256]{2,1,0:T(8,128)(2,1)S(1)}, u32[]{:S(2)}, u32[]{:S(2)}) collective-permute-start(bf16[4,64,256]{2,1,0:T(8,128)(2,1)S(1)} %pad_maximum_fusion.4.refs_0_), channel_id=1, source_target_pairs={{0,16},{4,20},{8,24},{12,28},{16,0},{20,4},{24,8},{28,12},{1,17},{... | collective-permute-start | bytes 393224 | tf_op jit(solution)/shard_map/ppermute | solution.py:31
  121.9 3.9 %collective-permute-start.23 = (bf16[4,64,256]{2,1,0:T(8,128)(2,1)S(1)}, bf16[4,64,256]{2,1,0:T(8,128)(2,1)S(1)}, u32[]{:S(2)}, u32[]{:S(2)}) collective-permute-start(bf16[4,64,256]{2,1,0:T(8,128)(2,1)S(1)} %pad_maximum_fusion.4.refs_0_), channel_id=1, source_target_pairs={{0,24},{4,28},{8,16},{12,20},{16,8},{20,12},{24,0},{28,4},{1,25},{... | collective-permute-start | bytes 393224 | tf_op jit(solution)/shard_map/ppermute | solution.py:31
  126.3 1.3 collective-permute-start.32
  127.6 2.2 %collective-permute-start.33 = (bf16[4,64,256]{2,1,0:T(8,128)(2,1)S(1)}, bf16[4,64,256]{2,1,0:T(8,128)(2,1)S(1)}, u32[]{:S(2)}, u32[]{:S(2)}) collective-permute-start(bf16[4,64,256]{2,1,0:T(8,128)(2,1)S(1)} %pad_maximum_fusion.5.refs_4_), channel_id=1, source_target_pairs={{0,24},{4,28},{8,16},{12,20},{16,8},{20,12},{24,0},{28,4},{1,25},{... | collective-permute-start | bytes 393224 | tf_op jit(solution)/shard_map/ppermute | solution.py:31
  129.9 0.8 collective-permute-done.31.refs_5_
  131.5 1.9 %collective-permute-done.33.refs_7_ = bf16[4,64,256]{2,1,0:T(8,128)(2,1)S(1)} collective-permute-done((bf16[4,64,256]{2,1,0:T(8,128)(2,1)S(1)}, bf16[4,64,256]{2,1,0:T(8,128)(2,1)S(1)}, u32[]{:S(2)}, u32[]{:S(2)}) %collective-permute-start.33) | collective-permute-done | bytes 131104 | tf_op jit(solution)/shard_map/ppermute | solution.py:31
  133.4 2.2 %collective-permute-start.43 = (bf16[256,640]{1,0:T(8,128)(2,1)S(1)}, bf16[256,640]{1,0:T(8,128)(2,1)S(1)}, u32[]{:S(2)}, u32[]{:S(2)}) collective-permute-start(bf16[256,640]{1,0:T(8,128)(2,1)S(1)} %get-tuple-element.66), channel_id=1, source_target_pairs={{0,24},{4,28},{8,16},{12,20},{16,8},{20,12},{24,0},{28,4},{1,25},{... | collective-permute-start | bytes 983048 | tf_op jit(solution)/shard_map/ppermute | solution.py:31
  135.7 3.7 %input_grad.1 = (bf16[64,1280]{1,0:T(8,128)(2,1)S(1)}, bf16[64,1280]{1,0:T(8,128)(2,1)S(1)}, bf16[64,1280]{1,0:T(8,128)(2,1)S(1)}, bf16[64,1280]{1,0:T(8,128)(2,1)S(1)}) custom-call(s32[2]{0:T(128)S(1)} %pad_add_fusion.place, bf16[4,64,256]{2,1,0:T(8,128)(2,1)S(1)} %pad_maximum_fusion.4.refs_0_, bf16[4,64,256]{2,1,0:T(8,128)(2,1)S(1)} %collective-permute-done.21.refs_1_, ...), custom_call_target="tpu_custom_call" | custom-call | tf_op jit(solution)/shard_map/input_grad/pallas_call | solution.py:273
  139.4 15.9 %collective-permute-done.42.refs_5_ = bf16[256,640]{1,0:T(8,128)(2,1)S(1)} collective-permute-done((bf16[256,640]{1,0:T(8,128)(2,1)S(1)}, bf16[256,640]{1,0:T(8,128)(2,1)S(1)}, u32[]{:S(2)}, u32[]{:S(2)}) %collective-permute-start.42) | collective-permute-done | bytes 327712 | tf_op jit(solution)/shard_map/ppermute | solution.py:31
  155.3 1.6 collective-permute-start.35
  157.0 1.8 %collective-permute-start.37 = (bf16[64,1280]{1,0:T(8,128)(2,1)S(1)}, bf16[64,1280]{1,0:T(8,128)(2,1)S(1)}, u32[]{:S(2)}, u32[]{:S(2)}) collective-permute-start(bf16[64,1280]{1,0:T(8,128)(2,1)S(1)} %get-tuple-element.56), channel_id=1, source_target_pairs={{0,24},{4,28},{8,16},{12,20},{16,8},{20,12},{24,0},{28,4},{1,25},{... | collective-permute-start | bytes 491528 | tf_op jit(solution)/shard_map/ppermute | solution.py:31
  158.8 3.2 %weight_grad.1 = f32[640,2,256]{2,1,0:T(2,128)} custom-call(bf16[256,640]{1,0:T(8,128)(2,1)S(1)} %get-tuple-element.65.refs_0_, bf16[256,640]{1,0:T(8,128)(2,1)S(1)} %collective-permute-done.38.refs_1_, bf16[256,640]{1,0:T(8,128)(2,1)S(1)} %collective-permute-done.39.refs_2_, bf16[256,640]{1,0:T(8,128)(2,1)S(1)} %collective-permute-done.40.refs_3_, ...), custom_call_target="tpu_custom_call" | custom-call | tf_op jit(solution)/shard_map/weight_grad/pallas_call | solution.py:237
  162.3 3.4 %collective-permute-done.36.refs_2_ = bf16[64,1280]{1,0:T(8,128)(2,1)S(1)} collective-permute-done((bf16[64,1280]{1,0:T(8,128)(2,1)S(1)}, bf16[64,1280]{1,0:T(8,128)(2,1)S(1)}, u32[]{:S(2)}, u32[]{:S(2)}) %collective-permute-start.36) | collective-permute-done | bytes 163872 | tf_op jit(solution)/shard_map/ppermute | solution.py:31
  165.7 1.4 lay_rows.1
  (87 shorter events, 9.2 us)
Async XLA Ops:
  2.2 8.1 %collective-permute-start.1 = (bf16[256,256]{1,0:T(8,128)(2,1)S(1)}, bf16[256,256]{1,0:T(8,128)(2,1)S(1)}, u32[]{:S(2)}, u32[]{:S(2)}) collective-permute-start(bf16[256,256]{1,0:T(8,128)(2,1)S(1)} %pad_maximum_fusion.2.refs_0_), channel_id=1, source_target_pairs={{0,8},{4,12},{8,0},{12,4},{16,24},{20,28},{24,16},{28,20},{1,9},{5... | collective-permute-start | bytes 393224 | tf_op jit(solution)/shard_map/ppermute | solution.py:31
  5.2 7.3 %collective-permute-start.3 = (bf16[256,256]{1,0:T(8,128)(2,1)S(1)}, bf16[256,256]{1,0:T(8,128)(2,1)S(1)}, u32[]{:S(2)}, u32[]{:S(2)}) collective-permute-start(bf16[256,256]{1,0:T(8,128)(2,1)S(1)} %pad_maximum_fusion.2.refs_0_), channel_id=1, source_target_pairs={{0,16},{4,20},{8,24},{12,28},{16,0},{20,4},{24,8},{28,12},{1,17},{... | collective-permute-start | bytes 393224 | tf_op jit(solution)/shard_map/ppermute | solution.py:31
  6.8 6.4 %collective-permute-start.8 = (bf16[256,256]{1,0:T(8,128)(2,1)S(1)}, bf16[256,256]{1,0:T(8,128)(2,1)S(1)}, u32[]{:S(2)}, u32[]{:S(2)}) collective-permute-start(bf16[256,256]{1,0:T(8,128)(2,1)S(1)} %pad_maximum_fusion.3.refs_0_), channel_id=1, source_target_pairs={{0,8},{4,12},{8,0},{12,4},{16,24},{20,28},{24,16},{28,20},{1,9},{5... | collective-permute-start | bytes 393224 | tf_op jit(solution)/shard_map/ppermute | solution.py:31
  7.4 11.2 %collective-permute-start.10 = (bf16[256,256]{1,0:T(8,128)(2,1)S(1)}, bf16[256,256]{1,0:T(8,128)(2,1)S(1)}, u32[]{:S(2)}, u32[]{:S(2)}) collective-permute-start(bf16[256,256]{1,0:T(8,128)(2,1)S(1)} %pad_maximum_fusion.3.refs_0_), channel_id=1, source_target_pairs={{0,16},{4,20},{8,24},{12,28},{16,0},{20,4},{24,8},{28,12},{1,17},{... | collective-permute-start | bytes 393224 | tf_op jit(solution)/shard_map/ppermute | solution.py:31
  7.5 11.2 %collective-permute-start.12 = (bf16[256,256]{1,0:T(8,128)(2,1)S(1)}, bf16[256,256]{1,0:T(8,128)(2,1)S(1)}, u32[]{:S(2)}, u32[]{:S(2)}) collective-permute-start(bf16[256,256]{1,0:T(8,128)(2,1)S(1)} %pad_maximum_fusion.3.refs_0_), channel_id=1, source_target_pairs={{0,24},{4,28},{8,16},{12,20},{16,8},{20,12},{24,0},{28,4},{1,25},{... | collective-permute-start | bytes 393224 | tf_op jit(solution)/shard_map/ppermute | solution.py:31
  10.4 14.3 %collective-permute-start.5 = (bf16[256,256]{1,0:T(8,128)(2,1)S(1)}, bf16[256,256]{1,0:T(8,128)(2,1)S(1)}, u32[]{:S(2)}, u32[]{:S(2)}) collective-permute-start(bf16[256,256]{1,0:T(8,128)(2,1)S(1)} %pad_maximum_fusion.2.refs_0_), channel_id=1, source_target_pairs={{0,24},{4,28},{8,16},{12,20},{16,8},{20,12},{24,0},{28,4},{1,25},{... | collective-permute-start | bytes 393224 | tf_op jit(solution)/shard_map/ppermute | solution.py:31
  12.6 12.1 %collective-permute-start.7 = (bf16[256,256]{1,0:T(8,128)(2,1)S(1)}, bf16[256,256]{1,0:T(8,128)(2,1)S(1)}, u32[]{:S(2)}, u32[]{:S(2)}) collective-permute-start(bf16[256,256]{1,0:T(8,128)(2,1)S(1)} %pad_maximum_fusion.3.refs_0_), channel_id=1, source_target_pairs={{0,4},{4,0},{8,12},{12,8},{16,20},{20,16},{24,28},{28,24},{1,5},{5... | collective-permute-start | bytes 393224 | tf_op jit(solution)/shard_map/ppermute | solution.py:31
  13.2 12.0 %collective-permute-start.9 = (bf16[256,256]{1,0:T(8,128)(2,1)S(1)}, bf16[256,256]{1,0:T(8,128)(2,1)S(1)}, u32[]{:S(2)}, u32[]{:S(2)}) collective-permute-start(bf16[256,256]{1,0:T(8,128)(2,1)S(1)} %collective-permute-done.8.refs_2_), channel_id=1, source_target_pairs={{0,4},{4,0},{8,12},{12,8},{16,20},{20,16},{24,28},{28,24},{1,5},{5... | collective-permute-start | bytes 393224 | tf_op jit(solution)/shard_map/ppermute | solution.py:31
  18.6 6.7 %collective-permute-start.11 = (bf16[256,256]{1,0:T(8,128)(2,1)S(1)}, bf16[256,256]{1,0:T(8,128)(2,1)S(1)}, u32[]{:S(2)}, u32[]{:S(2)}) collective-permute-start(bf16[256,256]{1,0:T(8,128)(2,1)S(1)} %collective-permute-done.10.refs_4_), channel_id=1, source_target_pairs={{0,4},{4,0},{8,12},{12,8},{16,20},{20,16},{24,28},{28,24},{1,5},{5... | collective-permute-start | bytes 393224 | tf_op jit(solution)/shard_map/ppermute | solution.py:31
  18.6 7.1 %collective-permute-start.13 = (bf16[256,256]{1,0:T(8,128)(2,1)S(1)}, bf16[256,256]{1,0:T(8,128)(2,1)S(1)}, u32[]{:S(2)}, u32[]{:S(2)}) collective-permute-start(bf16[256,256]{1,0:T(8,128)(2,1)S(1)} %collective-permute-done.12.refs_6_), channel_id=1, source_target_pairs={{0,4},{4,0},{8,12},{12,8},{16,20},{20,16},{24,28},{28,24},{1,5},{5... | collective-permute-start | bytes 393224 | tf_op jit(solution)/shard_map/ppermute | solution.py:31
  24.7 18.7 %collective-permute-start = (bf16[256,256]{1,0:T(8,128)(2,1)S(1)}, bf16[256,256]{1,0:T(8,128)(2,1)S(1)}, u32[]{:S(2)}, u32[]{:S(2)}) collective-permute-start(bf16[256,256]{1,0:T(8,128)(2,1)S(1)} %pad_maximum_fusion.2.refs_0_), channel_id=1, source_target_pairs={{0,4},{4,0},{8,12},{12,8},{16,20},{20,16},{24,28},{28,24},{1,5},{5... | collective-permute-start | bytes 393224 | tf_op jit(solution)/shard_map/ppermute | solution.py:31
  24.7 110.9 %collective-permute-start.34 = (bf16[640,2048]{1,0:T(8,128)(2,1)S(1)}, bf16[640,2048]{1,0:T(8,128)(2,1)}, u32[]{:S(2)}, u32[]{:S(2)}) collective-permute-start(bf16[640,2048]{1,0:T(8,128)(2,1)S(1)} %bitcast.31), channel_id=1, source_target_pairs={{0,4},{4,0},{8,12},{12,8},{16,20},{20,16},{24,28},{28,24},{1,5},{5... | collective-permute-start | bytes 7864328 | tf_op jit(solution)/shard_map/ppermute | solution.py:31
  25.2 18.6 %collective-permute-start.2 = (bf16[256,256]{1,0:T(8,128)(2,1)S(1)}, bf16[256,256]{1,0:T(8,128)(2,1)S(1)}, u32[]{:S(2)}, u32[]{:S(2)}) collective-permute-start(bf16[256,256]{1,0:T(8,128)(2,1)S(1)} %collective-permute-done.1.refs_2_), channel_id=1, source_target_pairs={{0,4},{4,0},{8,12},{12,8},{16,20},{20,16},{24,28},{28,24},{1,5},{5... | collective-permute-start | bytes 393224 | tf_op jit(solution)/shard_map/ppermute | solution.py:31
  25.3 18.6 %collective-permute-start.4 = (bf16[256,256]{1,0:T(8,128)(2,1)S(1)}, bf16[256,256]{1,0:T(8,128)(2,1)S(1)}, u32[]{:S(2)}, u32[]{:S(2)}) collective-permute-start(bf16[256,256]{1,0:T(8,128)(2,1)S(1)} %collective-permute-done.3.refs_4_), channel_id=1, source_target_pairs={{0,4},{4,0},{8,12},{12,8},{16,20},{20,16},{24,28},{28,24},{1,5},{5... | collective-permute-start | bytes 393224 | tf_op jit(solution)/shard_map/ppermute | solution.py:31
  25.7 18.2 %collective-permute-start.6 = (bf16[256,256]{1,0:T(8,128)(2,1)S(1)}, bf16[256,256]{1,0:T(8,128)(2,1)S(1)}, u32[]{:S(2)}, u32[]{:S(2)}) collective-permute-start(bf16[256,256]{1,0:T(8,128)(2,1)S(1)} %collective-permute-done.5.refs_6_), channel_id=1, source_target_pairs={{0,4},{4,0},{8,12},{12,8},{16,20},{20,16},{24,28},{28,24},{1,5},{5... | collective-permute-start | bytes 393224 | tf_op jit(solution)/shard_map/ppermute | solution.py:31
  43.4 18.6 %collective-permute-start.38 = (bf16[256,640]{1,0:T(8,128)(2,1)S(1)}, bf16[256,640]{1,0:T(8,128)(2,1)S(1)}, u32[]{:S(2)}, u32[]{:S(2)}) collective-permute-start(bf16[256,640]{1,0:T(8,128)(2,1)S(1)} %copy-done.3), channel_id=1, source_target_pairs={{0,4},{4,0},{8,12},{12,8},{16,20},{20,16},{24,28},{28,24},{1,5},{5... | collective-permute-start | bytes 983048 | tf_op jit(solution)/shard_map/ppermute | solution.py:31
  43.8 19.5 %collective-permute-start.14 = (bf16[4,256,256]{2,1,0:T(8,128)(2,1)S(1)}, bf16[4,256,256]{2,1,0:T(8,128)(2,1)S(1)}, u32[]{:S(2)}, u32[]{:S(2)}) collective-permute-start(bf16[4,256,256]{2,1,0:T(8,128)(2,1)S(1)} %get-tuple-element.34), channel_id=1, source_target_pairs={{0,4},{4,0},{8,12},{12,8},{16,20},{20,16},{24,28},{28,24},{1,5},{5... | collective-permute-start | bytes 1572872 | tf_op jit(solution)/shard_map/ppermute | solution.py:31
  61.5 17.8 %collective-permute-start.24 = (bf16[4,256,256]{2,1,0:T(8,128)(2,1)S(1)}, bf16[4,256,256]{2,1,0:T(8,128)(2,1)S(1)}, u32[]{:S(2)}, u32[]{:S(2)}) collective-permute-start(bf16[4,256,256]{2,1,0:T(8,128)(2,1)S(1)} %get-tuple-element.44), channel_id=1, source_target_pairs={{0,4},{4,0},{8,12},{12,8},{16,20},{20,16},{24,28},{28,24},{1,5},{5... | collective-permute-start | bytes 1572872 | tf_op jit(solution)/shard_map/ppermute | solution.py:31
  61.9 10.6 %collective-permute-start.39 = (bf16[256,640]{1,0:T(8,128)(2,1)S(1)}, bf16[256,640]{1,0:T(8,128)(2,1)S(1)}, u32[]{:S(2)}, u32[]{:S(2)}) collective-permute-start(bf16[256,640]{1,0:T(8,128)(2,1)S(1)} %copy-done.2), channel_id=1, source_target_pairs={{0,8},{4,12},{8,0},{12,4},{16,24},{20,28},{24,16},{28,20},{1,9},{5... | collective-permute-start | bytes 983048 | tf_op jit(solution)/shard_map/ppermute | solution.py:31
  61.9 15.8 %collective-permute-start.40 = (bf16[256,640]{1,0:T(8,128)(2,1)S(1)}, bf16[256,640]{1,0:T(8,128)(2,1)S(1)}, u32[]{:S(2)}, u32[]{:S(2)}) collective-permute-start(bf16[256,640]{1,0:T(8,128)(2,1)S(1)} %get-tuple-element.62), channel_id=1, source_target_pairs={{0,12},{4,8},{8,4},{12,0},{16,28},{20,24},{24,20},{28,16},{1,13},{... | collective-permute-start | bytes 983048 | tf_op jit(solution)/shard_map/ppermute | solution.py:31
  63.4 26.6 %collective-permute-start.41 = (bf16[256,640]{1,0:T(8,128)(2,1)S(1)}, bf16[256,640]{1,0:T(8,128)(2,1)S(1)}, u32[]{:S(2)}, u32[]{:S(2)}) collective-permute-start(bf16[256,640]{1,0:T(8,128)(2,1)S(1)} %get-tuple-element.61), channel_id=1, source_target_pairs={{0,16},{4,20},{8,24},{12,28},{16,0},{20,4},{24,8},{28,12},{1,17},{... | collective-permute-start | bytes 983048 | tf_op jit(solution)/shard_map/ppermute | solution.py:31
  72.5 9.0 %collective-permute-start.15 = (bf16[256,256]{1,0:T(8,128)(2,1)S(1)}, bf16[256,256]{1,0:T(8,128)(2,1)S(1)}, u32[]{:S(2)}, u32[]{:S(2)}) collective-permute-start(bf16[256,256]{1,0:T(8,128)(2,1)S(1)} %get-tuple-element.36), channel_id=1, source_target_pairs={{0,8},{4,12},{8,0},{12,4},{16,24},{20,28},{24,16},{28,20},{1,9},{5... | collective-permute-start | bytes 393224 | tf_op jit(solution)/shard_map/ppermute | solution.py:31
  77.8 7.5 %collective-permute-start.16 = (bf16[256,256]{1,0:T(8,128)(2,1)S(1)}, bf16[256,256]{1,0:T(8,128)(2,1)S(1)}, u32[]{:S(2)}, u32[]{:S(2)}) collective-permute-start(bf16[256,256]{1,0:T(8,128)(2,1)S(1)} %get-tuple-element.37), channel_id=1, source_target_pairs={{0,16},{4,20},{8,24},{12,28},{16,0},{20,4},{24,8},{28,12},{1,17},{... | collective-permute-start | bytes 393224 | tf_op jit(solution)/shard_map/ppermute | solution.py:31
  79.3 8.6 %collective-permute-start.17 = (bf16[256,256]{1,0:T(8,128)(2,1)S(1)}, bf16[256,256]{1,0:T(8,128)(2,1)S(1)}, u32[]{:S(2)}, u32[]{:S(2)}) collective-permute-start(bf16[256,256]{1,0:T(8,128)(2,1)S(1)} %get-tuple-element.38), channel_id=1, source_target_pairs={{0,24},{4,28},{8,16},{12,20},{16,8},{20,12},{24,0},{28,4},{1,25},{... | collective-permute-start | bytes 393224 | tf_op jit(solution)/shard_map/ppermute | solution.py:31
  81.5 8.9 %collective-permute-start.25 = (bf16[256,256]{1,0:T(8,128)(2,1)S(1)}, bf16[256,256]{1,0:T(8,128)(2,1)S(1)}, u32[]{:S(2)}, u32[]{:S(2)}) collective-permute-start(bf16[256,256]{1,0:T(8,128)(2,1)S(1)} %get-tuple-element.46), channel_id=1, source_target_pairs={{0,8},{4,12},{8,0},{12,4},{16,24},{20,28},{24,16},{28,20},{1,9},{5... | collective-permute-start | bytes 393224 | tf_op jit(solution)/shard_map/ppermute | solution.py:31
  85.3 9.3 %collective-permute-start.26 = (bf16[256,256]{1,0:T(8,128)(2,1)S(1)}, bf16[256,256]{1,0:T(8,128)(2,1)S(1)}, u32[]{:S(2)}, u32[]{:S(2)}) collective-permute-start(bf16[256,256]{1,0:T(8,128)(2,1)S(1)} %get-tuple-element.47), channel_id=1, source_target_pairs={{0,16},{4,20},{8,24},{12,28},{16,0},{20,4},{24,8},{28,12},{1,17},{... | collective-permute-start | bytes 393224 | tf_op jit(solution)/shard_map/ppermute | solution.py:31
  87.9 10.3 %collective-permute-start.27 = (bf16[256,256]{1,0:T(8,128)(2,1)S(1)}, bf16[256,256]{1,0:T(8,128)(2,1)S(1)}, u32[]{:S(2)}, u32[]{:S(2)}) collective-permute-start(bf16[256,256]{1,0:T(8,128)(2,1)S(1)} %get-tuple-element.48), channel_id=1, source_target_pairs={{0,24},{4,28},{8,16},{12,20},{16,8},{20,12},{24,0},{28,4},{1,25},{... | collective-permute-start | bytes 393224 | tf_op jit(solution)/shard_map/ppermute | solution.py:31
  90.0 24.4 %collective-permute-start.45 = (bf16[256,256]{1,0:T(8,128)(2,1)S(1)}, bf16[256,256]{1,0:T(8,128)(2,1)S(1)}, u32[]{:S(2)}, u32[]{:S(2)}) collective-permute-start(bf16[256,256]{1,0:T(8,128)(2,1)S(1)} %get-tuple-element.57.refs_8_), channel_id=1, source_target_pairs={{0,8},{4,12},{8,0},{12,4},{16,24},{20,28},{24,16},{28,20},{1,9},{5... | collective-permute-start | bytes 393224 | tf_op jit(solution)/shard_map/ppermute | solution.py:31
  90.3 26.5 %collective-permute-start.46 = (bf16[256,256]{1,0:T(8,128)(2,1)S(1)}, bf16[256,256]{1,0:T(8,128)(2,1)S(1)}, u32[]{:S(2)}, u32[]{:S(2)}) collective-permute-start(bf16[256,256]{1,0:T(8,128)(2,1)S(1)} %get-tuple-element.57.refs_8_), channel_id=1, source_target_pairs={{0,16},{4,20},{8,24},{12,28},{16,0},{20,4},{24,8},{28,12},{1,17},{... | collective-permute-start | bytes 393224 | tf_op jit(solution)/shard_map/ppermute | solution.py:31
  94.6 5.9 %collective-permute-start.20 = (bf16[64,256]{1,0:T(8,128)(2,1)S(1)}, bf16[64,256]{1,0:T(8,128)(2,1)S(1)}, u32[]{:S(2)}, u32[]{:S(2)}) collective-permute-start(bf16[64,256]{1,0:T(8,128)(2,1)S(1)} %get-tuple-element.42), channel_id=1, source_target_pairs={{0,3},{1,2},{2,1},{3,0},{4,7},{5,6},{6,5},{7,4},{8,11},{9,10},{10,... | collective-permute-start | bytes 98312 | tf_op jit(solution)/shard_map/ppermute | solution.py:31
  103.1 5.7 %collective-permute-start.30 = (bf16[64,256]{1,0:T(8,128)(2,1)S(1)}, bf16[64,256]{1,0:T(8,128)(2,1)S(1)}, u32[]{:S(2)}, u32[]{:S(2)}) collective-permute-start(bf16[64,256]{1,0:T(8,128)(2,1)S(1)} %get-tuple-element.52), channel_id=1, source_target_pairs={{0,3},{1,2},{2,1},{3,0},{4,7},{5,6},{6,5},{7,4},{8,11},{9,10},{10,... | collective-permute-start | bytes 98312 | tf_op jit(solution)/shard_map/ppermute | solution.py:31
  109.9 7.9 %collective-permute-start.47 = (bf16[256,256]{1,0:T(8,128)(2,1)S(1)}, bf16[256,256]{1,0:T(8,128)(2,1)S(1)}, u32[]{:S(2)}, u32[]{:S(2)}) collective-permute-start(bf16[256,256]{1,0:T(8,128)(2,1)S(1)} %get-tuple-element.57.refs_8_), channel_id=1, source_target_pairs={{0,24},{4,28},{8,16},{12,20},{16,8},{20,12},{24,0},{28,4},{1,25},{... | collective-permute-start | bytes 393224 | tf_op jit(solution)/shard_map/ppermute | solution.py:31
  113.4 6.5 %collective-permute-start.49 = (bf16[256,256]{1,0:T(8,128)(2,1)S(1)}, bf16[256,256]{1,0:T(8,128)(2,1)S(1)}, u32[]{:S(2)}, u32[]{:S(2)}) collective-permute-start(bf16[256,256]{1,0:T(8,128)(2,1)S(1)} %get-tuple-element.58.refs_13_), channel_id=1, source_target_pairs={{0,8},{4,12},{8,0},{12,4},{16,24},{20,28},{24,16},{28,20},{1,9},{5... | collective-permute-start | bytes 393224 | tf_op jit(solution)/shard_map/ppermute | solution.py:31
  114.4 7.6 %collective-permute-start.50 = (bf16[256,256]{1,0:T(8,128)(2,1)S(1)}, bf16[256,256]{1,0:T(8,128)(2,1)S(1)}, u32[]{:S(2)}, u32[]{:S(2)}) collective-permute-start(bf16[256,256]{1,0:T(8,128)(2,1)S(1)} %get-tuple-element.58.refs_13_), channel_id=1, source_target_pairs={{0,16},{4,20},{8,24},{12,28},{16,0},{20,4},{24,8},{28,12},{1,17},{... | collective-permute-start | bytes 393224 | tf_op jit(solution)/shard_map/ppermute | solution.py:31
  116.8 8.9 %collective-permute-start.51 = (bf16[256,256]{1,0:T(8,128)(2,1)S(1)}, bf16[256,256]{1,0:T(8,128)(2,1)S(1)}, u32[]{:S(2)}, u32[]{:S(2)}) collective-permute-start(bf16[256,256]{1,0:T(8,128)(2,1)S(1)} %get-tuple-element.58.refs_13_), channel_id=1, source_target_pairs={{0,24},{4,28},{8,16},{12,20},{16,8},{20,12},{24,0},{28,4},{1,25},{... | collective-permute-start | bytes 393224 | tf_op jit(solution)/shard_map/ppermute | solution.py:31
  117.8 8.5 %collective-permute-start.21 = (bf16[4,64,256]{2,1,0:T(8,128)(2,1)S(1)}, bf16[4,64,256]{2,1,0:T(8,128)(2,1)S(1)}, u32[]{:S(2)}, u32[]{:S(2)}) collective-permute-start(bf16[4,64,256]{2,1,0:T(8,128)(2,1)S(1)} %pad_maximum_fusion.4.refs_0_), channel_id=1, source_target_pairs={{0,8},{4,12},{8,0},{12,4},{16,24},{20,28},{24,16},{28,20},{1,9},{5... | collective-permute-start | bytes 393224 | tf_op jit(solution)/shard_map/ppermute | solution.py:31
  119.9 7.6 %collective-permute-start.22 = (bf16[4,64,256]{2,1,0:T(8,128)(2,1)S(1)}, bf16[4,64,256]{2,1,0:T(8,128)(2,1)S(1)}, u32[]{:S(2)}, u32[]{:S(2)}) collective-permute-start(bf16[4,64,256]{2,1,0:T(8,128)(2,1)S(1)} %pad_maximum_fusion.4.refs_0_), channel_id=1, source_target_pairs={{0,16},{4,20},{8,24},{12,28},{16,0},{20,4},{24,8},{28,12},{1,17},{... | collective-permute-start | bytes 393224 | tf_op jit(solution)/shard_map/ppermute | solution.py:31
  121.9 7.9 %collective-permute-start.23 = (bf16[4,64,256]{2,1,0:T(8,128)(2,1)S(1)}, bf16[4,64,256]{2,1,0:T(8,128)(2,1)S(1)}, u32[]{:S(2)}, u32[]{:S(2)}) collective-permute-start(bf16[4,64,256]{2,1,0:T(8,128)(2,1)S(1)} %pad_maximum_fusion.4.refs_0_), channel_id=1, source_target_pairs={{0,24},{4,28},{8,16},{12,20},{16,8},{20,12},{24,0},{28,4},{1,25},{... | collective-permute-start | bytes 393224 | tf_op jit(solution)/shard_map/ppermute | solution.py:31
  126.3 5.0 %collective-permute-start.32 = (bf16[4,64,256]{2,1,0:T(8,128)(2,1)S(1)}, bf16[4,64,256]{2,1,0:T(8,128)(2,1)S(1)}, u32[]{:S(2)}, u32[]{:S(2)}) collective-permute-start(bf16[4,64,256]{2,1,0:T(8,128)(2,1)S(1)} %pad_maximum_fusion.5.refs_4_), channel_id=1, source_target_pairs={{0,16},{4,20},{8,24},{12,28},{16,0},{20,4},{24,8},{28,12},{1,17},{... | collective-permute-start | bytes 393224 | tf_op jit(solution)/shard_map/ppermute | solution.py:31
  127.6 5.9 %collective-permute-start.33 = (bf16[4,64,256]{2,1,0:T(8,128)(2,1)S(1)}, bf16[4,64,256]{2,1,0:T(8,128)(2,1)S(1)}, u32[]{:S(2)}, u32[]{:S(2)}) collective-permute-start(bf16[4,64,256]{2,1,0:T(8,128)(2,1)S(1)} %pad_maximum_fusion.5.refs_4_), channel_id=1, source_target_pairs={{0,24},{4,28},{8,16},{12,20},{16,8},{20,12},{24,0},{28,4},{1,25},{... | collective-permute-start | bytes 393224 | tf_op jit(solution)/shard_map/ppermute | solution.py:31
  129.9 28.9 %collective-permute-start.48 = (bf16[4,256,256]{2,1,0:T(8,128)(2,1)S(1)}, bf16[4,256,256]{2,1,0:T(8,128)(2,1)S(1)}, u32[]{:S(2)}, u32[]{:S(2)}) collective-permute-start(bf16[4,256,256]{2,1,0:T(8,128)(2,1)S(1)} %pad_maximum_fusion), channel_id=1, source_target_pairs={{0,4},{4,0},{8,12},{12,8},{16,20},{20,16},{24,28},{28,24},{1,5},{5... | collective-permute-start | bytes 1572872 | tf_op jit(solution)/shard_map/ppermute | solution.py:31
  130.8 28.0 %collective-permute-start.52 = (bf16[4,256,256]{2,1,0:T(8,128)(2,1)S(1)}, bf16[4,256,256]{2,1,0:T(8,128)(2,1)S(1)}, u32[]{:S(2)}, u32[]{:S(2)}) collective-permute-start(bf16[4,256,256]{2,1,0:T(8,128)(2,1)S(1)} %pad_maximum_fusion.1), channel_id=1, source_target_pairs={{0,4},{4,0},{8,12},{12,8},{16,20},{20,16},{24,28},{28,24},{1,5},{5... | collective-permute-start | bytes 1572872 | tf_op jit(solution)/shard_map/ppermute | solution.py:31
  131.3 23.9 %collective-permute-start.42 = (bf16[256,640]{1,0:T(8,128)(2,1)S(1)}, bf16[256,640]{1,0:T(8,128)(2,1)S(1)}, u32[]{:S(2)}, u32[]{:S(2)}) collective-permute-start(bf16[256,640]{1,0:T(8,128)(2,1)S(1)} %get-tuple-element.60), channel_id=1, source_target_pairs={{0,20},{4,16},{8,28},{12,24},{16,4},{20,0},{24,12},{28,8},{1,21},{... | collective-permute-start | bytes 983048 | tf_op jit(solution)/shard_map/ppermute | solution.py:31
  133.4 23.5 %collective-permute-start.43 = (bf16[256,640]{1,0:T(8,128)(2,1)S(1)}, bf16[256,640]{1,0:T(8,128)(2,1)S(1)}, u32[]{:S(2)}, u32[]{:S(2)}) collective-permute-start(bf16[256,640]{1,0:T(8,128)(2,1)S(1)} %get-tuple-element.66), channel_id=1, source_target_pairs={{0,24},{4,28},{8,16},{12,20},{16,8},{20,12},{24,0},{28,4},{1,25},{... | collective-permute-start | bytes 983048 | tf_op jit(solution)/shard_map/ppermute | solution.py:31
  135.7 21.3 %collective-permute-start.44 = (bf16[256,640]{1,0:T(8,128)(2,1)S(1)}, bf16[256,640]{1,0:T(8,128)(2,1)S(1)}, u32[]{:S(2)}, u32[]{:S(2)}) collective-permute-start(bf16[256,640]{1,0:T(8,128)(2,1)S(1)} %get-tuple-element.59), channel_id=1, source_target_pairs={{0,28},{4,24},{8,20},{12,16},{16,12},{20,8},{24,4},{28,0},{1,29},{... | collective-permute-start | bytes 983048 | tf_op jit(solution)/shard_map/ppermute | solution.py:31
  155.3 7.0 %collective-permute-start.35 = (bf16[64,1280]{1,0:T(8,128)(2,1)S(1)}, bf16[64,1280]{1,0:T(8,128)(2,1)S(1)}, u32[]{:S(2)}, u32[]{:S(2)}) collective-permute-start(bf16[64,1280]{1,0:T(8,128)(2,1)S(1)} %get-tuple-element.54), channel_id=1, source_target_pairs={{0,8},{4,12},{8,0},{12,4},{16,24},{20,28},{24,16},{28,20},{1,9},{5... | collective-permute-start | bytes 491528 | tf_op jit(solution)/shard_map/ppermute | solution.py:31
  156.9 8.8 %collective-permute-start.36 = (bf16[64,1280]{1,0:T(8,128)(2,1)S(1)}, bf16[64,1280]{1,0:T(8,128)(2,1)S(1)}, u32[]{:S(2)}, u32[]{:S(2)}) collective-permute-start(bf16[64,1280]{1,0:T(8,128)(2,1)S(1)} %get-tuple-element.55), channel_id=1, source_target_pairs={{0,16},{4,20},{8,24},{12,28},{16,0},{20,4},{24,8},{28,12},{1,17},{... | collective-permute-start | bytes 491528 | tf_op jit(solution)/shard_map/ppermute | solution.py:31
  157.0 8.8 %collective-permute-start.37 = (bf16[64,1280]{1,0:T(8,128)(2,1)S(1)}, bf16[64,1280]{1,0:T(8,128)(2,1)S(1)}, u32[]{:S(2)}, u32[]{:S(2)}) collective-permute-start(bf16[64,1280]{1,0:T(8,128)(2,1)S(1)} %get-tuple-element.56), channel_id=1, source_target_pairs={{0,24},{4,28},{8,16},{12,20},{16,8},{20,12},{24,0},{28,4},{1,25},{... | collective-permute-start | bytes 491528 | tf_op jit(solution)/shard_map/ppermute | solution.py:31
  (9 other events, 67.2 us)

commit v2 on v1

--- a/solution.py
+++ b/solution.py
@@ -16,15 +16,16 @@
 NN = (((1,), (0,)), ((), ()))
 NT = (((1,), (1,)), ((), ()))
 TN = (((0,), (0,)), ((), ()))
-VMEM_BYTES = 48 * 1024 * 1024
+VMEM_BYTES = 24 * 1024 * 1024
+ATTEND_VMEM_BYTES = 52 * 1024 * 1024
 
 
 def dot(a, b, dims):
     return lax.dot_general(a, b, dims, preferred_element_type=F32)
 
 
-def params():
-    return pltpu.CompilerParams(vmem_limit_bytes=VMEM_BYTES)
+def params(limit=VMEM_BYTES):
+    return pltpu.CompilerParams(vmem_limit_bytes=limit)
 
 
 def exchange(x, offset, axis):
@@ -116,15 +117,15 @@
                     keep_ref[b // 2, :, HD:] = dv
 
 
-def attend(place, kv, q, do, dq, before, low, count, last):
+def attend(place, kv, head, q, do, dq, before, low, count, last):
     n = len(kv)
-    blk, width = kv[0].shape
+    blk, width = kv[0].shape[0], 2 * HD
     qlen = q.shape[0]
     whole = lambda shape: pl.BlockSpec(shape, lambda h, s: (0,) * len(shape))
     column = pl.BlockSpec((qlen, HD), lambda h, s: (0, low + h))
     first = before is None
     operands = [*kv, q, do]
-    in_specs = [whole((blk, width))] * n + [column, column]
+    in_specs = [pl.BlockSpec((blk, width), lambda h, s: (0, head))] * n + [column, column]
     if not first:
         operands.append(before)
         in_specs.append(whole((n, blk, width)))
@@ -163,7 +164,7 @@
         ),
         out_shape=out_shape,
         input_output_aliases=aliases,
-        compiler_params=params(),
+        compiler_params=params(ATTEND_VMEM_BYTES),
         cost_estimate=pl.CostEstimate(
             flops=work * 2, bytes_accessed=8 * n * blk * width, transcendentals=0
         ),
@@ -171,19 +172,26 @@
     )(place, *operands)
 
 
-def pair_sum_kernel(keep_ref, got_ref, own_ref, *send_refs):
-    own_ref[...] = keep_ref[0] + got_ref[0].astype(F32)
-    for k, send_ref in enumerate(send_refs, 1):
-        send_ref[...] = (keep_ref[k] + got_ref[k].astype(F32)).astype(BF16)
-
-
-def pair_sum(keep, got):
-    half, blk, width = keep.shape
-    out_shape = [jax.ShapeDtypeStruct((blk, width), F32)]
-    out_shape += [jax.ShapeDtypeStruct((blk, width), BF16)] * (half - 1)
-    return pl.pallas_call(
-        pair_sum_kernel, out_shape=out_shape, compiler_params=params(), name="pair_sum"
-    )(keep, got)
+def pair_sum_kernel(heads, *refs):
+    keeps, gots, own_ref, send_refs = refs[:heads], refs[heads : 2 * heads], refs[2 * heads], refs[2 * heads + 1 :]
+    for a in range(heads):
+        span = pl.ds(a * 2 * HD, 2 * HD)
+        own_ref[:, span] = keeps[a][0] + gots[a][0].astype(F32)
+        for k, send_ref in enumerate(send_refs, 1):
+            send_ref[:, span] = (keeps[a][k] + gots[a][k].astype(F32)).astype(BF16)
+
+
+def pair_sum(keeps, gots):
+    half, blk, width = keeps[0].shape
+    heads = len(keeps)
+    out_shape = [jax.ShapeDtypeStruct((blk, heads * width), F32)]
+    out_shape += [jax.ShapeDtypeStruct((blk, heads * width), BF16)] * (half - 1)
+    return pl.pallas_call(
+        functools.partial(pair_sum_kernel, heads),
+        out_shape=out_shape,
+        compiler_params=params(),
+        name="pair_sum",
+    )(*keeps, *gots)
 
 
 def owner_sum_kernel(lanes, place, own_ref, *refs):
@@ -213,50 +221,65 @@
     )(place, own, *got)
 
 
-def weight_grad_kernel(heads, half, *refs):
-    n = 2 * half
-    x_refs, refs = refs[:n], refs[n:]
-    out_ref = refs[-1]
+def weight_grad_kernel(half, place, *refs):
+    x_refs, grad_refs, keep_ref, send_ref = refs[:half], refs[half : 2 * half], refs[2 * half], refs[2 * half + 1]
+    cols = keep_ref.shape[0]
+    mine = lax.rem(place[0], 2)
+    for order, out_ref in enumerate((keep_ref, send_ref)):
+        start = pl.multiple_of(lax.bitwise_xor(mine, order) * cols, HD)
+        total = None
+        for x_ref, grad_ref in zip(x_refs, grad_refs):
+            part = dot(x_ref[:, pl.ds(start, cols)], grad_ref[...], TN)
+            total = part if total is None else total + part
+        out_ref[...] = total
+
+
+def weight_grad(place, columns, gathered):
+    half = len(columns)
+    cols = columns[0].shape[1] // 2
+    shape = jax.ShapeDtypeStruct((cols, gathered[0].shape[1]), F32)
+    return pl.pallas_call(
+        functools.partial(weight_grad_kernel, half),
+        in_specs=[pl.BlockSpec(memory_space=pltpu.SMEM)] + [pl.BlockSpec(memory_space=pltpu.VMEM)] * (2 * half),
+        out_shape=[shape, shape],
+        compiler_params=params(),
+        name="weight_grad",
+    )(place, *columns, *gathered)
+
+
+def weight_sum_kernel(heads, keep_ref, got_ref, out_ref):
     for a in range(heads):
-        even, odd = refs[a * (half + 1) : a * (half + 1) + half], refs[a * (half + 1) + half]
-        total = None
-        for b in range(n):
-            grads = odd[b // 2] if b % 2 else even[b // 2][...]
-            part = dot(x_refs[b][...], grads, TN)
-            total = part if total is None else total + part
-        out_ref[:, 0, a * HD : (a + 1) * HD] = total[:, :HD]
-        out_ref[:, 1, a * HD : (a + 1) * HD] = total[:, HD:]
-
-
-def weight_grad(columns, gathered):
-    half = len(columns) // 2
-    heads = len(gathered)
-    operands = list(columns)
-    for blocks in gathered:
-        operands += blocks
-    return pl.pallas_call(
-        functools.partial(weight_grad_kernel, heads, half),
-        out_shape=jax.ShapeDtypeStruct((columns[0].shape[1], 2, heads * HD), F32),
-        compiler_params=params(),
-        name="weight_grad",
-    )(*operands)
+        for c in range(2):
+            span = pl.ds((2 * a + c) * HD, HD)
+            out_ref[:, c, a * HD : (a + 1) * HD] = keep_ref[:, span] + got_ref[:, span]
+
+
+def weight_sum(keep, got):
+    cols, features = keep.shape
+    heads = features // (2 * HD)
+    return pl.pallas_call(
+        functools.partial(weight_sum_kernel, heads),
+        out_shape=jax.ShapeDtypeStruct((cols, 2, heads * HD), F32),
+        compiler_params=params(),
+        name="weight_sum",
+    )(keep, got)
 
 
 def input_grad_kernel(heads, half, lanes, place, *refs):
-    block_refs, refs = refs[: heads * half], refs[heads * half :]
+    block_refs, refs = refs[:half], refs[half:]
     w_refs, out_refs, left = refs[:2], refs[2 : 2 + half], refs[2 + half]
     me, lane = place[0], place[1]
     rows = block_refs[0].shape[1]
     width = w_refs[0].shape[0]
     features = w_refs[0].shape[1] // 2
-    for a in range(heads):
-        for k in range(half):
-            for b in range(lanes):
+    for k in range(half):
+        for b in range(lanes):
+            for a in range(heads):
                 head = lax.bitwise_xor(lane, b) * heads + a
-                block = block_refs[a * half + k][b]
                 for c in range(2):
                     start = pl.multiple_of(c * features + head * HD, HD)
-                    left[k * rows : (k + 1) * rows, pl.ds(start, HD)] = block[:, c * HD : (c + 1) * HD]
+                    span = pl.ds((2 * a + c) * HD, HD)
+                    left[k * rows : (k + 1) * rows, pl.ds(start, HD)] = block_refs[k][b, :, span]
     mine = lax.rem(me, 2)
     for order, w_ref in enumerate(w_refs):
         start = pl.multiple_of(lax.bitwise_xor(mine, order) * width, HD)
@@ -266,19 +289,18 @@
 
 
 def input_grad(place, blocks, own_w, other_w):
-    heads, half = len(blocks), len(blocks[0])
-    lanes, rows, _ = blocks[0][0].shape
+    half = len(blocks)
+    lanes, rows, here = blocks[0].shape
     width, features = own_w.shape
-    flat = [block for head in blocks for block in head]
-    return pl.pallas_call(
-        functools.partial(input_grad_kernel, heads, half, lanes),
+    return pl.pallas_call(
+        functools.partial(input_grad_kernel, here // (2 * HD), half, lanes),
         in_specs=[pl.BlockSpec(memory_space=pltpu.SMEM)]
-        + [pl.BlockSpec(memory_space=pltpu.VMEM)] * (len(flat) + 2),
+        + [pl.BlockSpec(memory_space=pltpu.VMEM)] * (half + 2),
         out_shape=[jax.ShapeDtypeStruct((rows, 2 * width), BF16)] * half,
         scratch_shapes=[pltpu.VMEM((half * rows, features), BF16)],
         compiler_params=params(),
         name="input_grad",
-    )(place, *flat, own_w, other_w)
+    )(place, *blocks, own_w, other_w)
 
 
 def lay_rows_kernel(place, *refs):
@@ -312,50 +334,50 @@
     half = n // 2
     q, do = queries[0], grad_out[0]
 
-    kv = []
-    for a in range(heads):
-        own = jnp.concatenate([key_value[:, c, a * HD : (a + 1) * HD] for c in range(2)], axis=1)
-        blocks = [own] + [exchange(own, 2 * k, "sec") for k in range(1, half)]
-        kv.append([x for block in blocks for x in (block, exchange(block, 1, "sec"))])
-
-    cols = inputs.shape[1] // n
-    columns = []
-    for b in range(n):
-        part = lax.dynamic_slice_in_dim(inputs, lax.bitwise_xor(me, b) * cols, cols, axis=1)
-        columns.append(exchange(part, b, "sec") if b else part)
+    def across(blocks):
+        return [blocks[0]] + [exchange(blocks[k], 2 * k, "sec") for k in range(1, half)]
+
+    own = jnp.concatenate(
+        [key_value[:, c, a * HD : (a + 1) * HD] for a in range(heads) for c in range(2)], axis=1
+    )
+    near = across([own] * half)
+    kv = [x for block in near for x in (block, exchange(block, 1, "sec"))]
+
+    cols = 2 * inputs.shape[1] // n
+    inputs, near = lax.optimization_barrier((inputs, near))
+    columns = across(
+        [
+            lax.dynamic_slice_in_dim(inputs, lax.bitwise_xor(me // 2, k) * cols, cols, axis=1)
+            for k in range(half)
+        ]
+    )
     own_w = w_kv.reshape(w_kv.shape[0], -1)
     other_w = exchange(own_w, 1, "sec")
 
     dq = None
-    sums = []
+    keeps, gots = [], []
     for a in range(heads):
-        pieces = [group]
-        before = None
-        low = a * group
-        for i, count in enumerate(pieces):
-            last = i == len(pieces) - 1
-            out = attend(place, kv[a], q, do, dq, before, low, count, last)
-            dq = out[0]
-            low += count
-            if not last:
-                before = out[1]
-        sums.append(out[1:])
-
-    gathered, blocks = [], []
-    for keep, send in sums:
-        own, *sends = pair_sum(keep, exchange(send, 1, "sec"))
-        got = [exchange(x, 2 * k, "sec") for k, x in enumerate(sends, 1)]
-        mine, *by_lane = owner_sum(place, own, got, lanes)
-        even = [mine] + [exchange(mine, 2 * k, "sec") for k in range(1, half)]
-        odd = exchange(jnp.stack(even), 1, "sec")
-        gathered.append([*even, odd])
-        all_lanes = jnp.stack([by_lane[0]] + [exchange(by_lane[b], b, "lane") for b in range(1, lanes)])
-        blocks.append([all_lanes] + [exchange(all_lanes, 2 * k, "sec") for k in range(1, half)])
+        dq, keep, send = attend(place, kv, a, q, do, dq, None, a * group, group, True)
+        if a == heads - 1:
+            send, columns[1:] = lax.optimization_barrier((send, columns[1:]))
+        keeps.append(keep)
+        gots.append(exchange(send, 1, "sec"))
+
+    own, *sends = pair_sum(keeps, gots)
+    own, *got = across([own, *sends])
+    mine, *by_lane = owner_sum(place, own, got, lanes)
+    by_lane[1:] = [exchange(by_lane[b], b, "lane") for b in range(1, lanes)]
+    mine, by_lane[1:-1] = lax.optimization_barrier((mine, by_lane[1:-1]))
+    gathered = across([mine] * half)
+    blocks = across([jnp.stack(by_lane)] * half)
 
     rows = input_grad(place, blocks, own_w, other_w)
-    rows = [rows[0]] + [exchange(rows[k], 2 * k, "sec") for k in range(1, half)]
+    rows, gathered = lax.optimization_barrier((rows, gathered))
+    rows = across(rows)
+    keep, send = weight_grad(place, columns, gathered)
+    grad_w_kv = weight_sum(keep, exchange(send, 1, "sec"))
+    rows, grad_w_kv = lax.optimization_barrier((rows, grad_w_kv))
     grad_inputs = lay_rows(place, rows)
-    grad_w_kv = weight_grad(columns, gathered)
     return dq[None], grad_inputs, grad_w_kv
 
 

time: 167 us -> 132 us (0.79)
  starting transfers between devices: 55.7 us -> 27.9 us
  waiting for transfers between devices: 58.4 us -> 46.8 us
  Pallas kernels: 44.9 us -> 48.4 us
    ppermute x53 -> x29, starting transfers between devices: 55.7 us -> 27.9 us  [exchange(): lax.ppermute(x, axis, [(i, i ^ offset) for i in range(lax.axis_size(axis))])]
    ppermute x53 -> x29, waiting for transfers between devices: 58.4 us -> 46.8 us  [exchange(): lax.ppermute(x, axis, [(i, i ^ offset) for i in range(lax.axis_size(axis))])]
    pallas_call x2, Pallas kernels: 35.1 us -> 38.3 us  [attend(): pl.pallas_call(functools.partial(attend_kernel, n, first, last), grid_spe...]
    unnamed x9 -> x7, local copies, waits for them, and re-layouts: 2.7 us -> 4.51 us
  transfers between devices with their start and end apart: 53 -> 29, of which waited for: 20 -> 15; matrix products, arithmetic and copies ran while one was open for 3% -> 3% of each run, Pallas kernels for 26% -> 34%
where the time goes in v2:
time: 132 us
  Pallas kernels  48.4 us (37%)
  waiting for transfers between devices  46.8 us (35%)
  starting transfers between devices  27.9 us (21%)
  local copies, waits for them, and re-layouts  7.96 us (6%)
    ppermute x29, waiting for transfers between devices, exchange(): lax.ppermute(x, axis, [(i, i ^ offset) for i in range(lax.axis_size(axis))])  46.8 us
    pallas_call x2, Pallas kernels, attend(): pl.pallas_call(functools.partial(attend_kernel, n, first, last), grid_spe...  38.3 us
    ppermute x29, starting transfers between devices, exchange(): lax.ppermute(x, axis, [(i, i ^ offset) for i in range(lax.axis_size(axis))])  27.9 us
    unnamed x7, local copies, waits for them, and re-layouts  4.51 us
    pallas_call x1, Pallas kernels, input_grad(): pl.pallas_call(functools.partial(input_grad_kernel, here // (2 * HD), hal...  3.78 us
  transfers between devices with their start and end apart: 29, of which 15 were waited for; matrix products, arithmetic and copies ran while one was open for 3% of the time, Pallas kernels for 34%

profile of v2, /device:TPU:0, one launch (start us, length us, event | category | flops | bytes accessed | tf_op | source)
XLA Modules:
  0.0 132.0 jit_solution(9757241901614823479)
XLA Ops:
  0.6 1.5 %fusion = (bf16[256,1,128]{2,1,0:T(2,128)(2,1)S(1)}, bf16[256,1,128]{2,1,0:T(2,128)(2,1)S(1)}, bf16[256,1,128]{2,1,0:T(2,128)(2,1)S(1)}, bf16[256,1,128]{2,1,0:T(2,128)(2,1)S(1)}) fusion(bf16[256,2,256]{2,1,0:T(2,128)(2,1)} %param.6), kind=kLoop, calls=%fused_computation.11 | loop fusion | bytes 524288 | tf_op jit(solution)/shard_map/slice | solution.py:341
  2.3 3.0 %collective-permute-start.1 = (bf16[256,512]{1,0:T(8,128)(2,1)S(1)}, bf16[256,512]{1,0:T(8,128)(2,1)S(1)}, u32[]{:S(2)}, u32[]{:S(2)}) collective-permute-start(bf16[256,512]{1,0:T(8,128)(2,1)S(1)} %pad_maximum_fusion.refs_0_), channel_id=1, source_target_pairs={{0,8},{4,12},{8,0},{12,4},{16,24},{20,28},{24,16},{28,20},{1,9},{5... | collective-permute-start | bytes 786440 | tf_op jit(solution)/shard_map/ppermute | solution.py:32
  5.3 1.5 %collective-permute-start.3 = (bf16[256,512]{1,0:T(8,128)(2,1)S(1)}, bf16[256,512]{1,0:T(8,128)(2,1)S(1)}, u32[]{:S(2)}, u32[]{:S(2)}) collective-permute-start(bf16[256,512]{1,0:T(8,128)(2,1)S(1)} %pad_maximum_fusion.refs_0_), channel_id=1, source_target_pairs={{0,16},{4,20},{8,24},{12,28},{16,0},{20,4},{24,8},{28,12},{1,17},{... | collective-permute-start | bytes 786440 | tf_op jit(solution)/shard_map/ppermute | solution.py:32
  6.8 2.6 %copy.17 = bf16[80,8,2,1024]{3,1,2,0:T(8,128)(2,1)S(1)} copy(bf16[80,8,2,1024]{3,2,1,0:T(2,128)(2,1)} %bitcast.22) | data formatting | bytes 5242880
  9.4 0.6 collective-permute-start.21
  10.0 2.4 %collective-permute-done.1.refs_2_ = bf16[256,512]{1,0:T(8,128)(2,1)S(1)} collective-permute-done((bf16[256,512]{1,0:T(8,128)(2,1)S(1)}, bf16[256,512]{1,0:T(8,128)(2,1)S(1)}, u32[]{:S(2)}, u32[]{:S(2)}) %collective-permute-start.1) | collective-permute-done | bytes 262176 | tf_op jit(solution)/shard_map/ppermute | solution.py:32
  12.4 6.2 %collective-permute-done.3.refs_4_ = bf16[256,512]{1,0:T(8,128)(2,1)S(1)} collective-permute-done((bf16[256,512]{1,0:T(8,128)(2,1)S(1)}, bf16[256,512]{1,0:T(8,128)(2,1)S(1)}, u32[]{:S(2)}, u32[]{:S(2)}) %collective-permute-start.3) | collective-permute-done | bytes 262176 | tf_op jit(solution)/shard_map/ppermute | solution.py:32
  18.7 0.5 collective-permute-start.4
  19.2 1.9 %constant_dynamic-slice_fusion = (bf16[256,1280]{1,0:T(8,128)(2,1)S(1)}, bf16[256,1280]{1,0:T(8,128)(2,1)S(1)}, bf16[256,1280]{1,0:T(8,128)(2,1)S(1)}, bf16[256,1280]{1,0:T(8,128)(2,1)S(1)}) fusion(bf16[256,5120]{1,0:T(8,128)(2,1)} %param.8, s32[]{:T(128)S(6)} %select_n.24, s32[]{:T(128)S(6)} %select_n.23, s32[]{:T(128)S(6)} %select_n.22, s32[]{:T(128)S(6)} %select_n.21), kind=kLoop, calls=%fused_computation.6 | loop fusion | bytes 5242896 | tf_op jit(solution)/shard_map/dynamic_slice | solution.py:350
  21.1 1.4 %collective-permute-start.8 = (bf16[256,1280]{1,0:T(8,128)(2,1)S(1)}, bf16[256,1280]{1,0:T(8,128)(2,1)S(1)}, u32[]{:S(2)}, u32[]{:S(2)}) collective-permute-start(bf16[256,1280]{1,0:T(8,128)(2,1)S(1)} %get-tuple-element.90), channel_id=1, source_target_pairs={{0,8},{4,12},{8,0},{12,4},{16,24},{20,28},{24,16},{28,20},{1,9},{5... | collective-permute-start | bytes 1966088 | tf_op jit(solution)/shard_map/ppermute | solution.py:32
  22.5 0.7 collective-permute-start.9
  23.2 1.4 %collective-permute-start.10 = (bf16[256,1280]{1,0:T(8,128)(2,1)S(1)}, bf16[256,1280]{1,0:T(8,128)(2,1)S(1)}, u32[]{:S(2)}, u32[]{:S(2)}) collective-permute-start(bf16[256,1280]{1,0:T(8,128)(2,1)S(1)} %get-tuple-element.88), channel_id=1, source_target_pairs={{0,24},{4,28},{8,16},{12,20},{16,8},{20,12},{24,0},{28,4},{1,25},{... | collective-permute-start | bytes 1966088 | tf_op jit(solution)/shard_map/ppermute | solution.py:32
  24.6 0.7 copy-done.2
  25.3 19.2 %attend.2 = (bf16[384,1280]{1,0:T(8,128)(2,1)}, f32[4,256,256]{2,1,0:T(8,128)}, bf16[4,256,256]{2,1,0:T(8,128)(2,1)}) custom-call(s32[2]{0:T(128)S(1)} %pad_add_fusion.place, bf16[256,512]{1,0:T(8,128)(2,1)S(1)} %pad_maximum_fusion.refs_0_, bf16[256,512]{1,0:T(8,128)(2,1)} %collective-permute-done.refs_1_, ...), custom_call_target="tpu_custom_call" | custom-call | flops 10066329600 | bytes 4194304 | tf_op jit(solution)/shard_map/attend/pallas_call | solution.py:156
  44.5 19.2 %attend.3 = (bf16[384,1280]{1,0:T(8,128)(2,1)}, f32[4,256,256]{2,1,0:T(8,128)}, bf16[4,256,256]{2,1,0:T(8,128)(2,1)}) custom-call(s32[2]{0:T(128)S(1)} %pad_add_fusion.place, bf16[256,512]{1,0:T(8,128)(2,1)S(1)} %pad_maximum_fusion.refs_0_, bf16[256,512]{1,0:T(8,128)(2,1)} %collective-permute-done.refs_1_, ...), custom_call_target="tpu_custom_call", output_to_operand_aliasing={{0}: (11, {})} | custom-call | flops 10066329600 | bytes 4194304 | tf_op jit(solution)/shard_map/attend/pallas_call | solution.py:156
  63.7 0.6 collective-permute-start.11
  64.3 1.7 %collective-permute-done.11.refs_3_ = bf16[4,256,256]{2,1,0:T(8,128)(2,1)S(1)} collective-permute-done((bf16[4,256,256]{2,1,0:T(8,128)(2,1)}, bf16[4,256,256]{2,1,0:T(8,128)(2,1)S(1)}, u32[]{:S(2)}, u32[]{:S(2)}) %collective-permute-start.11) | collective-permute-done | bytes 524320 | tf_op jit(solution)/shard_map/ppermute | solution.py:32
  66.0 1.2 copy-done.1
  67.4 1.4 %collective-permute-start.12 = (bf16[256,512]{1,0:T(8,128)(2,1)S(1)}, bf16[256,512]{1,0:T(8,128)(2,1)S(1)}, u32[]{:S(2)}, u32[]{:S(2)}) collective-permute-start(bf16[256,512]{1,0:T(8,128)(2,1)S(1)} %get-tuple-element.54), channel_id=1, source_target_pairs={{0,8},{4,12},{8,0},{12,4},{16,24},{20,28},{24,16},{28,20},{1,9},{5... | collective-permute-start | bytes 786440 | tf_op jit(solution)/shard_map/ppermute | solution.py:32
  68.8 0.7 collective-permute-start.13
  69.6 1.4 %collective-permute-start.14 = (bf16[256,512]{1,0:T(8,128)(2,1)S(1)}, bf16[256,512]{1,0:T(8,128)(2,1)S(1)}, u32[]{:S(2)}, u32[]{:S(2)}) collective-permute-start(bf16[256,512]{1,0:T(8,128)(2,1)S(1)} %get-tuple-element.56), channel_id=1, source_target_pairs={{0,24},{4,28},{8,16},{12,20},{16,8},{20,12},{24,0},{28,4},{1,25},{... | collective-permute-start | bytes 786440 | tf_op jit(solution)/shard_map/ppermute | solution.py:32
  71.0 5.6 %collective-permute-done.12.refs_0_ = bf16[256,512]{1,0:T(8,128)(2,1)S(1)} collective-permute-done((bf16[256,512]{1,0:T(8,128)(2,1)S(1)}, bf16[256,512]{1,0:T(8,128)(2,1)S(1)}, u32[]{:S(2)}, u32[]{:S(2)}) %collective-permute-start.12) | collective-permute-done | bytes 262176 | tf_op jit(solution)/shard_map/ppermute | solution.py:32
  76.6 4.4 %collective-permute-done.13.refs_1_ = bf16[256,512]{1,0:T(8,128)(2,1)S(1)} collective-permute-done((bf16[256,512]{1,0:T(8,128)(2,1)S(1)}, bf16[256,512]{1,0:T(8,128)(2,1)S(1)}, u32[]{:S(2)}, u32[]{:S(2)}) %collective-permute-start.13) | collective-permute-done | bytes 262176 | tf_op jit(solution)/shard_map/ppermute | solution.py:32
  81.0 1.7 %collective-permute-done.14.refs_2_ = bf16[256,512]{1,0:T(8,128)(2,1)S(1)} collective-permute-done((bf16[256,512]{1,0:T(8,128)(2,1)S(1)}, bf16[256,512]{1,0:T(8,128)(2,1)S(1)}, u32[]{:S(2)}, u32[]{:S(2)}) %collective-permute-start.14) | collective-permute-done | bytes 262176 | tf_op jit(solution)/shard_map/ppermute | solution.py:32
  82.7 0.8 owner_sum.1
  83.5 1.7 %collective-permute-start.15 = (bf16[64,512]{1,0:T(8,128)(2,1)S(1)}, bf16[64,512]{1,0:T(8,128)(2,1)S(1)}, u32[]{:S(2)}, u32[]{:S(2)}) collective-permute-start(bf16[64,512]{1,0:T(8,128)(2,1)S(1)} %get-tuple-element.59), channel_id=1, source_target_pairs={{0,1},{1,0},{2,3},{3,2},{4,5},{5,4},{6,7},{7,6},{8,9},{9,8},{10,11... | collective-permute-start | bytes 196616 | tf_op jit(solution)/shard_map/ppermute | solution.py:32
  85.2 2.6 %collective-permute-start.16 = (bf16[64,512]{1,0:T(8,128)(2,1)S(1)}, bf16[64,512]{1,0:T(8,128)(2,1)S(1)}, u32[]{:S(2)}, u32[]{:S(2)}) collective-permute-start(bf16[64,512]{1,0:T(8,128)(2,1)S(1)} %get-tuple-element.60), channel_id=1, source_target_pairs={{0,2},{1,3},{2,0},{3,1},{4,6},{5,7},{6,4},{7,5},{8,10},{9,11},{10,... | collective-permute-start | bytes 196616 | tf_op jit(solution)/shard_map/ppermute | solution.py:32
  88.0 4.1 %collective-permute-done.16 = bf16[64,512]{1,0:T(8,128)(2,1)S(1)} collective-permute-done((bf16[64,512]{1,0:T(8,128)(2,1)S(1)}, bf16[64,512]{1,0:T(8,128)(2,1)S(1)}, u32[]{:S(2)}, u32[]{:S(2)}) %collective-permute-start.16) | collective-permute-done | bytes 65568 | tf_op jit(solution)/shard_map/ppermute | solution.py:32
  92.1 1.7 %collective-permute-done.17 = bf16[64,512]{1,0:T(8,128)(2,1)S(1)} collective-permute-done((bf16[64,512]{1,0:T(8,128)(2,1)S(1)}, bf16[64,512]{1,0:T(8,128)(2,1)S(1)}, u32[]{:S(2)}, u32[]{:S(2)}) %collective-permute-start.17) | collective-permute-done | bytes 65568 | tf_op jit(solution)/shard_map/ppermute | solution.py:32
  93.8 0.8 collective-permute-start.18
  94.6 1.5 %collective-permute-start.19 = (bf16[4,64,512]{2,1,0:T(8,128)(2,1)S(1)}, bf16[4,64,512]{2,1,0:T(8,128)(2,1)S(1)}, u32[]{:S(2)}, u32[]{:S(2)}) collective-permute-start(bf16[4,64,512]{2,1,0:T(8,128)(2,1)S(1)} %pad_maximum_fusion.1.refs_0_), channel_id=1, source_target_pairs={{0,16},{4,20},{8,24},{12,28},{16,0},{20,4},{24,8},{28,12},{1,17},{... | collective-permute-start | bytes 786440 | tf_op jit(solution)/shard_map/ppermute | solution.py:32
  96.1 1.3 collective-permute-start.20
  97.4 0.7 collective-permute-start.22
  98.1 5.1 %collective-permute-done.18.refs_1_ = bf16[4,64,512]{2,1,0:T(8,128)(2,1)S(1)} collective-permute-done((bf16[4,64,512]{2,1,0:T(8,128)(2,1)S(1)}, bf16[4,64,512]{2,1,0:T(8,128)(2,1)S(1)}, u32[]{:S(2)}, u32[]{:S(2)}) %collective-permute-start.18) | collective-permute-done | bytes 262176 | tf_op jit(solution)/shard_map/ppermute | solution.py:32
  103.2 0.8 collective-permute-start.23
  103.9 3.2 %collective-permute-done.19.refs_2_ = bf16[4,64,512]{2,1,0:T(8,128)(2,1)S(1)} collective-permute-done((bf16[4,64,512]{2,1,0:T(8,128)(2,1)S(1)}, bf16[4,64,512]{2,1,0:T(8,128)(2,1)S(1)}, u32[]{:S(2)}, u32[]{:S(2)}) %collective-permute-start.19) | collective-permute-done | bytes 262176 | tf_op jit(solution)/shard_map/ppermute | solution.py:32
  107.1 1.6 %collective-permute-start.24 = (bf16[256,512]{1,0:T(8,128)(2,1)S(1)}, bf16[256,512]{1,0:T(8,128)(2,1)S(1)}, u32[]{:S(2)}, u32[]{:S(2)}) collective-permute-start(bf16[256,512]{1,0:T(8,128)(2,1)S(1)} %get-tuple-element.76.refs_4_), channel_id=1, source_target_pairs={{0,24},{4,28},{8,16},{12,20},{16,8},{20,12},{24,0},{28,4},{1,25},{... | collective-permute-start | bytes 786440 | tf_op jit(solution)/shard_map/ppermute | solution.py:32
  109.1 3.8 %input_grad.1 = (bf16[64,1280]{1,0:T(8,128)(2,1)S(1)}, bf16[64,1280]{1,0:T(8,128)(2,1)S(1)}, bf16[64,1280]{1,0:T(8,128)(2,1)S(1)}, bf16[64,1280]{1,0:T(8,128)(2,1)S(1)}) custom-call(s32[2]{0:T(128)S(1)} %pad_add_fusion.place, bf16[4,64,512]{2,1,0:T(8,128)(2,1)S(1)} %pad_maximum_fusion.1.refs_0_, bf16[4,64,512]{2,1,0:T(8,128)(2,1)S(1)} %collective-permute-done.18.refs_1_, ...), custom_call_target="tpu_custom_call" | custom-call | tf_op jit(solution)/shard_map/input_grad/pallas_call | solution.py:295
  112.9 1.1 collective-permute-done.22.refs_5_
  114.0 3.1 %collective-permute-done.23.refs_6_ = bf16[256,512]{1,0:T(8,128)(2,1)S(1)} collective-permute-done((bf16[256,512]{1,0:T(8,128)(2,1)S(1)}, bf16[256,512]{1,0:T(8,128)(2,1)S(1)}, u32[]{:S(2)}, u32[]{:S(2)}) %collective-permute-start.23) | collective-permute-done | bytes 262176 | tf_op jit(solution)/shard_map/ppermute | solution.py:32
  117.1 2.1 %weight_grad.1 = (f32[640,512]{1,0:T(8,128)S(1)}, f32[640,512]{1,0:T(8,128)S(1)}) custom-call(s32[2]{0:T(128)S(1)} %pad_add_fusion.place, bf16[256,1280]{1,0:T(8,128)(2,1)S(1)} %get-tuple-element.87.refs_0_, bf16[256,1280]{1,0:T(8,128)(2,1)S(1)} %collective-permute-done.8.refs_1_, bf16[256,1280]{1,0:T(8,128)(2,1)S(1)} %collective-permute-done.9.refs_2_, ...), custom_call_target="tpu_custom_call" | custom-call | tf_op jit(solution)/shard_map/weight_grad/pallas_call | solution.py:241
  119.2 1.5 %collective-permute-start.25 = (bf16[64,1280]{1,0:T(8,128)(2,1)S(1)}, bf16[64,1280]{1,0:T(8,128)(2,1)S(1)}, u32[]{:S(2)}, u32[]{:S(2)}) collective-permute-start(bf16[64,1280]{1,0:T(8,128)(2,1)S(1)} %get-tuple-element.70), channel_id=1, source_target_pairs={{0,8},{4,12},{8,0},{12,4},{16,24},{20,28},{24,16},{28,20},{1,9},{5... | collective-permute-start | bytes 491528 | tf_op jit(solution)/shard_map/ppermute | solution.py:32
  120.8 0.6 collective-permute-start.26
  121.3 1.5 %collective-permute-start.27 = (bf16[64,1280]{1,0:T(8,128)(2,1)S(1)}, bf16[64,1280]{1,0:T(8,128)(2,1)S(1)}, u32[]{:S(2)}, u32[]{:S(2)}) collective-permute-start(bf16[64,1280]{1,0:T(8,128)(2,1)S(1)} %get-tuple-element.72), channel_id=1, source_target_pairs={{0,24},{4,28},{8,16},{12,20},{16,8},{20,12},{24,0},{28,4},{1,25},{... | collective-permute-start | bytes 491528 | tf_op jit(solution)/shard_map/ppermute | solution.py:32
  122.8 1.8 %weight_sum.1 = f32[640,2,256]{2,1,0:T(2,128)} custom-call(f32[640,512]{1,0:T(8,128)S(1)} %get-tuple-element.80.keep_ref, f32[640,512]{1,0:T(8,128)S(1)} %collective-permute-done.28.got_ref), custom_call_target="tpu_custom_call" | custom-call | tf_op jit(solution)/shard_map/weight_sum/pallas_call | solution.py:260
  124.6 1.7 %collective-permute-done.25.refs_1_ = bf16[64,1280]{1,0:T(8,128)(2,1)S(1)} collective-permute-done((bf16[64,1280]{1,0:T(8,128)(2,1)S(1)}, bf16[64,1280]{1,0:T(8,128)(2,1)S(1)}, u32[]{:S(2)}, u32[]{:S(2)}) %collective-permute-start.25) | collective-permute-done | bytes 163872 | tf_op jit(solution)/shard_map/ppermute | solution.py:32
  126.3 4.2 %collective-permute-done.26.refs_2_ = bf16[64,1280]{1,0:T(8,128)(2,1)S(1)} collective-permute-done((bf16[64,1280]{1,0:T(8,128)(2,1)S(1)}, bf16[64,1280]{1,0:T(8,128)(2,1)S(1)}, u32[]{:S(2)}, u32[]{:S(2)}) %collective-permute-start.26) | collective-permute-done | bytes 163872 | tf_op jit(solution)/shard_map/ppermute | solution.py:32
  130.6 1.4 %lay_rows.1 = bf16[64,5120]{1,0:T(8,128)(2,1)} custom-call(s32[2]{0:T(128)S(1)} %pad_add_fusion.place, bf16[64,1280]{1,0:T(8,128)(2,1)S(1)} %get-tuple-element.82.refs_0_, bf16[64,1280]{1,0:T(8,128)(2,1)S(1)} %collective-permute-done.25.refs_1_, bf16[64,1280]{1,0:T(8,128)(2,1)S(1)} %collective-permute-done.26.refs_2_, ...), custom_call_target="tpu_custom_call" | custom-call | tf_op jit(solution)/shard_map/lay_rows/pallas_call | solution.py:317
  (32 shorter events, 1.1 us)
Async XLA Ops:
  2.3 10.1 %collective-permute-start.1 = (bf16[256,512]{1,0:T(8,128)(2,1)S(1)}, bf16[256,512]{1,0:T(8,128)(2,1)S(1)}, u32[]{:S(2)}, u32[]{:S(2)}) collective-permute-start(bf16[256,512]{1,0:T(8,128)(2,1)S(1)} %pad_maximum_fusion.refs_0_), channel_id=1, source_target_pairs={{0,8},{4,12},{8,0},{12,4},{16,24},{20,28},{24,16},{28,20},{1,9},{5... | collective-permute-start | bytes 786440 | tf_op jit(solution)/shard_map/ppermute | solution.py:32
  5.3 13.4 %collective-permute-start.3 = (bf16[256,512]{1,0:T(8,128)(2,1)S(1)}, bf16[256,512]{1,0:T(8,128)(2,1)S(1)}, u32[]{:S(2)}, u32[]{:S(2)}) collective-permute-start(bf16[256,512]{1,0:T(8,128)(2,1)S(1)} %pad_maximum_fusion.refs_0_), channel_id=1, source_target_pairs={{0,16},{4,20},{8,24},{12,28},{16,0},{20,4},{24,8},{28,12},{1,17},{... | collective-permute-start | bytes 786440 | tf_op jit(solution)/shard_map/ppermute | solution.py:32
  6.8 11.9 %collective-permute-start.5 = (bf16[256,512]{1,0:T(8,128)(2,1)S(1)}, bf16[256,512]{1,0:T(8,128)(2,1)}, u32[]{:S(2)}, u32[]{:S(2)}) collective-permute-start(bf16[256,512]{1,0:T(8,128)(2,1)S(1)} %pad_maximum_fusion.refs_0_), channel_id=1, source_target_pairs={{0,24},{4,28},{8,16},{12,20},{16,8},{20,12},{24,0},{28,4},{1,25},{... | collective-permute-start | bytes 786440 | tf_op jit(solution)/shard_map/ppermute | solution.py:32
  6.8 14.2 %collective-permute-start = (bf16[256,512]{1,0:T(8,128)(2,1)S(1)}, bf16[256,512]{1,0:T(8,128)(2,1)}, u32[]{:S(2)}, u32[]{:S(2)}) collective-permute-start(bf16[256,512]{1,0:T(8,128)(2,1)S(1)} %pad_maximum_fusion.refs_0_), channel_id=1, source_target_pairs={{0,4},{4,0},{8,12},{12,8},{16,20},{20,16},{24,28},{28,24},{1,5},{5... | collective-permute-start | bytes 786440 | tf_op jit(solution)/shard_map/ppermute | solution.py:32
  9.4 99.7 %collective-permute-start.21 = (bf16[640,2048]{1,0:T(8,128)(2,1)S(1)}, bf16[640,2048]{1,0:T(8,128)(2,1)}, u32[]{:S(2)}, u32[]{:S(2)}) collective-permute-start(bf16[640,2048]{1,0:T(8,128)(2,1)S(1)} %bitcast.19), channel_id=1, source_target_pairs={{0,4},{4,0},{8,12},{12,8},{16,20},{20,16},{24,28},{28,24},{1,5},{5... | collective-permute-start | bytes 7864328 | tf_op jit(solution)/shard_map/ppermute | solution.py:32
  18.7 3.8 %collective-permute-start.2 = (bf16[256,512]{1,0:T(8,128)(2,1)S(1)}, bf16[256,512]{1,0:T(8,128)(2,1)S(1)}, u32[]{:S(2)}, u32[]{:S(2)}) collective-permute-start(bf16[256,512]{1,0:T(8,128)(2,1)S(1)} %collective-permute-done.1.refs_2_), channel_id=1, source_target_pairs={{0,4},{4,0},{8,12},{12,8},{16,20},{20,16},{24,28},{28,24},{1,5},{5... | collective-permute-start | bytes 786440 | tf_op jit(solution)/shard_map/ppermute | solution.py:32
  18.7 4.5 %collective-permute-start.4 = (bf16[256,512]{1,0:T(8,128)(2,1)S(1)}, bf16[256,512]{1,0:T(8,128)(2,1)S(1)}, u32[]{:S(2)}, u32[]{:S(2)}) collective-permute-start(bf16[256,512]{1,0:T(8,128)(2,1)S(1)} %collective-permute-done.3.refs_4_), channel_id=1, source_target_pairs={{0,4},{4,0},{8,12},{12,8},{16,20},{20,16},{24,28},{28,24},{1,5},{5... | collective-permute-start | bytes 786440 | tf_op jit(solution)/shard_map/ppermute | solution.py:32
  19.2 5.4 %collective-permute-start.6 = (bf16[256,512]{1,0:T(8,128)(2,1)}, bf16[256,512]{1,0:T(8,128)(2,1)S(1)}, u32[]{:S(2)}, u32[]{:S(2)}) collective-permute-start(bf16[256,512]{1,0:T(8,128)(2,1)} %collective-permute-done.5.refs_6_), channel_id=1, source_target_pairs={{0,4},{4,0},{8,12},{12,8},{16,20},{20,16},{24,28},{28,24},{1,5},{5... | collective-permute-start | bytes 786440 | tf_op jit(solution)/shard_map/ppermute | solution.py:32
  21.1 42.6 %collective-permute-start.8 = (bf16[256,1280]{1,0:T(8,128)(2,1)S(1)}, bf16[256,1280]{1,0:T(8,128)(2,1)S(1)}, u32[]{:S(2)}, u32[]{:S(2)}) collective-permute-start(bf16[256,1280]{1,0:T(8,128)(2,1)S(1)} %get-tuple-element.90), channel_id=1, source_target_pairs={{0,8},{4,12},{8,0},{12,4},{16,24},{20,28},{24,16},{28,20},{1,9},{5... | collective-permute-start | bytes 1966088 | tf_op jit(solution)/shard_map/ppermute | solution.py:32
  22.5 41.2 %collective-permute-start.9 = (bf16[256,1280]{1,0:T(8,128)(2,1)S(1)}, bf16[256,1280]{1,0:T(8,128)(2,1)S(1)}, u32[]{:S(2)}, u32[]{:S(2)}) collective-permute-start(bf16[256,1280]{1,0:T(8,128)(2,1)S(1)} %get-tuple-element.89), channel_id=1, source_target_pairs={{0,16},{4,20},{8,24},{12,28},{16,0},{20,4},{24,8},{28,12},{1,17},{... | collective-permute-start | bytes 1966088 | tf_op jit(solution)/shard_map/ppermute | solution.py:32
  23.2 40.5 %collective-permute-start.10 = (bf16[256,1280]{1,0:T(8,128)(2,1)S(1)}, bf16[256,1280]{1,0:T(8,128)(2,1)S(1)}, u32[]{:S(2)}, u32[]{:S(2)}) collective-permute-start(bf16[256,1280]{1,0:T(8,128)(2,1)S(1)} %get-tuple-element.88), channel_id=1, source_target_pairs={{0,24},{4,28},{8,16},{12,20},{16,8},{20,12},{24,0},{28,4},{1,25},{... | collective-permute-start | bytes 1966088 | tf_op jit(solution)/shard_map/ppermute | solution.py:32
  24.6 0.7 copy-start.2
  44.5 19.8 %collective-permute-start.7 = (bf16[4,256,256]{2,1,0:T(8,128)(2,1)}, bf16[4,256,256]{2,1,0:T(8,128)(2,1)S(1)}, u32[]{:S(2)}, u32[]{:S(2)}) collective-permute-start(bf16[4,256,256]{2,1,0:T(8,128)(2,1)} %get-tuple-element.49), channel_id=1, source_target_pairs={{0,4},{4,0},{8,12},{12,8},{16,20},{20,16},{24,28},{28,24},{1,5},{5... | collective-permute-start | bytes 1572872 | tf_op jit(solution)/shard_map/ppermute | solution.py:32
  44.5 21.5 %copy-start = (f32[4,256,256]{2,1,0:T(8,128)S(1)}, f32[4,256,256]{2,1,0:T(8,128)}, u32[]{:S(2)}) copy-start(f32[4,256,256]{2,1,0:T(8,128)} %get-tuple-element.47.refs_0_) | copy-start | bytes 3145732
  63.7 2.3 %collective-permute-start.11 = (bf16[4,256,256]{2,1,0:T(8,128)(2,1)}, bf16[4,256,256]{2,1,0:T(8,128)(2,1)S(1)}, u32[]{:S(2)}, u32[]{:S(2)}) collective-permute-start(bf16[4,256,256]{2,1,0:T(8,128)(2,1)} %get-tuple-element.52), channel_id=1, source_target_pairs={{0,4},{4,0},{8,12},{12,8},{16,20},{20,16},{24,28},{28,24},{1,5},{5... | collective-permute-start | bytes 1572872 | tf_op jit(solution)/shard_map/ppermute | solution.py:32
  66.0 1.2 copy-start.1
  67.4 9.2 %collective-permute-start.12 = (bf16[256,512]{1,0:T(8,128)(2,1)S(1)}, bf16[256,512]{1,0:T(8,128)(2,1)S(1)}, u32[]{:S(2)}, u32[]{:S(2)}) collective-permute-start(bf16[256,512]{1,0:T(8,128)(2,1)S(1)} %get-tuple-element.54), channel_id=1, source_target_pairs={{0,8},{4,12},{8,0},{12,4},{16,24},{20,28},{24,16},{28,20},{1,9},{5... | collective-permute-start | bytes 786440 | tf_op jit(solution)/shard_map/ppermute | solution.py:32
  68.8 12.2 %collective-permute-start.13 = (bf16[256,512]{1,0:T(8,128)(2,1)S(1)}, bf16[256,512]{1,0:T(8,128)(2,1)S(1)}, u32[]{:S(2)}, u32[]{:S(2)}) collective-permute-start(bf16[256,512]{1,0:T(8,128)(2,1)S(1)} %get-tuple-element.55), channel_id=1, source_target_pairs={{0,16},{4,20},{8,24},{12,28},{16,0},{20,4},{24,8},{28,12},{1,17},{... | collective-permute-start | bytes 786440 | tf_op jit(solution)/shard_map/ppermute | solution.py:32
  69.6 13.2 %collective-permute-start.14 = (bf16[256,512]{1,0:T(8,128)(2,1)S(1)}, bf16[256,512]{1,0:T(8,128)(2,1)S(1)}, u32[]{:S(2)}, u32[]{:S(2)}) collective-permute-start(bf16[256,512]{1,0:T(8,128)(2,1)S(1)} %get-tuple-element.56), channel_id=1, source_target_pairs={{0,24},{4,28},{8,16},{12,20},{16,8},{20,12},{24,0},{28,4},{1,25},{... | collective-permute-start | bytes 786440 | tf_op jit(solution)/shard_map/ppermute | solution.py:32
  83.5 4.5 %collective-permute-start.15 = (bf16[64,512]{1,0:T(8,128)(2,1)S(1)}, bf16[64,512]{1,0:T(8,128)(2,1)S(1)}, u32[]{:S(2)}, u32[]{:S(2)}) collective-permute-start(bf16[64,512]{1,0:T(8,128)(2,1)S(1)} %get-tuple-element.59), channel_id=1, source_target_pairs={{0,1},{1,0},{2,3},{3,2},{4,5},{5,4},{6,7},{7,6},{8,9},{9,8},{10,11... | collective-permute-start | bytes 196616 | tf_op jit(solution)/shard_map/ppermute | solution.py:32
  85.2 6.9 %collective-permute-start.16 = (bf16[64,512]{1,0:T(8,128)(2,1)S(1)}, bf16[64,512]{1,0:T(8,128)(2,1)S(1)}, u32[]{:S(2)}, u32[]{:S(2)}) collective-permute-start(bf16[64,512]{1,0:T(8,128)(2,1)S(1)} %get-tuple-element.60), channel_id=1, source_target_pairs={{0,2},{1,3},{2,0},{3,1},{4,6},{5,7},{6,4},{7,5},{8,10},{9,11},{10,... | collective-permute-start | bytes 196616 | tf_op jit(solution)/shard_map/ppermute | solution.py:32
  87.7 6.1 %collective-permute-start.17 = (bf16[64,512]{1,0:T(8,128)(2,1)S(1)}, bf16[64,512]{1,0:T(8,128)(2,1)S(1)}, u32[]{:S(2)}, u32[]{:S(2)}) collective-permute-start(bf16[64,512]{1,0:T(8,128)(2,1)S(1)} %get-tuple-element.63), channel_id=1, source_target_pairs={{0,3},{1,2},{2,1},{3,0},{4,7},{5,6},{6,5},{7,4},{8,11},{9,10},{10,... | collective-permute-start | bytes 196616 | tf_op jit(solution)/shard_map/ppermute | solution.py:32
  93.8 9.3 %collective-permute-start.18 = (bf16[4,64,512]{2,1,0:T(8,128)(2,1)S(1)}, bf16[4,64,512]{2,1,0:T(8,128)(2,1)S(1)}, u32[]{:S(2)}, u32[]{:S(2)}) collective-permute-start(bf16[4,64,512]{2,1,0:T(8,128)(2,1)S(1)} %pad_maximum_fusion.1.refs_0_), channel_id=1, source_target_pairs={{0,8},{4,12},{8,0},{12,4},{16,24},{20,28},{24,16},{28,20},{1,9},{5... | collective-permute-start | bytes 786440 | tf_op jit(solution)/shard_map/ppermute | solution.py:32
  94.6 12.5 %collective-permute-start.19 = (bf16[4,64,512]{2,1,0:T(8,128)(2,1)S(1)}, bf16[4,64,512]{2,1,0:T(8,128)(2,1)S(1)}, u32[]{:S(2)}, u32[]{:S(2)}) collective-permute-start(bf16[4,64,512]{2,1,0:T(8,128)(2,1)S(1)} %pad_maximum_fusion.1.refs_0_), channel_id=1, source_target_pairs={{0,16},{4,20},{8,24},{12,28},{16,0},{20,4},{24,8},{28,12},{1,17},{... | collective-permute-start | bytes 786440 | tf_op jit(solution)/shard_map/ppermute | solution.py:32
  96.1 12.9 %collective-permute-start.20 = (bf16[4,64,512]{2,1,0:T(8,128)(2,1)S(1)}, bf16[4,64,512]{2,1,0:T(8,128)(2,1)S(1)}, u32[]{:S(2)}, u32[]{:S(2)}) collective-permute-start(bf16[4,64,512]{2,1,0:T(8,128)(2,1)S(1)} %pad_maximum_fusion.1.refs_0_), channel_id=1, source_target_pairs={{0,24},{4,28},{8,16},{12,20},{16,8},{20,12},{24,0},{28,4},{1,25},{... | collective-permute-start | bytes 786440 | tf_op jit(solution)/shard_map/ppermute | solution.py:32
  97.4 16.6 %collective-permute-start.22 = (bf16[256,512]{1,0:T(8,128)(2,1)S(1)}, bf16[256,512]{1,0:T(8,128)(2,1)S(1)}, u32[]{:S(2)}, u32[]{:S(2)}) collective-permute-start(bf16[256,512]{1,0:T(8,128)(2,1)S(1)} %get-tuple-element.76.refs_4_), channel_id=1, source_target_pairs={{0,8},{4,12},{8,0},{12,4},{16,24},{20,28},{24,16},{28,20},{1,9},{5... | collective-permute-start | bytes 786440 | tf_op jit(solution)/shard_map/ppermute | solution.py:32
  103.2 13.9 %collective-permute-start.23 = (bf16[256,512]{1,0:T(8,128)(2,1)S(1)}, bf16[256,512]{1,0:T(8,128)(2,1)S(1)}, u32[]{:S(2)}, u32[]{:S(2)}) collective-permute-start(bf16[256,512]{1,0:T(8,128)(2,1)S(1)} %get-tuple-element.76.refs_4_), channel_id=1, source_target_pairs={{0,16},{4,20},{8,24},{12,28},{16,0},{20,4},{24,8},{28,12},{1,17},{... | collective-permute-start | bytes 786440 | tf_op jit(solution)/shard_map/ppermute | solution.py:32
  107.1 10.0 %collective-permute-start.24 = (bf16[256,512]{1,0:T(8,128)(2,1)S(1)}, bf16[256,512]{1,0:T(8,128)(2,1)S(1)}, u32[]{:S(2)}, u32[]{:S(2)}) collective-permute-start(bf16[256,512]{1,0:T(8,128)(2,1)S(1)} %get-tuple-element.76.refs_4_), channel_id=1, source_target_pairs={{0,24},{4,28},{8,16},{12,20},{16,8},{20,12},{24,0},{28,4},{1,25},{... | collective-permute-start | bytes 786440 | tf_op jit(solution)/shard_map/ppermute | solution.py:32
  119.2 3.6 %collective-permute-start.28 = (f32[640,512]{1,0:T(8,128)S(1)}, f32[640,512]{1,0:T(8,128)S(1)}, u32[]{:S(2)}, u32[]{:S(2)}) collective-permute-start(f32[640,512]{1,0:T(8,128)S(1)} %get-tuple-element.81), channel_id=1, source_target_pairs={{0,4},{4,0},{8,12},{12,8},{16,20},{20,16},{24,28},{28,24},{1,5},{5... | collective-permute-start | bytes 3932168 | tf_op jit(solution)/shard_map/ppermute | solution.py:32
  119.2 7.1 %collective-permute-start.25 = (bf16[64,1280]{1,0:T(8,128)(2,1)S(1)}, bf16[64,1280]{1,0:T(8,128)(2,1)S(1)}, u32[]{:S(2)}, u32[]{:S(2)}) collective-permute-start(bf16[64,1280]{1,0:T(8,128)(2,1)S(1)} %get-tuple-element.70), channel_id=1, source_target_pairs={{0,8},{4,12},{8,0},{12,4},{16,24},{20,28},{24,16},{28,20},{1,9},{5... | collective-permute-start | bytes 491528 | tf_op jit(solution)/shard_map/ppermute | solution.py:32
  120.8 9.8 %collective-permute-start.26 = (bf16[64,1280]{1,0:T(8,128)(2,1)S(1)}, bf16[64,1280]{1,0:T(8,128)(2,1)S(1)}, u32[]{:S(2)}, u32[]{:S(2)}) collective-permute-start(bf16[64,1280]{1,0:T(8,128)(2,1)S(1)} %get-tuple-element.71), channel_id=1, source_target_pairs={{0,16},{4,20},{8,24},{12,28},{16,0},{20,4},{24,8},{28,12},{1,17},{... | collective-permute-start | bytes 491528 | tf_op jit(solution)/shard_map/ppermute | solution.py:32
  121.3 9.2 %collective-permute-start.27 = (bf16[64,1280]{1,0:T(8,128)(2,1)S(1)}, bf16[64,1280]{1,0:T(8,128)(2,1)S(1)}, u32[]{:S(2)}, u32[]{:S(2)}) collective-permute-start(bf16[64,1280]{1,0:T(8,128)(2,1)S(1)} %get-tuple-element.72), channel_id=1, source_target_pairs={{0,24},{4,28},{8,16},{12,20},{16,8},{20,12},{24,0},{28,4},{1,25},{... | collective-permute-start | bytes 491528 | tf_op jit(solution)/shard_map/ppermute | solution.py:32

commit v3 on v2

v3 whole, which is shorter than its diff:
```python
import functools

import jax
import jax.numpy as jnp
from jax import lax
from jax.experimental import pallas as pl
from jax.experimental.pallas import tpu as pltpu
from jax.sharding import PartitionSpec as P

NQH = 40
KVH = 8
HD = 128
LOG2E = 1.4426950408889634
F32 = jnp.float32
BF16 = jnp.bfloat16
NN = (((1,), (0,)), ((), ()))
NT = (((1,), (1,)), ((), ()))
TN = (((0,), (0,)), ((), ()))
VMEM_BYTES = 24 * 1024 * 1024
ATTEND_VMEM_BYTES = 16 * 1024
SEG = 128
UNIT = 2


def dot(a, b, dims):
    return lax.dot_general(a, b, dims, preferred_element_type=F32)


def params(limit=VMEM_BYTES):
    return pltpu.CompilerParams(vmem_limit_bytes=limit)


def exchange(x, offset, axis):
    return lax.ppermute(x, axis, [(i, i ^ offset) for i in range(lax.axis_size(axis))])


def key_blocks(keys, qlen):
    first = keys - qlen
    blocks = []
    at = 0
    while at < keys:
        size = 2 * SEG if at + 2 * SEG <= first + SEG else SEG
        blocks.append((at, size, sum(first + qlen - t * SEG > at for t in range(qlen // SEG))))
        at += size
    return blocks


def attend_kernel(n, group, aliased, place, *refs):
    kv, refs = refs[:n], refs[n:]
    q_ref, do_ref = refs[:2]
    dq_ref, keep_ref, send_ref = refs[2 + aliased : 5 + aliased]
    k_s, v_s, q_s, do_s, qt_s, dot_s, s_s, dp_s, top_s, sum_s, weighted_s, acc = refs[5 + aliased :]
    qlen = q_ref.shape[0]
    keys = k_s.shape[0]
    blk = keys // n
    first = keys - qlen
    segments = qlen // SEG
    scale = HD**-0.5
    factor = scale * LOG2E
    me = place[0]

    def place_of(b):
        return pl.multiple_of(lax.bitwise_xor(me, b) * blk, blk)

    for b in range(n):
        k_s[pl.ds(place_of(b), blk), :] = kv[b][:, :HD]
        v_s[pl.ds(place_of(b), blk), :] = kv[b][:, HD:]

    units = [range(h, min(h + UNIT, group)) for h in range(0, group, UNIT)]
    at = 0
    for unit in units:
        for t in range(segments):
            low = qlen - (t + 1) * SEG
            for h in unit:
                x = q_ref[low : low + SEG, h * HD : (h + 1) * HD]
                y = do_ref[low : low + SEG, h * HD : (h + 1) * HD]
                q_s[at : at + SEG, :] = x
                do_s[at : at + SEG, :] = y
                qt_s[:, at : at + SEG] = x.T
                dot_s[:, at : at + SEG] = y.T
                at += SEG

    def spread(x):
        return jnp.broadcast_to(x, (x.shape[0], SEG))

    base = 0
    for index, unit in enumerate(units):
        width = len(unit) * SEG
        whole = width * segments
        blocks = [(k0, size, seen * width) for k0, size, seen in key_blocks(keys, qlen)]

        for k0, size, high in blocks:
            s = dot(q_s[base : base + high, :], k_s[k0 : k0 + size, :], NT)
            top = None
            for k in range(k0, k0 + size, SEG):
                piece = s[:, k - k0 : k - k0 + SEG]
                last = first + qlen - high // width * SEG
                if k + SEG - 1 > last:
                    edge = piece[high - width :]
                    key = k + lax.broadcasted_iota(jnp.int32, edge.shape, 1)
                    row = last + lax.rem(lax.broadcasted_iota(jnp.int32, edge.shape, 0), SEG)
                    edge = jnp.where(key <= row, edge, -jnp.inf)
                    piece = edge if high == width else jnp.concatenate([piece[: high - width], edge], axis=0)
                s_s[:high, k : k + SEG] = piece
                top = piece if top is None else jnp.maximum(top, piece)
            top_s[:high, :] = top if k0 == 0 else jnp.maximum(top_s[:high, :], top)
        top_s[:whole, :] = spread(jnp.max(top_s[:whole, :], axis=1, keepdims=True) * factor)

        for k0, size, high in blocks:
            dp = dot(do_s[base : base + high, :], v_s[k0 : k0 + size, :], NT)
            total = weighted = None
            for k in range(k0, k0 + size, SEG):
                p = jnp.exp2(s_s[:high, k : k + SEG] * factor - top_s[:high, :])
                s_s[:high, k : k + SEG] = p
                piece = dp[:, k - k0 : k - k0 + SEG]
                dp_s[:high, k : k + SEG] = piece
                total = p if total is None else total + p
                weighted = p * piece if weighted is None else weighted + p * piece
            sum_s[:high, :] = total if k0 == 0 else sum_s[:high, :] + total
            weighted_s[:high, :] = weighted if k0 == 0 else weighted_s[:high, :] + weighted
        inverse = 1.0 / jnp.sum(sum_s[:whole, :], axis=1, keepdims=True)
        delta = jnp.sum(weighted_s[:whole, :], axis=1, keepdims=True) * inverse
        sum_s[:whole, :] = spread(inverse)
        weighted_s[:whole, :] = spread(delta)

        dq = None
        for k0, size, high in blocks:
            low_parts, ds_parts = [], []
            for k in range(k0, k0 + size, SEG):
                p = s_s[:high, k : k + SEG] * sum_s[:high, :]
                ds_parts.append((p * (dp_s[:high, k : k + SEG] - weighted_s[:high, :])).astype(BF16))
                low_parts.append(p.astype(BF16))
            low = jnp.concatenate(low_parts, axis=1)
            ds = jnp.concatenate(ds_parts, axis=1)
            dv = dot(dot_s[:, base : base + high], low, NN)
            dk = dot(qt_s[:, base : base + high], ds, NN)
            if index:
                dv = acc[HD:, k0 : k0 + size] + dv
                dk = acc[:HD, k0 : k0 + size] + dk
            acc[HD:, k0 : k0 + size] = dv
            acc[:HD, k0 : k0 + size] = dk
            part = dot(ds, k_s[k0 : k0 + size, :], NN)
            if dq is None:
                dq = part
            elif high == whole:
                dq = dq + part
            else:
                dq = jnp.concatenate([dq[:high] + part, dq[high:]], axis=0)
        dq = (dq * scale).astype(BF16)
        at = 0
        for t in range(segments):
            low = qlen - (t + 1) * SEG
            for h in unit:
                dq_ref[low : low + SEG, h * HD : (h + 1) * HD] = dq[at : at + SEG]
                at += SEG
        base += whole

    for b in range(n):
        dk = acc[:HD, pl.ds(place_of(b), blk)] * scale
        dv = acc[HD:, pl.ds(place_of(b), blk)]
        if b % 2:
            send_ref[b // 2, :HD, :] = dk.astype(BF16)
            send_ref[b // 2, HD:, :] = dv.astype(BF16)
        else:
            keep_ref[b // 2, :HD, :] = dk
            keep_ref[b // 2, HD:, :] = dv


def attend(place, kv, head, q, do, dq, group):
    n = len(kv)
    blk, width = kv[0].shape[0], 2 * HD
    qlen = q.shape[0]
    keys = n * blk
    column = pl.BlockSpec((qlen, group * HD), lambda i, s: (0, head))
    full = lambda shape: pl.BlockSpec(shape, lambda i, s: (0,) * len(shape))
    in_specs = [pl.BlockSpec((blk, width), lambda i, s: (0, head))] * n + [column, column]
    operands = [*kv, q, do]
    aliases = {}
    if dq is not None:
        aliases = {1 + len(operands): 0}
        operands.append(dq)
        in_specs.append(pl.BlockSpec(memory_space=pl.ANY))
    rows = min(UNIT, group) * qlen
    parts = (n // 2, width, blk)
    work = group * qlen * keys * HD * 10
    return pl.pallas_call(
        functools.partial(attend_kernel, n, group, dq is not None),
        grid_spec=pltpu.PrefetchScalarGridSpec(
            num_scalar_prefetch=1,
            grid=(1,),
            in_specs=in_specs,
            out_specs=[column, full(parts), full(parts)],
            scratch_shapes=[
                pltpu.VMEM((keys, HD), BF16),
                pltpu.VMEM((keys, HD), BF16),
                pltpu.VMEM((group * qlen, HD), BF16),
                pltpu.VMEM((group * qlen, HD), BF16),
                pltpu.VMEM((HD, group * qlen), BF16),
                pltpu.VMEM((HD, group * qlen), BF16),
                pltpu.VMEM((rows, keys), F32),
                pltpu.VMEM((rows, keys), F32),
                pltpu.VMEM((rows, SEG), F32),
                pltpu.VMEM((rows, SEG), F32),
                pltpu.VMEM((rows, SEG), F32),
                pltpu.VMEM((width, keys), F32),
            ],
        ),
        out_shape=[
            jax.ShapeDtypeStruct(q.shape, BF16),
            jax.ShapeDtypeStruct(parts, F32),
            jax.ShapeDtypeStruct(parts, BF16),
        ],
        input_output_aliases=aliases,
        compiler_params=params(keys * ATTEND_VMEM_BYTES),
        cost_estimate=pl.CostEstimate(flops=work * 2, bytes_accessed=8 * keys * width, transcendentals=0),
        name="attend",
    )(place, *operands)


def pair_sum_kernel(heads, *refs):
    keeps, gots, own_ref, send_refs = refs[:heads], refs[heads : 2 * heads], refs[2 * heads], refs[2 * heads + 1 :]
    for a in range(heads):
        span = pl.ds(a * 2 * HD, 2 * HD)
        own_ref[span, :] = keeps[a][0] + gots[a][0].astype(F32)
        for k, send_ref in enumerate(send_refs, 1):
            send_ref[span, :] = (keeps[a][k] + gots[a][k].astype(F32)).astype(BF16)


def pair_sum(keeps, gots):
    half, width, blk = keeps[0].shape
    heads = len(keeps)
    out_shape = [jax.ShapeDtypeStruct((heads * width, blk), F32)]
    out_shape += [jax.ShapeDtypeStruct((heads * width, blk), BF16)] * (half - 1)
    return pl.pallas_call(
        functools.partial(pair_sum_kernel, heads),
        out_shape=out_shape,
        compiler_params=params(),
        name="pair_sum",
    )(*keeps, *gots)


def owner_sum_kernel(lanes, place, own_ref, *refs):
    got_refs = refs[: -1 - lanes]
    sum_ref, lane_refs = refs[-1 - lanes], refs[-lanes:]
    total = own_ref[...]
    for got_ref in got_refs:
        total = total + got_ref[...].astype(F32)
    sum_ref[...] = total.astype(BF16).T
    rows = lane_refs[0].shape[0]
    for b, lane_ref in enumerate(lane_refs):
        start = pl.multiple_of(lax.bitwise_xor(place[1], b) * rows, rows)
        lane_ref[...] = sum_ref[pl.ds(start, rows), :]


def owner_sum(place, own, got, lanes):
    width, blk = own.shape
    out_shape = [jax.ShapeDtypeStruct((blk, width), BF16)]
    out_shape += [jax.ShapeDtypeStruct((blk // lanes, width), BF16)] * lanes
    return pl.pallas_call(
        functools.partial(owner_sum_kernel, lanes),
        in_specs=[pl.BlockSpec(memory_space=pltpu.SMEM)]
        + [pl.BlockSpec(memory_space=pltpu.VMEM)] * (1 + len(got)),
        out_shape=out_shape,
        compiler_params=params(),
        name="owner_sum",
    )(place, own, *got)


def weight_grad_kernel(half, place, *refs):
    x_refs, grad_refs, keep_ref, send_ref = refs[:half], refs[half:-2], refs[-2], refs[-1]
    cols = keep_ref.shape[0]
    mine = lax.rem(place[0], 2)
    for order, out_ref in enumerate((keep_ref, send_ref)):
        start = pl.multiple_of(lax.bitwise_xor(mine, order) * cols, HD)
        total = None
        for x_ref, grad_ref in zip(x_refs, grad_refs):
            part = dot(x_ref[:, pl.ds(start, cols)], grad_ref[...], TN)
            total = part if total is None else total + part
        out_ref[...] = total


def weight_grad(place, columns, gathered):
    half = len(columns)
    cols = columns[0].shape[1] // 2
    shape = jax.ShapeDtypeStruct((cols, gathered[0].shape[1]), F32)
    return pl.pallas_call(
        functools.partial(weight_grad_kernel, half),
        in_specs=[pl.BlockSpec(memory_space=pltpu.SMEM)] + [pl.BlockSpec(memory_space=pltpu.VMEM)] * (2 * half),
        out_shape=[shape, shape],
        compiler_params=params(),
        name="weight_grad",
    )(place, *columns, *gathered)


def weight_sum_kernel(heads, keep_ref, got_ref, out_ref):
    for a in range(heads):
        for c in range(2):
            span = pl.ds((2 * a + c) * HD, HD)
            out_ref[:, c, a * HD : (a + 1) * HD] = keep_ref[:, span] + got_ref[:, span]


def weight_sum(keep, got):
    cols, features = keep.shape
    heads = features // (2 * HD)
    return pl.pallas_call(
        functools.partial(weight_sum_kernel, heads),
        out_shape=jax.ShapeDtypeStruct((cols, 2, heads * HD), F32),
        compiler_params=params(),
        name="weight_sum",
    )(keep, got)


def input_grad_kernel(heads, half, lanes, place, *refs):
    block_refs, refs = refs[:half], refs[half:]
    w_refs, out_refs, left = refs[:2], refs[2 : 2 + half], refs[2 + half]
    me, lane = place[0], place[1]
    rows = block_refs[0].shape[1]
    width = w_refs[0].shape[0]
    features = w_refs[0].shape[1] // 2
    for k in range(half):
        for b in range(lanes):
            for a in range(heads):
                head = lax.bitwise_xor(lane, b) * heads + a
                for c in range(2):
                    start = pl.multiple_of(c * features + head * HD, HD)
                    span = pl.ds((2 * a + c) * HD, HD)
                    left[k * rows : (k + 1) * rows, pl.ds(start, HD)] = block_refs[k][b, :, span]
    mine = lax.rem(me, 2)
    for order, w_ref in enumerate(w_refs):
        start = pl.multiple_of(lax.bitwise_xor(mine, order) * width, HD)
        result = dot(left[...], w_ref[...], NT).astype(BF16)
        for k in range(half):
            out_refs[k][:, pl.ds(start, width)] = result[k * rows : (k + 1) * rows]


def input_grad(place, blocks, own_w, other_w):
    half = len(blocks)
    lanes, rows, here = blocks[0].shape
    width, features = own_w.shape
    return pl.pallas_call(
        functools.partial(input_grad_kernel, here // (2 * HD), half, lanes),
        in_specs=[pl.BlockSpec(memory_space=pltpu.SMEM)]
        + [pl.BlockSpec(memory_space=pltpu.VMEM)] * (len(blocks) + 2),
        out_shape=[jax.ShapeDtypeStruct((rows, 2 * width), BF16)] * half,
        scratch_shapes=[pltpu.VMEM((half * rows, features), BF16)],
        compiler_params=params(),
        name="input_grad",
    )(place, *blocks, own_w, other_w)


def lay_rows_kernel(place, *refs):
    blocks, out_ref, sems = refs[:-2], refs[-2], refs[-1]
    width = blocks[0].shape[1]
    chip = lax.div(place[0], 2)
    copies = []
    for k, block in enumerate(blocks):
        start = pl.multiple_of(lax.bitwise_xor(chip, k) * width, HD)
        copies.append(pltpu.make_async_copy(block, out_ref.at[:, pl.ds(start, width)], sems.at[k]))
        copies[-1].start()
    for copy in copies:
        copy.wait()


def lay_rows(place, blocks):
    rows, width = blocks[0].shape
    count = len(blocks)
    return pl.pallas_call(
        lay_rows_kernel,
        in_specs=[pl.BlockSpec(memory_space=pltpu.SMEM)] + [pl.BlockSpec(memory_space=pl.ANY)] * count,
        out_specs=pl.BlockSpec(memory_space=pl.ANY),
        out_shape=jax.ShapeDtypeStruct((rows, width * count), BF16),
        scratch_shapes=[pltpu.SemaphoreType.DMA((count,))],
        compiler_params=params(),
        name="lay_rows",
    )(place, *blocks)


def local(queries, key_value, grad_out, inputs, w_kv):
    n = lax.axis_size("sec")
    lanes = lax.axis_size("lane")
    me = lax.axis_index("sec")
    place = jnp.stack([me, lax.axis_index("lane")]).astype(jnp.int32)
    heads = key_value.shape[2] // HD
    group = NQH // KVH
    half = n // 2
    q, do = queries[0], grad_out[0]

    def across(blocks):
        return [blocks[0]] + [exchange(blocks[k], 2 * k, "sec") for k in range(1, half)]

    own = jnp.concatenate(
        [key_value[:, c, a * HD : (a + 1) * HD] for a in range(heads) for c in range(2)], axis=1
    )
    near = across([own] * half)
    kv = [x for block in near for x in (block, exchange(block, 1, "sec"))]

    cols = 2 * inputs.shape[1] // n
    columns = [
        lax.dynamic_slice_in_dim(inputs, lax.bitwise_xor(me // 2, k) * cols, cols, axis=1)
        for k in range(half)
    ]
    columns, near = lax.optimization_barrier((columns, near))
    columns = across(columns)
    own_w = w_kv.reshape(w_kv.shape[0], -1)
    other_w = exchange(own_w, 1, "sec")

    dq = None
    keeps, gots = [], []
    for a in range(heads):
        dq, keep, send = attend(place, kv, a, q, do, dq, group)
        if a == heads - 1:
            keep, columns[1:] = lax.optimization_barrier((keep, columns[1:]))
        keeps.append(keep)
        gots.append(exchange(send, 1, "sec"))

    own, *sends = pair_sum(keeps, gots)
    _, *got = across([own, *sends])
    mine, *by_lane = owner_sum(place, own, got, lanes)
    by_lane[1:] = [exchange(by_lane[b], b, "lane") for b in range(1, lanes)]
    gathered = across([mine] * half)
    blocks = across([jnp.stack(by_lane)] * half)
    blocks, gathered = lax.optimization_barrier((blocks, gathered))

    rows = list(input_grad(place, blocks, own_w, other_w))
    rows[0], gathered = lax.optimization_barrier((rows[0], gathered))
    rows = across(rows)
    keep, send = weight_grad(place, columns, gathered)
    grad_w_kv = weight_sum(keep, exchange(send, 1, "sec"))
    rows, grad_w_kv = lax.optimization_barrier((rows, grad_w_kv))
    grad_inputs = lay_rows(place, rows)
    return dq[None], grad_inputs, grad_w_kv


def solution(mesh):
    in_specs = (
        P("sec", None, "lane"),
        P("sec", None, "lane"),
        P("sec", None, "lane"),
        P("sec", None),
        P("sec", None, None),
    )
    out_specs = (P("sec", None, "lane"), P(("sec", "lane"), None), P("sec", None, "lane"))
    return jax.shard_map(local, mesh=mesh, in_specs=in_specs, out_specs=out_specs, check_vma=False)
```

time: 132 us -> 118 us (0.89)
  Pallas kernels: 48.4 us -> 39.3 us
  waiting for transfers between devices: 46.8 us -> 40.7 us
  starting transfers between devices: 27.9 us -> 31.1 us
  local copies, waits for them, and re-layouts: 7.96 us -> 6.01 us
    pallas_call x2, Pallas kernels: 38.3 us -> 29.3 us  [attend(): pl.pallas_call(functools.partial(attend_kernel, n, group, dq is not None)...]
    ppermute x29, waiting for transfers between devices: 46.8 us -> 40.7 us  [exchange(): lax.ppermute(x, axis, [(i, i ^ offset) for i in range(lax.axis_size(axis))])]
    ppermute x29, starting transfers between devices: 27.9 us -> 31.1 us  [exchange(): lax.ppermute(x, axis, [(i, i ^ offset) for i in range(lax.axis_size(axis))])]
    unnamed x7 -> x5, local copies, waits for them, and re-layouts: 4.51 us -> 2.57 us
  transfers between devices with their start and end apart: 29 -> 29, of which waited for: 15 -> 16; matrix products, arithmetic and copies ran while one was open for 3% -> 4% of each run, Pallas kernels for 34% -> 27%
where the time goes in v3:
time: 118 us
  waiting for transfers between devices  40.7 us (34%)
  Pallas kernels  39.3 us (33%)
  starting transfers between devices  31.1 us (26%)
  local copies, waits for them, and re-layouts  6.01 us (5%)
    ppermute x29, waiting for transfers between devices, exchange(): lax.ppermute(x, axis, [(i, i ^ offset) for i in range(lax.axis_size(axis))])  40.7 us
    ppermute x29, starting transfers between devices, exchange(): lax.ppermute(x, axis, [(i, i ^ offset) for i in range(lax.axis_size(axis))])  31.1 us
    pallas_call x2, Pallas kernels, attend(): pl.pallas_call(functools.partial(attend_kernel, n, group, dq is not None)...  29.3 us
    pallas_call x1, Pallas kernels, input_grad(): pl.pallas_call(functools.partial(input_grad_kernel, here // (2 * HD), hal...  3.78 us
    unnamed x5, local copies, waits for them, and re-layouts  2.57 us
  transfers between devices with their start and end apart: 29, of which 16 were waited for; matrix products, arithmetic and copies ran while one was open for 4% of the time, Pallas kernels for 27%

profile of v3, /device:TPU:0, one launch (start us, length us, event | category | flops | bytes accessed | tf_op | source)
XLA Modules:
  0.0 118.2 jit_solution(11120512806890795418)
XLA Ops:
  0.6 1.5 %fusion = (bf16[256,1,128]{2,1,0:T(2,128)(2,1)S(1)}, bf16[256,1,128]{2,1,0:T(2,128)(2,1)S(1)}, bf16[256,1,128]{2,1,0:T(2,128)(2,1)S(1)}, bf16[256,1,128]{2,1,0:T(2,128)(2,1)S(1)}) fusion(bf16[256,2,256]{2,1,0:T(2,128)(2,1)} %param.6), kind=kLoop, calls=%fused_computation.11 | loop fusion | bytes 524288 | tf_op jit(solution)/shard_map/slice | solution.py:392
  2.3 4.0 %collective-permute-start.5 = (bf16[256,512]{1,0:T(8,128)(2,1)S(1)}, bf16[256,512]{1,0:T(8,128)(2,1)S(1)}, u32[]{:S(2)}, u32[]{:S(2)}) collective-permute-start(bf16[256,512]{1,0:T(8,128)(2,1)S(1)} %pad_maximum_fusion.refs_0_), channel_id=1, source_target_pairs={{0,24},{4,28},{8,16},{12,20},{16,8},{20,12},{24,0},{28,4},{1,25},{... | collective-permute-start | bytes 786440 | tf_op jit(solution)/shard_map/ppermute | solution.py:34
  6.2 0.5 collective-permute-start.3
  6.9 2.6 %copy.17 = bf16[80,8,2,1024]{3,1,2,0:T(8,128)(2,1)S(1)} copy(bf16[80,8,2,1024]{3,2,1,0:T(2,128)(2,1)} %bitcast.26) | data formatting | bytes 5242880
  9.5 0.6 collective-permute-start.24
  10.1 3.3 %collective-permute-done.5.refs_6_ = bf16[256,512]{1,0:T(8,128)(2,1)S(1)} collective-permute-done((bf16[256,512]{1,0:T(8,128)(2,1)S(1)}, bf16[256,512]{1,0:T(8,128)(2,1)S(1)}, u32[]{:S(2)}, u32[]{:S(2)}) %collective-permute-start.5) | collective-permute-done | bytes 262176 | tf_op jit(solution)/shard_map/ppermute | solution.py:34
  13.4 4.7 %collective-permute-done.3.refs_4_ = bf16[256,512]{1,0:T(8,128)(2,1)S(1)} collective-permute-done((bf16[256,512]{1,0:T(8,128)(2,1)S(1)}, bf16[256,512]{1,0:T(8,128)(2,1)S(1)}, u32[]{:S(2)}, u32[]{:S(2)}) %collective-permute-start.3) | collective-permute-done | bytes 262176 | tf_op jit(solution)/shard_map/ppermute | solution.py:34
  18.3 0.3 collective-permute-done.1.refs_2_
  18.7 1.9 %constant_dynamic-slice_fusion = (bf16[256,1280]{1,0:T(8,128)(2,1)S(1)}, bf16[256,1280]{1,0:T(8,128)(2,1)S(1)}, bf16[256,1280]{1,0:T(8,128)(2,1)S(1)}, bf16[256,1280]{1,0:T(8,128)(2,1)S(1)}) fusion(bf16[256,5120]{1,0:T(8,128)(2,1)} %param.8, s32[]{:T(128)S(6)} %select_n.24, s32[]{:T(128)S(6)} %select_n.22, s32[]{:T(128)S(6)} %select_n.21, s32[]{:T(128)S(6)} %select_n.23), kind=kLoop, calls=%fused_computation.6 | loop fusion | bytes 5242896 | tf_op jit(solution)/shard_map/dynamic_slice | solution.py:399
  20.5 1.7 %collective-permute-start.7 = (bf16[256,1280]{1,0:T(8,128)(2,1)S(1)}, bf16[256,1280]{1,0:T(8,128)(2,1)S(1)}, u32[]{:S(2)}, u32[]{:S(2)}) collective-permute-start(bf16[256,1280]{1,0:T(8,128)(2,1)S(1)} %get-tuple-element.54), channel_id=1, source_target_pairs={{0,8},{4,12},{8,0},{12,4},{16,24},{20,28},{24,16},{28,20},{1,9},{5... | collective-permute-start | bytes 1966088 | tf_op jit(solution)/shard_map/ppermute | solution.py:34
  22.3 0.7 collective-permute-start.8
  23.0 1.1 collective-permute-start.9
  24.2 14.6 %attend.2 = (bf16[384,1280]{1,0:T(8,128)(2,1)}, f32[4,256,256]{2,1,0:T(8,128)S(1)}, bf16[4,256,256]{2,1,0:T(8,128)(2,1)S(1)}) custom-call(s32[2]{0:T(128)S(1)} %pad_add_fusion.place, bf16[256,512]{1,0:T(8,128)(2,1)S(1)} %pad_maximum_fusion.refs_0_, bf16[256,512]{1,0:T(8,128)(2,1)} %collective-permute-done.refs_1_, ...), custom_call_target="tpu_custom_call" | custom-call | flops 10066329600 | bytes 4194304 | tf_op jit(solution)/shard_map/attend/pallas_call | solution.py:186
  38.8 14.7 %attend.3 = (bf16[384,1280]{1,0:T(8,128)(2,1)}, f32[4,256,256]{2,1,0:T(8,128)S(1)}, bf16[4,256,256]{2,1,0:T(8,128)(2,1)S(1)}) custom-call(s32[2]{0:T(128)S(1)} %pad_add_fusion.place, bf16[256,512]{1,0:T(8,128)(2,1)S(1)} %pad_maximum_fusion.refs_0_, bf16[256,512]{1,0:T(8,128)(2,1)} %collective-permute-done.refs_1_, ...), custom_call_target="tpu_custom_call", output_to_operand_aliasing={{0}: (11, {})} | custom-call | flops 10066329600 | bytes 4194304 | tf_op jit(solution)/shard_map/attend/pallas_call | solution.py:186
  53.5 0.5 collective-permute-start.10
  54.0 1.4 %collective-permute-done.11.refs_3_ = bf16[4,256,256]{2,1,0:T(8,128)(2,1)S(1)} collective-permute-done((bf16[4,256,256]{2,1,0:T(8,128)(2,1)S(1)}, bf16[4,256,256]{2,1,0:T(8,128)(2,1)S(1)}, u32[]{:S(2)}, u32[]{:S(2)}) %collective-permute-start.11) | collective-permute-done | bytes 524320 | tf_op jit(solution)/shard_map/ppermute | solution.py:34
  55.4 0.7 collective-permute-done.10.refs_2_
  56.3 1.7 %collective-permute-start.12 = (bf16[512,256]{1,0:T(8,128)(2,1)S(1)}, bf16[512,256]{1,0:T(8,128)(2,1)S(1)}, u32[]{:S(2)}, u32[]{:S(2)}) collective-permute-start(bf16[512,256]{1,0:T(8,128)(2,1)S(1)} %get-tuple-element.61), channel_id=1, source_target_pairs={{0,8},{4,12},{8,0},{12,4},{16,24},{20,28},{24,16},{28,20},{1,9},{5... | collective-permute-start | bytes 786440 | tf_op jit(solution)/shard_map/ppermute | solution.py:34
  58.0 0.7 collective-permute-start.13
  58.7 1.1 collective-permute-start.14
  59.8 5.7 %collective-permute-done.12.refs_0_ = bf16[512,256]{1,0:T(8,128)(2,1)S(1)} collective-permute-done((bf16[512,256]{1,0:T(8,128)(2,1)S(1)}, bf16[512,256]{1,0:T(8,128)(2,1)S(1)}, u32[]{:S(2)}, u32[]{:S(2)}) %collective-permute-start.12) | collective-permute-done | bytes 262176 | tf_op jit(solution)/shard_map/ppermute | solution.py:34
  65.5 6.2 %collective-permute-done.13.refs_1_ = bf16[512,256]{1,0:T(8,128)(2,1)S(1)} collective-permute-done((bf16[512,256]{1,0:T(8,128)(2,1)S(1)}, bf16[512,256]{1,0:T(8,128)(2,1)S(1)}, u32[]{:S(2)}, u32[]{:S(2)}) %collective-permute-start.13) | collective-permute-done | bytes 262176 | tf_op jit(solution)/shard_map/ppermute | solution.py:34
  71.7 0.7 owner_sum.1
  72.4 1.6 %collective-permute-start.23 = (bf16[256,512]{1,0:T(8,128)(2,1)S(1)}, bf16[256,512]{1,0:T(8,128)(2,1)S(1)}, u32[]{:S(2)}, u32[]{:S(2)}) collective-permute-start(bf16[256,512]{1,0:T(8,128)(2,1)S(1)} %get-tuple-element.86.refs_4_), channel_id=1, source_target_pairs={{0,24},{4,28},{8,16},{12,20},{16,8},{20,12},{24,0},{28,4},{1,25},{... | collective-permute-start | bytes 786440 | tf_op jit(solution)/shard_map/ppermute | solution.py:34
  74.0 0.4 collective-permute-start.22
  74.4 1.7 %collective-permute-start.15 = (bf16[64,512]{1,0:T(8,128)(2,1)S(1)}, bf16[64,512]{1,0:T(8,128)(2,1)S(1)}, u32[]{:S(2)}, u32[]{:S(2)}) collective-permute-start(bf16[64,512]{1,0:T(8,128)(2,1)S(1)} %get-tuple-element.65), channel_id=1, source_target_pairs={{0,1},{1,0},{2,3},{3,2},{4,5},{5,4},{6,7},{7,6},{8,9},{9,8},{10,11... | collective-permute-start | bytes 196616 | tf_op jit(solution)/shard_map/ppermute | solution.py:34
  76.1 2.6 %collective-permute-start.16 = (bf16[64,512]{1,0:T(8,128)(2,1)S(1)}, bf16[64,512]{1,0:T(8,128)(2,1)S(1)}, u32[]{:S(2)}, u32[]{:S(2)}) collective-permute-start(bf16[64,512]{1,0:T(8,128)(2,1)S(1)} %get-tuple-element.66), channel_id=1, source_target_pairs={{0,2},{1,3},{2,0},{3,1},{4,6},{5,7},{6,4},{7,5},{8,10},{9,11},{10,... | collective-permute-start | bytes 196616 | tf_op jit(solution)/shard_map/ppermute | solution.py:34
  78.7 0.6 collective-permute-done.15
  79.3 3.1 %collective-permute-start.17 = (bf16[64,512]{1,0:T(8,128)(2,1)S(1)}, bf16[64,512]{1,0:T(8,128)(2,1)S(1)}, u32[]{:S(2)}, u32[]{:S(2)}) collective-permute-start(bf16[64,512]{1,0:T(8,128)(2,1)S(1)} %get-tuple-element.67), channel_id=1, source_target_pairs={{0,3},{1,2},{2,1},{3,0},{4,7},{5,6},{6,5},{7,4},{8,11},{9,10},{10,... | collective-permute-start | bytes 196616 | tf_op jit(solution)/shard_map/ppermute | solution.py:34
  82.4 0.4 collective-permute-done.16
  82.8 1.6 %collective-permute-start.21 = (bf16[256,512]{1,0:T(8,128)(2,1)S(1)}, bf16[256,512]{1,0:T(8,128)(2,1)S(1)}, u32[]{:S(2)}, u32[]{:S(2)}) collective-permute-start(bf16[256,512]{1,0:T(8,128)(2,1)S(1)} %get-tuple-element.86.refs_4_), channel_id=1, source_target_pairs={{0,8},{4,12},{8,0},{12,4},{16,24},{20,28},{24,16},{28,20},{1,9},{5... | collective-permute-start | bytes 786440 | tf_op jit(solution)/shard_map/ppermute | solution.py:34
  84.4 1.0 collective-permute-done.17
  85.4 1.5 %collective-permute-start.20 = (bf16[4,64,512]{2,1,0:T(8,128)(2,1)S(1)}, bf16[4,64,512]{2,1,0:T(8,128)(2,1)S(1)}, u32[]{:S(2)}, u32[]{:S(2)}) collective-permute-start(bf16[4,64,512]{2,1,0:T(8,128)(2,1)S(1)} %pad_maximum_fusion.1.refs_0_), channel_id=1, source_target_pairs={{0,24},{4,28},{8,16},{12,20},{16,8},{20,12},{24,0},{28,4},{1,25},{... | collective-permute-start | bytes 786440 | tf_op jit(solution)/shard_map/ppermute | solution.py:34
  86.9 1.5 %collective-permute-start.19 = (bf16[4,64,512]{2,1,0:T(8,128)(2,1)S(1)}, bf16[4,64,512]{2,1,0:T(8,128)(2,1)S(1)}, u32[]{:S(2)}, u32[]{:S(2)}) collective-permute-start(bf16[4,64,512]{2,1,0:T(8,128)(2,1)S(1)} %pad_maximum_fusion.1.refs_0_), channel_id=1, source_target_pairs={{0,16},{4,20},{8,24},{12,28},{16,0},{20,4},{24,8},{28,12},{1,17},{... | collective-permute-start | bytes 786440 | tf_op jit(solution)/shard_map/ppermute | solution.py:34
  88.4 0.5 collective-permute-start.18
  88.9 2.9 %collective-permute-done.21.refs_5_ = bf16[256,512]{1,0:T(8,128)(2,1)S(1)} collective-permute-done((bf16[256,512]{1,0:T(8,128)(2,1)S(1)}, bf16[256,512]{1,0:T(8,128)(2,1)S(1)}, u32[]{:S(2)}, u32[]{:S(2)}) %collective-permute-start.21) | collective-permute-done | bytes 262176 | tf_op jit(solution)/shard_map/ppermute | solution.py:34
  91.9 5.3 %collective-permute-done.20.refs_3_ = bf16[4,64,512]{2,1,0:T(8,128)(2,1)S(1)} collective-permute-done((bf16[4,64,512]{2,1,0:T(8,128)(2,1)S(1)}, bf16[4,64,512]{2,1,0:T(8,128)(2,1)S(1)}, u32[]{:S(2)}, u32[]{:S(2)}) %collective-permute-start.20) | collective-permute-done | bytes 262176 | tf_op jit(solution)/shard_map/ppermute | solution.py:34
  97.2 0.4 collective-permute-done.19.refs_2_
  97.6 2.3 %collective-permute-done.18.refs_1_ = bf16[4,64,512]{2,1,0:T(8,128)(2,1)S(1)} collective-permute-done((bf16[4,64,512]{2,1,0:T(8,128)(2,1)S(1)}, bf16[4,64,512]{2,1,0:T(8,128)(2,1)S(1)}, u32[]{:S(2)}, u32[]{:S(2)}) %collective-permute-start.18) | collective-permute-done | bytes 262176 | tf_op jit(solution)/shard_map/ppermute | solution.py:34
  99.8 3.8 %input_grad.1 = (bf16[64,1280]{1,0:T(8,128)(2,1)S(1)}, bf16[64,1280]{1,0:T(8,128)(2,1)S(1)}, bf16[64,1280]{1,0:T(8,128)(2,1)S(1)}, bf16[64,1280]{1,0:T(8,128)(2,1)S(1)}) custom-call(s32[2]{0:T(128)S(1)} %pad_add_fusion.place, bf16[4,64,512]{2,1,0:T(8,128)(2,1)S(1)} %pad_maximum_fusion.1.refs_0_, bf16[4,64,512]{2,1,0:T(8,128)(2,1)S(1)} %collective-permute-done.18.refs_1_, ...), custom_call_target="tpu_custom_call" | custom-call | tf_op jit(solution)/shard_map/input_grad/pallas_call | solution.py:340
  103.6 2.1 %weight_grad.1 = (f32[640,512]{1,0:T(8,128)S(1)}, f32[640,512]{1,0:T(8,128)S(1)}) custom-call(s32[2]{0:T(128)S(1)} %pad_add_fusion.place, bf16[256,1280]{1,0:T(8,128)(2,1)S(1)} %get-tuple-element.82.refs_0_, bf16[256,1280]{1,0:T(8,128)(2,1)S(1)} %collective-permute-done.7.refs_1_, bf16[256,1280]{1,0:T(8,128)(2,1)S(1)} %collective-permute-done.8.refs_2_, ...), custom_call_target="tpu_custom_call" | custom-call | tf_op jit(solution)/shard_map/weight_grad/pallas_call | solution.py:286
  105.8 1.0 collective-permute-start.25
  106.8 1.0 collective-permute-start.26
  107.8 1.5 %collective-permute-start.27 = (bf16[64,1280]{1,0:T(8,128)(2,1)S(1)}, bf16[64,1280]{1,0:T(8,128)(2,1)S(1)}, u32[]{:S(2)}, u32[]{:S(2)}) collective-permute-start(bf16[64,1280]{1,0:T(8,128)(2,1)S(1)} %get-tuple-element.81), channel_id=1, source_target_pairs={{0,24},{4,28},{8,16},{12,20},{16,8},{20,12},{24,0},{28,4},{1,25},{... | collective-permute-start | bytes 491528 | tf_op jit(solution)/shard_map/ppermute | solution.py:34
  109.4 1.8 %weight_sum.1 = f32[640,2,256]{2,1,0:T(2,128)} custom-call(f32[640,512]{1,0:T(8,128)S(1)} %get-tuple-element.90.keep_ref, f32[640,512]{1,0:T(8,128)S(1)} %collective-permute-done.28.got_ref), custom_call_target="tpu_custom_call" | custom-call | tf_op jit(solution)/shard_map/weight_sum/pallas_call | solution.py:305
  111.2 1.7 %collective-permute-done.25.refs_1_ = bf16[64,1280]{1,0:T(8,128)(2,1)S(1)} collective-permute-done((bf16[64,1280]{1,0:T(8,128)(2,1)S(1)}, bf16[64,1280]{1,0:T(8,128)(2,1)S(1)}, u32[]{:S(2)}, u32[]{:S(2)}) %collective-permute-start.25) | collective-permute-done | bytes 163872 | tf_op jit(solution)/shard_map/ppermute | solution.py:34
  112.9 3.7 %collective-permute-done.26.refs_2_ = bf16[64,1280]{1,0:T(8,128)(2,1)S(1)} collective-permute-done((bf16[64,1280]{1,0:T(8,128)(2,1)S(1)}, bf16[64,1280]{1,0:T(8,128)(2,1)S(1)}, u32[]{:S(2)}, u32[]{:S(2)}) %collective-permute-start.26) | collective-permute-done | bytes 163872 | tf_op jit(solution)/shard_map/ppermute | solution.py:34
  116.6 1.4 %lay_rows.1 = bf16[64,5120]{1,0:T(8,128)(2,1)} custom-call(s32[2]{0:T(128)S(1)} %pad_add_fusion.place, bf16[64,1280]{1,0:T(8,128)(2,1)S(1)} %get-tuple-element.92.refs_0_, bf16[64,1280]{1,0:T(8,128)(2,1)S(1)} %collective-permute-done.25.refs_1_, bf16[64,1280]{1,0:T(8,128)(2,1)S(1)} %collective-permute-done.26.refs_2_, ...), custom_call_target="tpu_custom_call" | custom-call | tf_op jit(solution)/shard_map/lay_rows/pallas_call | solution.py:367
  (30 shorter events, 0.9 us)
Async XLA Ops:
  2.3 11.1 %collective-permute-start.5 = (bf16[256,512]{1,0:T(8,128)(2,1)S(1)}, bf16[256,512]{1,0:T(8,128)(2,1)S(1)}, u32[]{:S(2)}, u32[]{:S(2)}) collective-permute-start(bf16[256,512]{1,0:T(8,128)(2,1)S(1)} %pad_maximum_fusion.refs_0_), channel_id=1, source_target_pairs={{0,24},{4,28},{8,16},{12,20},{16,8},{20,12},{24,0},{28,4},{1,25},{... | collective-permute-start | bytes 786440 | tf_op jit(solution)/shard_map/ppermute | solution.py:34
  6.2 11.9 %collective-permute-start.3 = (bf16[256,512]{1,0:T(8,128)(2,1)S(1)}, bf16[256,512]{1,0:T(8,128)(2,1)S(1)}, u32[]{:S(2)}, u32[]{:S(2)}) collective-permute-start(bf16[256,512]{1,0:T(8,128)(2,1)S(1)} %pad_maximum_fusion.refs_0_), channel_id=1, source_target_pairs={{0,16},{4,20},{8,24},{12,28},{16,0},{20,4},{24,8},{28,12},{1,17},{... | collective-permute-start | bytes 786440 | tf_op jit(solution)/shard_map/ppermute | solution.py:34
  6.7 11.8 %collective-permute-start.1 = (bf16[256,512]{1,0:T(8,128)(2,1)S(1)}, bf16[256,512]{1,0:T(8,128)(2,1)}, u32[]{:S(2)}, u32[]{:S(2)}) collective-permute-start(bf16[256,512]{1,0:T(8,128)(2,1)S(1)} %pad_maximum_fusion.refs_0_), channel_id=1, source_target_pairs={{0,8},{4,12},{8,0},{12,4},{16,24},{20,28},{24,16},{28,20},{1,9},{5... | collective-permute-start | bytes 786440 | tf_op jit(solution)/shard_map/ppermute | solution.py:34
  6.9 13.7 %collective-permute-start = (bf16[256,512]{1,0:T(8,128)(2,1)S(1)}, bf16[256,512]{1,0:T(8,128)(2,1)}, u32[]{:S(2)}, u32[]{:S(2)}) collective-permute-start(bf16[256,512]{1,0:T(8,128)(2,1)S(1)} %pad_maximum_fusion.refs_0_), channel_id=1, source_target_pairs={{0,4},{4,0},{8,12},{12,8},{16,20},{20,16},{24,28},{28,24},{1,5},{5... | collective-permute-start | bytes 786440 | tf_op jit(solution)/shard_map/ppermute | solution.py:34
  9.5 90.4 %collective-permute-start.24 = (bf16[640,2048]{1,0:T(8,128)(2,1)S(1)}, bf16[640,2048]{1,0:T(8,128)(2,1)}, u32[]{:S(2)}, u32[]{:S(2)}) collective-permute-start(bf16[640,2048]{1,0:T(8,128)(2,1)S(1)} %bitcast.19), channel_id=1, source_target_pairs={{0,4},{4,0},{8,12},{12,8},{16,20},{20,16},{24,28},{28,24},{1,5},{5... | collective-permute-start | bytes 7864328 | tf_op jit(solution)/shard_map/ppermute | solution.py:34
  10.1 14.0 %copy-start = (bf16[1,384,1280]{2,1,0:T(8,128)(2,1)S(1)}, bf16[1,384,1280]{2,1,0:T(8,128)(2,1)}, u32[]{:S(2)}) copy-start(bf16[1,384,1280]{2,1,0:T(8,128)(2,1)} %param.5) | copy-start | bytes 2949124
  10.1 14.0 %copy-start.1 = (bf16[1,384,1280]{2,1,0:T(8,128)(2,1)S(1)}, bf16[1,384,1280]{2,1,0:T(8,128)(2,1)}, u32[]{:S(2)}) copy-start(bf16[1,384,1280]{2,1,0:T(8,128)(2,1)} %param.7) | copy-start | bytes 2949124
  13.4 8.9 %collective-permute-start.6 = (bf16[256,512]{1,0:T(8,128)(2,1)S(1)}, bf16[256,512]{1,0:T(8,128)(2,1)S(1)}, u32[]{:S(2)}, u32[]{:S(2)}) collective-permute-start(bf16[256,512]{1,0:T(8,128)(2,1)S(1)} %collective-permute-done.5.refs_6_), channel_id=1, source_target_pairs={{0,4},{4,0},{8,12},{12,8},{16,20},{20,16},{24,28},{28,24},{1,5},{5... | collective-permute-start | bytes 786440 | tf_op jit(solution)/shard_map/ppermute | solution.py:34
  18.2 4.8 %collective-permute-start.4 = (bf16[256,512]{1,0:T(8,128)(2,1)S(1)}, bf16[256,512]{1,0:T(8,128)(2,1)S(1)}, u32[]{:S(2)}, u32[]{:S(2)}) collective-permute-start(bf16[256,512]{1,0:T(8,128)(2,1)S(1)} %collective-permute-done.3.refs_4_), channel_id=1, source_target_pairs={{0,4},{4,0},{8,12},{12,8},{16,20},{20,16},{24,28},{28,24},{1,5},{5... | collective-permute-start | bytes 786440 | tf_op jit(solution)/shard_map/ppermute | solution.py:34
  18.6 5.6 %collective-permute-start.2 = (bf16[256,512]{1,0:T(8,128)(2,1)}, bf16[256,512]{1,0:T(8,128)(2,1)S(1)}, u32[]{:S(2)}, u32[]{:S(2)}) collective-permute-start(bf16[256,512]{1,0:T(8,128)(2,1)} %collective-permute-done.1.refs_2_), channel_id=1, source_target_pairs={{0,4},{4,0},{8,12},{12,8},{16,20},{20,16},{24,28},{28,24},{1,5},{5... | collective-permute-start | bytes 786440 | tf_op jit(solution)/shard_map/ppermute | solution.py:34
  20.5 32.9 %collective-permute-start.7 = (bf16[256,1280]{1,0:T(8,128)(2,1)S(1)}, bf16[256,1280]{1,0:T(8,128)(2,1)S(1)}, u32[]{:S(2)}, u32[]{:S(2)}) collective-permute-start(bf16[256,1280]{1,0:T(8,128)(2,1)S(1)} %get-tuple-element.54), channel_id=1, source_target_pairs={{0,8},{4,12},{8,0},{12,4},{16,24},{20,28},{24,16},{28,20},{1,9},{5... | collective-permute-start | bytes 1966088 | tf_op jit(solution)/shard_map/ppermute | solution.py:34
  22.3 31.7 %collective-permute-start.8 = (bf16[256,1280]{1,0:T(8,128)(2,1)S(1)}, bf16[256,1280]{1,0:T(8,128)(2,1)S(1)}, u32[]{:S(2)}, u32[]{:S(2)}) collective-permute-start(bf16[256,1280]{1,0:T(8,128)(2,1)S(1)} %get-tuple-element.55), channel_id=1, source_target_pairs={{0,16},{4,20},{8,24},{12,28},{16,0},{20,4},{24,8},{28,12},{1,17},{... | collective-permute-start | bytes 1966088 | tf_op jit(solution)/shard_map/ppermute | solution.py:34
  23.0 31.0 %collective-permute-start.9 = (bf16[256,1280]{1,0:T(8,128)(2,1)S(1)}, bf16[256,1280]{1,0:T(8,128)(2,1)S(1)}, u32[]{:S(2)}, u32[]{:S(2)}) collective-permute-start(bf16[256,1280]{1,0:T(8,128)(2,1)S(1)} %get-tuple-element.56), channel_id=1, source_target_pairs={{0,24},{4,28},{8,16},{12,20},{16,8},{20,12},{24,0},{28,4},{1,25},{... | collective-permute-start | bytes 1966088 | tf_op jit(solution)/shard_map/ppermute | solution.py:34
  53.4 1.9 %collective-permute-start.11 = (bf16[4,256,256]{2,1,0:T(8,128)(2,1)S(1)}, bf16[4,256,256]{2,1,0:T(8,128)(2,1)S(1)}, u32[]{:S(2)}, u32[]{:S(2)}) collective-permute-start(bf16[4,256,256]{2,1,0:T(8,128)(2,1)S(1)} %get-tuple-element.59), channel_id=1, source_target_pairs={{0,4},{4,0},{8,12},{12,8},{16,20},{20,16},{24,28},{28,24},{1,5},{5... | collective-permute-start | bytes 1572872 | tf_op jit(solution)/shard_map/ppermute | solution.py:34
  53.5 2.7 %collective-permute-start.10 = (bf16[4,256,256]{2,1,0:T(8,128)(2,1)S(1)}, bf16[4,256,256]{2,1,0:T(8,128)(2,1)S(1)}, u32[]{:S(2)}, u32[]{:S(2)}) collective-permute-start(bf16[4,256,256]{2,1,0:T(8,128)(2,1)S(1)} %get-tuple-element.58), channel_id=1, source_target_pairs={{0,4},{4,0},{8,12},{12,8},{16,20},{20,16},{24,28},{28,24},{1,5},{5... | collective-permute-start | bytes 1572872 | tf_op jit(solution)/shard_map/ppermute | solution.py:34
  56.3 9.2 %collective-permute-start.12 = (bf16[512,256]{1,0:T(8,128)(2,1)S(1)}, bf16[512,256]{1,0:T(8,128)(2,1)S(1)}, u32[]{:S(2)}, u32[]{:S(2)}) collective-permute-start(bf16[512,256]{1,0:T(8,128)(2,1)S(1)} %get-tuple-element.61), channel_id=1, source_target_pairs={{0,8},{4,12},{8,0},{12,4},{16,24},{20,28},{24,16},{28,20},{1,9},{5... | collective-permute-start | bytes 786440 | tf_op jit(solution)/shard_map/ppermute | solution.py:34
  58.0 13.7 %collective-permute-start.13 = (bf16[512,256]{1,0:T(8,128)(2,1)S(1)}, bf16[512,256]{1,0:T(8,128)(2,1)S(1)}, u32[]{:S(2)}, u32[]{:S(2)}) collective-permute-start(bf16[512,256]{1,0:T(8,128)(2,1)S(1)} %get-tuple-element.62), channel_id=1, source_target_pairs={{0,16},{4,20},{8,24},{12,28},{16,0},{20,4},{24,8},{28,12},{1,17},{... | collective-permute-start | bytes 786440 | tf_op jit(solution)/shard_map/ppermute | solution.py:34
  58.7 13.0 %collective-permute-start.14 = (bf16[512,256]{1,0:T(8,128)(2,1)S(1)}, bf16[512,256]{1,0:T(8,128)(2,1)S(1)}, u32[]{:S(2)}, u32[]{:S(2)}) collective-permute-start(bf16[512,256]{1,0:T(8,128)(2,1)S(1)} %get-tuple-element.63), channel_id=1, source_target_pairs={{0,24},{4,28},{8,16},{12,20},{16,8},{20,12},{24,0},{28,4},{1,25},{... | collective-permute-start | bytes 786440 | tf_op jit(solution)/shard_map/ppermute | solution.py:34
  72.4 14.4 %collective-permute-start.23 = (bf16[256,512]{1,0:T(8,128)(2,1)S(1)}, bf16[256,512]{1,0:T(8,128)(2,1)S(1)}, u32[]{:S(2)}, u32[]{:S(2)}) collective-permute-start(bf16[256,512]{1,0:T(8,128)(2,1)S(1)} %get-tuple-element.86.refs_4_), channel_id=1, source_target_pairs={{0,24},{4,28},{8,16},{12,20},{16,8},{20,12},{24,0},{28,4},{1,25},{... | collective-permute-start | bytes 786440 | tf_op jit(solution)/shard_map/ppermute | solution.py:34
  74.0 14.4 %collective-permute-start.22 = (bf16[256,512]{1,0:T(8,128)(2,1)S(1)}, bf16[256,512]{1,0:T(8,128)(2,1)S(1)}, u32[]{:S(2)}, u32[]{:S(2)}) collective-permute-start(bf16[256,512]{1,0:T(8,128)(2,1)S(1)} %get-tuple-element.86.refs_4_), channel_id=1, source_target_pairs={{0,16},{4,20},{8,24},{12,28},{16,0},{20,4},{24,8},{28,12},{1,17},{... | collective-permute-start | bytes 786440 | tf_op jit(solution)/shard_map/ppermute | solution.py:34
  74.4 4.9 %collective-permute-start.15 = (bf16[64,512]{1,0:T(8,128)(2,1)S(1)}, bf16[64,512]{1,0:T(8,128)(2,1)S(1)}, u32[]{:S(2)}, u32[]{:S(2)}) collective-permute-start(bf16[64,512]{1,0:T(8,128)(2,1)S(1)} %get-tuple-element.65), channel_id=1, source_target_pairs={{0,1},{1,0},{2,3},{3,2},{4,5},{5,4},{6,7},{7,6},{8,9},{9,8},{10,11... | collective-permute-start | bytes 196616 | tf_op jit(solution)/shard_map/ppermute | solution.py:34
  76.1 6.7 %collective-permute-start.16 = (bf16[64,512]{1,0:T(8,128)(2,1)S(1)}, bf16[64,512]{1,0:T(8,128)(2,1)S(1)}, u32[]{:S(2)}, u32[]{:S(2)}) collective-permute-start(bf16[64,512]{1,0:T(8,128)(2,1)S(1)} %get-tuple-element.66), channel_id=1, source_target_pairs={{0,2},{1,3},{2,0},{3,1},{4,6},{5,7},{6,4},{7,5},{8,10},{9,11},{10,... | collective-permute-start | bytes 196616 | tf_op jit(solution)/shard_map/ppermute | solution.py:34
  79.3 6.1 %collective-permute-start.17 = (bf16[64,512]{1,0:T(8,128)(2,1)S(1)}, bf16[64,512]{1,0:T(8,128)(2,1)S(1)}, u32[]{:S(2)}, u32[]{:S(2)}) collective-permute-start(bf16[64,512]{1,0:T(8,128)(2,1)S(1)} %get-tuple-element.67), channel_id=1, source_target_pairs={{0,3},{1,2},{2,1},{3,0},{4,7},{5,6},{6,5},{7,4},{8,11},{9,10},{10,... | collective-permute-start | bytes 196616 | tf_op jit(solution)/shard_map/ppermute | solution.py:34
  82.8 9.1 %collective-permute-start.21 = (bf16[256,512]{1,0:T(8,128)(2,1)S(1)}, bf16[256,512]{1,0:T(8,128)(2,1)S(1)}, u32[]{:S(2)}, u32[]{:S(2)}) collective-permute-start(bf16[256,512]{1,0:T(8,128)(2,1)S(1)} %get-tuple-element.86.refs_4_), channel_id=1, source_target_pairs={{0,8},{4,12},{8,0},{12,4},{16,24},{20,28},{24,16},{28,20},{1,9},{5... | collective-permute-start | bytes 786440 | tf_op jit(solution)/shard_map/ppermute | solution.py:34
  85.4 11.8 %collective-permute-start.20 = (bf16[4,64,512]{2,1,0:T(8,128)(2,1)S(1)}, bf16[4,64,512]{2,1,0:T(8,128)(2,1)S(1)}, u32[]{:S(2)}, u32[]{:S(2)}) collective-permute-start(bf16[4,64,512]{2,1,0:T(8,128)(2,1)S(1)} %pad_maximum_fusion.1.refs_0_), channel_id=1, source_target_pairs={{0,24},{4,28},{8,16},{12,20},{16,8},{20,12},{24,0},{28,4},{1,25},{... | collective-permute-start | bytes 786440 | tf_op jit(solution)/shard_map/ppermute | solution.py:34
  86.9 10.7 %collective-permute-start.19 = (bf16[4,64,512]{2,1,0:T(8,128)(2,1)S(1)}, bf16[4,64,512]{2,1,0:T(8,128)(2,1)S(1)}, u32[]{:S(2)}, u32[]{:S(2)}) collective-permute-start(bf16[4,64,512]{2,1,0:T(8,128)(2,1)S(1)} %pad_maximum_fusion.1.refs_0_), channel_id=1, source_target_pairs={{0,16},{4,20},{8,24},{12,28},{16,0},{20,4},{24,8},{28,12},{1,17},{... | collective-permute-start | bytes 786440 | tf_op jit(solution)/shard_map/ppermute | solution.py:34
  88.4 11.4 %collective-permute-start.18 = (bf16[4,64,512]{2,1,0:T(8,128)(2,1)S(1)}, bf16[4,64,512]{2,1,0:T(8,128)(2,1)S(1)}, u32[]{:S(2)}, u32[]{:S(2)}) collective-permute-start(bf16[4,64,512]{2,1,0:T(8,128)(2,1)S(1)} %pad_maximum_fusion.1.refs_0_), channel_id=1, source_target_pairs={{0,8},{4,12},{8,0},{12,4},{16,24},{20,28},{24,16},{28,20},{1,9},{5... | collective-permute-start | bytes 786440 | tf_op jit(solution)/shard_map/ppermute | solution.py:34
  105.7 3.6 %collective-permute-start.28 = (f32[640,512]{1,0:T(8,128)S(1)}, f32[640,512]{1,0:T(8,128)S(1)}, u32[]{:S(2)}, u32[]{:S(2)}) collective-permute-start(f32[640,512]{1,0:T(8,128)S(1)} %get-tuple-element.91), channel_id=1, source_target_pairs={{0,4},{4,0},{8,12},{12,8},{16,20},{20,16},{24,28},{28,24},{1,5},{5... | collective-permute-start | bytes 3932168 | tf_op jit(solution)/shard_map/ppermute | solution.py:34
  105.8 7.1 %collective-permute-start.25 = (bf16[64,1280]{1,0:T(8,128)(2,1)S(1)}, bf16[64,1280]{1,0:T(8,128)(2,1)S(1)}, u32[]{:S(2)}, u32[]{:S(2)}) collective-permute-start(bf16[64,1280]{1,0:T(8,128)(2,1)S(1)} %get-tuple-element.79), channel_id=1, source_target_pairs={{0,8},{4,12},{8,0},{12,4},{16,24},{20,28},{24,16},{28,20},{1,9},{5... | collective-permute-start | bytes 491528 | tf_op jit(solution)/shard_map/ppermute | solution.py:34
  106.8 9.8 %collective-permute-start.26 = (bf16[64,1280]{1,0:T(8,128)(2,1)S(1)}, bf16[64,1280]{1,0:T(8,128)(2,1)S(1)}, u32[]{:S(2)}, u32[]{:S(2)}) collective-permute-start(bf16[64,1280]{1,0:T(8,128)(2,1)S(1)} %get-tuple-element.80), channel_id=1, source_target_pairs={{0,16},{4,20},{8,24},{12,28},{16,0},{20,4},{24,8},{28,12},{1,17},{... | collective-permute-start | bytes 491528 | tf_op jit(solution)/shard_map/ppermute | solution.py:34
  107.8 8.8 %collective-permute-start.27 = (bf16[64,1280]{1,0:T(8,128)(2,1)S(1)}, bf16[64,1280]{1,0:T(8,128)(2,1)S(1)}, u32[]{:S(2)}, u32[]{:S(2)}) collective-permute-start(bf16[64,1280]{1,0:T(8,128)(2,1)S(1)} %get-tuple-element.81), channel_id=1, source_target_pairs={{0,24},{4,28},{8,16},{12,20},{16,8},{20,12},{24,0},{28,4},{1,25},{... | collective-permute-start | bytes 491528 | tf_op jit(solution)/shard_map/ppermute | solution.py:34

commit v4 on v3

--- a/solution.py
+++ b/solution.py
@@ -217,53 +217,50 @@
     )(place, *operands)
 
 
-def pair_sum_kernel(heads, *refs):
-    keeps, gots, own_ref, send_refs = refs[:heads], refs[heads : 2 * heads], refs[2 * heads], refs[2 * heads + 1 :]
+def pair_sum_kernel(keep_ref, got_ref, own_ref, *send_refs):
+    own_ref[...] = keep_ref[0] + got_ref[0].astype(F32)
+    for k, send_ref in enumerate(send_refs, 1):
+        send_ref[...] = (keep_ref[k] + got_ref[k].astype(F32)).astype(BF16)
+
+
+def pair_sum(keep, got):
+    half, width, blk = keep.shape
+    out_shape = [jax.ShapeDtypeStruct((width, blk), F32)]
+    out_shape += [jax.ShapeDtypeStruct((width, blk), BF16)] * (half - 1)
+    return pl.pallas_call(
+        pair_sum_kernel, out_shape=out_shape, compiler_params=params(), name="pair_sum"
+    )(keep, got)
+
+
+def owner_sum_kernel(heads, lanes, place, *refs):
+    part_refs, sum_ref, lane_refs = refs[: -1 - lanes], refs[-1 - lanes], refs[-lanes:]
+    each = len(part_refs) // heads
     for a in range(heads):
-        span = pl.ds(a * 2 * HD, 2 * HD)
-        own_ref[span, :] = keeps[a][0] + gots[a][0].astype(F32)
-        for k, send_ref in enumerate(send_refs, 1):
-            send_ref[span, :] = (keeps[a][k] + gots[a][k].astype(F32)).astype(BF16)
-
-
-def pair_sum(keeps, gots):
-    half, width, blk = keeps[0].shape
-    heads = len(keeps)
-    out_shape = [jax.ShapeDtypeStruct((heads * width, blk), F32)]
-    out_shape += [jax.ShapeDtypeStruct((heads * width, blk), BF16)] * (half - 1)
-    return pl.pallas_call(
-        functools.partial(pair_sum_kernel, heads),
-        out_shape=out_shape,
-        compiler_params=params(),
-        name="pair_sum",
-    )(*keeps, *gots)
-
-
-def owner_sum_kernel(lanes, place, own_ref, *refs):
-    got_refs = refs[: -1 - lanes]
-    sum_ref, lane_refs = refs[-1 - lanes], refs[-lanes:]
-    total = own_ref[...]
-    for got_ref in got_refs:
-        total = total + got_ref[...].astype(F32)
-    sum_ref[...] = total.astype(BF16).T
+        own_ref, *got_refs = part_refs[a * each : (a + 1) * each]
+        total = own_ref[...]
+        for got_ref in got_refs:
+            total = total + got_ref[...].astype(F32)
+        sum_ref[:, a * 2 * HD : (a + 1) * 2 * HD] = total.astype(BF16).T
     rows = lane_refs[0].shape[0]
     for b, lane_ref in enumerate(lane_refs):
         start = pl.multiple_of(lax.bitwise_xor(place[1], b) * rows, rows)
         lane_ref[...] = sum_ref[pl.ds(start, rows), :]
 
 
-def owner_sum(place, own, got, lanes):
-    width, blk = own.shape
-    out_shape = [jax.ShapeDtypeStruct((blk, width), BF16)]
-    out_shape += [jax.ShapeDtypeStruct((blk // lanes, width), BF16)] * lanes
-    return pl.pallas_call(
-        functools.partial(owner_sum_kernel, lanes),
+def owner_sum(place, parts, lanes):
+    heads = len(parts)
+    width, blk = parts[0][0].shape
+    parts = [x for head in parts for x in head]
+    out_shape = [jax.ShapeDtypeStruct((blk, heads * width), BF16)]
+    out_shape += [jax.ShapeDtypeStruct((blk // lanes, heads * width), BF16)] * lanes
+    return pl.pallas_call(
+        functools.partial(owner_sum_kernel, heads, lanes),
         in_specs=[pl.BlockSpec(memory_space=pltpu.SMEM)]
-        + [pl.BlockSpec(memory_space=pltpu.VMEM)] * (1 + len(got)),
+        + [pl.BlockSpec(memory_space=pltpu.VMEM)] * len(parts),
         out_shape=out_shape,
         compiler_params=params(),
         name="owner_sum",
-    )(place, own, *got)
+    )(place, *parts)
 
 
 def weight_grad_kernel(half, place, *refs):
@@ -413,9 +410,8 @@
         keeps.append(keep)
         gots.append(exchange(send, 1, "sec"))
 
-    own, *sends = pair_sum(keeps, gots)
-    _, *got = across([own, *sends])
-    mine, *by_lane = owner_sum(place, own, got, lanes)
+    parts = [across(pair_sum(keep, got)) for keep, got in zip(keeps, gots)]
+    mine, *by_lane = owner_sum(place, parts, lanes)
     by_lane[1:] = [exchange(by_lane[b], b, "lane") for b in range(1, lanes)]
     gathered = across([mine] * half)
     blocks = across([jnp.stack(by_lane)] * half)

time: 118 us -> 115 us (0.975)
  waiting for transfers between devices: 40.7 us -> 32.6 us
  starting transfers between devices: 31.1 us -> 36.2 us
    ppermute x29 -> x32, waiting for transfers between devices: 40.7 us -> 32.6 us  [exchange(): lax.ppermute(x, axis, [(i, i ^ offset) for i in range(lax.axis_size(axis))])]
    ppermute x29 -> x32, starting transfers between devices: 31.1 us -> 36.2 us  [exchange(): lax.ppermute(x, axis, [(i, i ^ offset) for i in range(lax.axis_size(axis))])]
  transfers between devices with their start and end apart: 29 -> 32, of which waited for: 16 -> 17; matrix products, arithmetic and copies ran while one was open for 4% -> 4% of each run, Pallas kernels for 27% -> 28%
where the time goes in v4:
time: 115 us
  Pallas kernels  39.3 us (34%)
  starting transfers between devices  36.2 us (31%)
  waiting for transfers between devices  32.6 us (28%)
  local copies, waits for them, and re-layouts  6.01 us (5%)
    ppermute x32, starting transfers between devices, exchange(): lax.ppermute(x, axis, [(i, i ^ offset) for i in range(lax.axis_size(axis))])  36.2 us
    ppermute x32, waiting for transfers between devices, exchange(): lax.ppermute(x, axis, [(i, i ^ offset) for i in range(lax.axis_size(axis))])  32.6 us
    pallas_call x2, Pallas kernels, attend(): pl.pallas_call(functools.partial(attend_kernel, n, group, dq is not None)...  29.3 us
    pallas_call x1, Pallas kernels, input_grad(): pl.pallas_call(functools.partial(input_grad_kernel, here // (2 * HD), hal...  3.78 us
    unnamed x5, local copies, waits for them, and re-layouts  2.57 us
  transfers between devices with their start and end apart: 32, of which 17 were waited for; matrix products, arithmetic and copies ran while one was open for 4% of the time, Pallas kernels for 28%

profile of v4, /device:TPU:0, one launch (start us, length us, event | category | flops | bytes accessed | tf_op | source)
XLA Modules:
  0.0 115.2 jit_solution(3562487840157649555)
XLA Ops:
  0.6 1.5 %fusion = (bf16[256,1,128]{2,1,0:T(2,128)(2,1)S(1)}, bf16[256,1,128]{2,1,0:T(2,128)(2,1)S(1)}, bf16[256,1,128]{2,1,0:T(2,128)(2,1)S(1)}, bf16[256,1,128]{2,1,0:T(2,128)(2,1)S(1)}) fusion(bf16[256,2,256]{2,1,0:T(2,128)(2,1)} %param.6), kind=kLoop, calls=%fused_computation.11 | loop fusion | bytes 524288 | tf_op jit(solution)/shard_map/slice | solution.py:389
  2.3 4.0 %collective-permute-start.5 = (bf16[256,512]{1,0:T(8,128)(2,1)S(1)}, bf16[256,512]{1,0:T(8,128)(2,1)S(1)}, u32[]{:S(2)}, u32[]{:S(2)}) collective-permute-start(bf16[256,512]{1,0:T(8,128)(2,1)S(1)} %pad_maximum_fusion.refs_0_), channel_id=1, source_target_pairs={{0,24},{4,28},{8,16},{12,20},{16,8},{20,12},{24,0},{28,4},{1,25},{... | collective-permute-start | bytes 786440 | tf_op jit(solution)/shard_map/ppermute | solution.py:34
  6.9 2.6 %copy.17 = bf16[80,8,2,1024]{3,1,2,0:T(8,128)(2,1)S(1)} copy(bf16[80,8,2,1024]{3,2,1,0:T(2,128)(2,1)} %bitcast.26) | data formatting | bytes 5242880
  9.5 0.6 collective-permute-start.27
  10.1 3.3 %collective-permute-done.5.refs_6_ = bf16[256,512]{1,0:T(8,128)(2,1)S(1)} collective-permute-done((bf16[256,512]{1,0:T(8,128)(2,1)S(1)}, bf16[256,512]{1,0:T(8,128)(2,1)S(1)}, u32[]{:S(2)}, u32[]{:S(2)}) %collective-permute-start.5) | collective-permute-done | bytes 262176 | tf_op jit(solution)/shard_map/ppermute | solution.py:34
  13.4 4.7 %collective-permute-done.3.refs_4_ = bf16[256,512]{1,0:T(8,128)(2,1)S(1)} collective-permute-done((bf16[256,512]{1,0:T(8,128)(2,1)S(1)}, bf16[256,512]{1,0:T(8,128)(2,1)S(1)}, u32[]{:S(2)}, u32[]{:S(2)}) %collective-permute-start.3) | collective-permute-done | bytes 262176 | tf_op jit(solution)/shard_map/ppermute | solution.py:34
  18.7 1.9 %constant_dynamic-slice_fusion = (bf16[256,1280]{1,0:T(8,128)(2,1)S(1)}, bf16[256,1280]{1,0:T(8,128)(2,1)S(1)}, bf16[256,1280]{1,0:T(8,128)(2,1)S(1)}, bf16[256,1280]{1,0:T(8,128)(2,1)S(1)}) fusion(bf16[256,5120]{1,0:T(8,128)(2,1)} %param.8, s32[]{:T(128)S(6)} %select_n.24, s32[]{:T(128)S(6)} %select_n.22, s32[]{:T(128)S(6)} %select_n.21, s32[]{:T(128)S(6)} %select_n.23), kind=kLoop, calls=%fused_computation.6 | loop fusion | bytes 5242896 | tf_op jit(solution)/shard_map/dynamic_slice | solution.py:396
  20.5 1.7 %collective-permute-start.11 = (bf16[256,1280]{1,0:T(8,128)(2,1)S(1)}, bf16[256,1280]{1,0:T(8,128)(2,1)S(1)}, u32[]{:S(2)}, u32[]{:S(2)}) collective-permute-start(bf16[256,1280]{1,0:T(8,128)(2,1)S(1)} %get-tuple-element.63), channel_id=1, source_target_pairs={{0,8},{4,12},{8,0},{12,4},{16,24},{20,28},{24,16},{28,20},{1,9},{5... | collective-permute-start | bytes 1966088 | tf_op jit(solution)/shard_map/ppermute | solution.py:34
  22.3 0.7 collective-permute-start.12
  23.0 1.1 collective-permute-start.13
  24.2 14.7 %attend.2 = (bf16[384,1280]{1,0:T(8,128)(2,1)}, f32[4,256,256]{2,1,0:T(8,128)S(1)}, bf16[4,256,256]{2,1,0:T(8,128)(2,1)S(1)}) custom-call(s32[2]{0:T(128)S(1)} %pad_add_fusion.place, bf16[256,512]{1,0:T(8,128)(2,1)S(1)} %pad_maximum_fusion.refs_0_, bf16[256,512]{1,0:T(8,128)(2,1)} %collective-permute-done.refs_1_, ...), custom_call_target="tpu_custom_call" | custom-call | flops 10066329600 | bytes 4194304 | tf_op jit(solution)/shard_map/attend/pallas_call | solution.py:186
  38.8 14.7 %attend.3 = (bf16[384,1280]{1,0:T(8,128)(2,1)}, f32[4,256,256]{2,1,0:T(8,128)S(1)}, bf16[4,256,256]{2,1,0:T(8,128)(2,1)S(1)}) custom-call(s32[2]{0:T(128)S(1)} %pad_add_fusion.place, bf16[256,512]{1,0:T(8,128)(2,1)S(1)} %pad_maximum_fusion.refs_0_, bf16[256,512]{1,0:T(8,128)(2,1)} %collective-permute-done.refs_1_, ...), custom_call_target="tpu_custom_call", output_to_operand_aliasing={{0}: (11, {})} | custom-call | flops 10066329600 | bytes 4194304 | tf_op jit(solution)/shard_map/attend/pallas_call | solution.py:186
  53.5 0.5 collective-permute-start.14
  54.1 1.7 %collective-permute-start.8 = (bf16[256,256]{1,0:T(8,128)(2,1)S(1)}, bf16[256,256]{1,0:T(8,128)(2,1)S(1)}, u32[]{:S(2)}, u32[]{:S(2)}) collective-permute-start(bf16[256,256]{1,0:T(8,128)(2,1)S(1)} %get-tuple-element.59), channel_id=1, source_target_pairs={{0,8},{4,12},{8,0},{12,4},{16,24},{20,28},{24,16},{28,20},{1,9},{5... | collective-permute-start | bytes 393224 | tf_op jit(solution)/shard_map/ppermute | solution.py:34
  55.8 0.7 collective-permute-start.9
  56.5 1.1 collective-permute-start.10
  57.7 1.7 %collective-permute-start.15 = (bf16[256,256]{1,0:T(8,128)(2,1)S(1)}, bf16[256,256]{1,0:T(8,128)(2,1)S(1)}, u32[]{:S(2)}, u32[]{:S(2)}) collective-permute-start(bf16[256,256]{1,0:T(8,128)(2,1)S(1)} %get-tuple-element.69), channel_id=1, source_target_pairs={{0,8},{4,12},{8,0},{12,4},{16,24},{20,28},{24,16},{28,20},{1,9},{5... | collective-permute-start | bytes 393224 | tf_op jit(solution)/shard_map/ppermute | solution.py:34
  59.7 2.4 %collective-permute-start.16 = (bf16[256,256]{1,0:T(8,128)(2,1)S(1)}, bf16[256,256]{1,0:T(8,128)(2,1)S(1)}, u32[]{:S(2)}, u32[]{:S(2)}) collective-permute-start(bf16[256,256]{1,0:T(8,128)(2,1)S(1)} %get-tuple-element.70), channel_id=1, source_target_pairs={{0,16},{4,20},{8,24},{12,28},{16,0},{20,4},{24,8},{28,12},{1,17},{... | collective-permute-start | bytes 393224 | tf_op jit(solution)/shard_map/ppermute | solution.py:34
  62.2 1.5 %collective-permute-done.9.refs_2_ = bf16[256,256]{1,0:T(8,128)(2,1)S(1)} collective-permute-done((bf16[256,256]{1,0:T(8,128)(2,1)S(1)}, bf16[256,256]{1,0:T(8,128)(2,1)S(1)}, u32[]{:S(2)}, u32[]{:S(2)}) %collective-permute-start.9) | collective-permute-done | bytes 131104 | tf_op jit(solution)/shard_map/ppermute | solution.py:34
  63.7 1.3 %collective-permute-start.17 = (bf16[256,256]{1,0:T(8,128)(2,1)S(1)}, bf16[256,256]{1,0:T(8,128)(2,1)S(1)}, u32[]{:S(2)}, u32[]{:S(2)}) collective-permute-start(bf16[256,256]{1,0:T(8,128)(2,1)S(1)} %get-tuple-element.71), channel_id=1, source_target_pairs={{0,24},{4,28},{8,16},{12,20},{16,8},{20,12},{24,0},{28,4},{1,25},{... | collective-permute-start | bytes 393224 | tf_op jit(solution)/shard_map/ppermute | solution.py:34
  65.0 1.5 %collective-permute-done.15.refs_5_ = bf16[256,256]{1,0:T(8,128)(2,1)S(1)} collective-permute-done((bf16[256,256]{1,0:T(8,128)(2,1)S(1)}, bf16[256,256]{1,0:T(8,128)(2,1)S(1)}, u32[]{:S(2)}, u32[]{:S(2)}) %collective-permute-start.15) | collective-permute-done | bytes 131104 | tf_op jit(solution)/shard_map/ppermute | solution.py:34
  66.5 1.4 %collective-permute-done.16.refs_6_ = bf16[256,256]{1,0:T(8,128)(2,1)S(1)} collective-permute-done((bf16[256,256]{1,0:T(8,128)(2,1)S(1)}, bf16[256,256]{1,0:T(8,128)(2,1)S(1)}, u32[]{:S(2)}, u32[]{:S(2)}) %collective-permute-start.16) | collective-permute-done | bytes 131104 | tf_op jit(solution)/shard_map/ppermute | solution.py:34
  67.9 1.6 %collective-permute-done.17.refs_7_ = bf16[256,256]{1,0:T(8,128)(2,1)S(1)} collective-permute-done((bf16[256,256]{1,0:T(8,128)(2,1)S(1)}, bf16[256,256]{1,0:T(8,128)(2,1)S(1)}, u32[]{:S(2)}, u32[]{:S(2)}) %collective-permute-start.17) | collective-permute-done | bytes 131104 | tf_op jit(solution)/shard_map/ppermute | solution.py:34
  69.6 0.7 owner_sum.1
  70.3 1.4 %collective-permute-start.26 = (bf16[256,512]{1,0:T(8,128)(2,1)S(1)}, bf16[256,512]{1,0:T(8,128)(2,1)S(1)}, u32[]{:S(2)}, u32[]{:S(2)}) collective-permute-start(bf16[256,512]{1,0:T(8,128)(2,1)S(1)} %get-tuple-element.94.refs_4_), channel_id=1, source_target_pairs={{0,24},{4,28},{8,16},{12,20},{16,8},{20,12},{24,0},{28,4},{1,25},{... | collective-permute-start | bytes 786440 | tf_op jit(solution)/shard_map/ppermute | solution.py:34
  71.7 0.5 collective-permute-start.25
  72.2 1.6 %collective-permute-start.18 = (bf16[64,512]{1,0:T(8,128)(2,1)S(1)}, bf16[64,512]{1,0:T(8,128)(2,1)S(1)}, u32[]{:S(2)}, u32[]{:S(2)}) collective-permute-start(bf16[64,512]{1,0:T(8,128)(2,1)S(1)} %get-tuple-element.73), channel_id=1, source_target_pairs={{0,1},{1,0},{2,3},{3,2},{4,5},{5,4},{6,7},{7,6},{8,9},{9,8},{10,11... | collective-permute-start | bytes 196616 | tf_op jit(solution)/shard_map/ppermute | solution.py:34
  73.8 2.6 %collective-permute-start.19 = (bf16[64,512]{1,0:T(8,128)(2,1)S(1)}, bf16[64,512]{1,0:T(8,128)(2,1)S(1)}, u32[]{:S(2)}, u32[]{:S(2)}) collective-permute-start(bf16[64,512]{1,0:T(8,128)(2,1)S(1)} %get-tuple-element.74), channel_id=1, source_target_pairs={{0,2},{1,3},{2,0},{3,1},{4,6},{5,7},{6,4},{7,5},{8,10},{9,11},{10,... | collective-permute-start | bytes 196616 | tf_op jit(solution)/shard_map/ppermute | solution.py:34
  76.4 0.5 collective-permute-done.18
  76.9 3.2 %collective-permute-start.20 = (bf16[64,512]{1,0:T(8,128)(2,1)S(1)}, bf16[64,512]{1,0:T(8,128)(2,1)S(1)}, u32[]{:S(2)}, u32[]{:S(2)}) collective-permute-start(bf16[64,512]{1,0:T(8,128)(2,1)S(1)} %get-tuple-element.75), channel_id=1, source_target_pairs={{0,3},{1,2},{2,1},{3,0},{4,7},{5,6},{6,5},{7,4},{8,11},{9,10},{10,... | collective-permute-start | bytes 196616 | tf_op jit(solution)/shard_map/ppermute | solution.py:34
  80.3 1.3 %collective-permute-start.24 = (bf16[256,512]{1,0:T(8,128)(2,1)S(1)}, bf16[256,512]{1,0:T(8,128)(2,1)S(1)}, u32[]{:S(2)}, u32[]{:S(2)}) collective-permute-start(bf16[256,512]{1,0:T(8,128)(2,1)S(1)} %get-tuple-element.94.refs_4_), channel_id=1, source_target_pairs={{0,8},{4,12},{8,0},{12,4},{16,24},{20,28},{24,16},{28,20},{1,9},{5... | collective-permute-start | bytes 786440 | tf_op jit(solution)/shard_map/ppermute | solution.py:34
  81.7 1.4 %collective-permute-done.20 = bf16[64,512]{1,0:T(8,128)(2,1)S(1)} collective-permute-done((bf16[64,512]{1,0:T(8,128)(2,1)S(1)}, bf16[64,512]{1,0:T(8,128)(2,1)S(1)}, u32[]{:S(2)}, u32[]{:S(2)}) %collective-permute-start.20) | collective-permute-done | bytes 65568 | tf_op jit(solution)/shard_map/ppermute | solution.py:34
  83.1 1.5 %collective-permute-start.23 = (bf16[4,64,512]{2,1,0:T(8,128)(2,1)S(1)}, bf16[4,64,512]{2,1,0:T(8,128)(2,1)S(1)}, u32[]{:S(2)}, u32[]{:S(2)}) collective-permute-start(bf16[4,64,512]{2,1,0:T(8,128)(2,1)S(1)} %pad_maximum_fusion.1.refs_0_), channel_id=1, source_target_pairs={{0,24},{4,28},{8,16},{12,20},{16,8},{20,12},{24,0},{28,4},{1,25},{... | collective-permute-start | bytes 786440 | tf_op jit(solution)/shard_map/ppermute | solution.py:34
  84.6 1.2 %collective-permute-start.22 = (bf16[4,64,512]{2,1,0:T(8,128)(2,1)S(1)}, bf16[4,64,512]{2,1,0:T(8,128)(2,1)S(1)}, u32[]{:S(2)}, u32[]{:S(2)}) collective-permute-start(bf16[4,64,512]{2,1,0:T(8,128)(2,1)S(1)} %pad_maximum_fusion.1.refs_0_), channel_id=1, source_target_pairs={{0,16},{4,20},{8,24},{12,28},{16,0},{20,4},{24,8},{28,12},{1,17},{... | collective-permute-start | bytes 786440 | tf_op jit(solution)/shard_map/ppermute | solution.py:34
  85.9 0.8 collective-permute-start.21
  86.7 2.9 %collective-permute-done.24.refs_5_ = bf16[256,512]{1,0:T(8,128)(2,1)S(1)} collective-permute-done((bf16[256,512]{1,0:T(8,128)(2,1)S(1)}, bf16[256,512]{1,0:T(8,128)(2,1)S(1)}, u32[]{:S(2)}, u32[]{:S(2)}) %collective-permute-start.24) | collective-permute-done | bytes 262176 | tf_op jit(solution)/shard_map/ppermute | solution.py:34
  89.5 5.2 %collective-permute-done.23.refs_3_ = bf16[4,64,512]{2,1,0:T(8,128)(2,1)S(1)} collective-permute-done((bf16[4,64,512]{2,1,0:T(8,128)(2,1)S(1)}, bf16[4,64,512]{2,1,0:T(8,128)(2,1)S(1)}, u32[]{:S(2)}, u32[]{:S(2)}) %collective-permute-start.23) | collective-permute-done | bytes 262176 | tf_op jit(solution)/shard_map/ppermute | solution.py:34
  94.7 2.1 %collective-permute-done.21.refs_1_ = bf16[4,64,512]{2,1,0:T(8,128)(2,1)S(1)} collective-permute-done((bf16[4,64,512]{2,1,0:T(8,128)(2,1)S(1)}, bf16[4,64,512]{2,1,0:T(8,128)(2,1)S(1)}, u32[]{:S(2)}, u32[]{:S(2)}) %collective-permute-start.21) | collective-permute-done | bytes 262176 | tf_op jit(solution)/shard_map/ppermute | solution.py:34
  96.8 3.8 %input_grad.1 = (bf16[64,1280]{1,0:T(8,128)(2,1)S(1)}, bf16[64,1280]{1,0:T(8,128)(2,1)S(1)}, bf16[64,1280]{1,0:T(8,128)(2,1)S(1)}, bf16[64,1280]{1,0:T(8,128)(2,1)S(1)}) custom-call(s32[2]{0:T(128)S(1)} %pad_add_fusion.place, bf16[4,64,512]{2,1,0:T(8,128)(2,1)S(1)} %pad_maximum_fusion.1.refs_0_, bf16[4,64,512]{2,1,0:T(8,128)(2,1)S(1)} %collective-permute-done.21.refs_1_, ...), custom_call_target="tpu_custom_call" | custom-call | tf_op jit(solution)/shard_map/input_grad/pallas_call | solution.py:337
  100.6 2.1 %weight_grad.1 = (f32[640,512]{1,0:T(8,128)S(1)}, f32[640,512]{1,0:T(8,128)S(1)}) custom-call(s32[2]{0:T(128)S(1)} %pad_add_fusion.place, bf16[256,1280]{1,0:T(8,128)(2,1)S(1)} %get-tuple-element.90.refs_0_, bf16[256,1280]{1,0:T(8,128)(2,1)S(1)} %collective-permute-done.11.refs_1_, bf16[256,1280]{1,0:T(8,128)(2,1)S(1)} %collective-permute-done.12.refs_2_, ...), custom_call_target="tpu_custom_call" | custom-call | tf_op jit(solution)/shard_map/weight_grad/pallas_call | solution.py:283
  102.8 0.6 collective-permute-start.28
  103.4 1.5 %collective-permute-start.29 = (bf16[64,1280]{1,0:T(8,128)(2,1)S(1)}, bf16[64,1280]{1,0:T(8,128)(2,1)S(1)}, u32[]{:S(2)}, u32[]{:S(2)}) collective-permute-start(bf16[64,1280]{1,0:T(8,128)(2,1)S(1)} %get-tuple-element.88), channel_id=1, source_target_pairs={{0,16},{4,20},{8,24},{12,28},{16,0},{20,4},{24,8},{28,12},{1,17},{... | collective-permute-start | bytes 491528 | tf_op jit(solution)/shard_map/ppermute | solution.py:34
  104.9 1.4 %collective-permute-start.30 = (bf16[64,1280]{1,0:T(8,128)(2,1)S(1)}, bf16[64,1280]{1,0:T(8,128)(2,1)S(1)}, u32[]{:S(2)}, u32[]{:S(2)}) collective-permute-start(bf16[64,1280]{1,0:T(8,128)(2,1)S(1)} %get-tuple-element.89), channel_id=1, source_target_pairs={{0,24},{4,28},{8,16},{12,20},{16,8},{20,12},{24,0},{28,4},{1,25},{... | collective-permute-start | bytes 491528 | tf_op jit(solution)/shard_map/ppermute | solution.py:34
  106.4 1.8 %weight_sum.1 = f32[640,2,256]{2,1,0:T(2,128)} custom-call(f32[640,512]{1,0:T(8,128)S(1)} %get-tuple-element.98.keep_ref, f32[640,512]{1,0:T(8,128)S(1)} %collective-permute-done.31.got_ref), custom_call_target="tpu_custom_call" | custom-call | tf_op jit(solution)/shard_map/weight_sum/pallas_call | solution.py:302
  108.2 1.7 %collective-permute-done.28.refs_1_ = bf16[64,1280]{1,0:T(8,128)(2,1)S(1)} collective-permute-done((bf16[64,1280]{1,0:T(8,128)(2,1)S(1)}, bf16[64,1280]{1,0:T(8,128)(2,1)S(1)}, u32[]{:S(2)}, u32[]{:S(2)}) %collective-permute-start.28) | collective-permute-done | bytes 163872 | tf_op jit(solution)/shard_map/ppermute | solution.py:34
  109.9 2.4 %collective-permute-done.29.refs_2_ = bf16[64,1280]{1,0:T(8,128)(2,1)S(1)} collective-permute-done((bf16[64,1280]{1,0:T(8,128)(2,1)S(1)}, bf16[64,1280]{1,0:T(8,128)(2,1)S(1)}, u32[]{:S(2)}, u32[]{:S(2)}) %collective-permute-start.29) | collective-permute-done | bytes 163872 | tf_op jit(solution)/shard_map/ppermute | solution.py:34
  112.2 1.4 %collective-permute-done.30.refs_3_ = bf16[64,1280]{1,0:T(8,128)(2,1)S(1)} collective-permute-done((bf16[64,1280]{1,0:T(8,128)(2,1)S(1)}, bf16[64,1280]{1,0:T(8,128)(2,1)S(1)}, u32[]{:S(2)}, u32[]{:S(2)}) %collective-permute-start.30) | collective-permute-done | bytes 163872 | tf_op jit(solution)/shard_map/ppermute | solution.py:34
  113.6 1.4 %lay_rows.1 = bf16[64,5120]{1,0:T(8,128)(2,1)} custom-call(s32[2]{0:T(128)S(1)} %pad_add_fusion.place, bf16[64,1280]{1,0:T(8,128)(2,1)S(1)} %get-tuple-element.100.refs_0_, bf16[64,1280]{1,0:T(8,128)(2,1)S(1)} %collective-permute-done.28.refs_1_, bf16[64,1280]{1,0:T(8,128)(2,1)S(1)} %collective-permute-done.29.refs_2_, ...), custom_call_target="tpu_custom_call" | custom-call | tf_op jit(solution)/shard_map/lay_rows/pallas_call | solution.py:364
  (37 shorter events, 2.2 us)
Async XLA Ops:
  2.3 11.1 %collective-permute-start.5 = (bf16[256,512]{1,0:T(8,128)(2,1)S(1)}, bf16[256,512]{1,0:T(8,128)(2,1)S(1)}, u32[]{:S(2)}, u32[]{:S(2)}) collective-permute-start(bf16[256,512]{1,0:T(8,128)(2,1)S(1)} %pad_maximum_fusion.refs_0_), channel_id=1, source_target_pairs={{0,24},{4,28},{8,16},{12,20},{16,8},{20,12},{24,0},{28,4},{1,25},{... | collective-permute-start | bytes 786440 | tf_op jit(solution)/shard_map/ppermute | solution.py:34
  6.2 11.9 %collective-permute-start.3 = (bf16[256,512]{1,0:T(8,128)(2,1)S(1)}, bf16[256,512]{1,0:T(8,128)(2,1)S(1)}, u32[]{:S(2)}, u32[]{:S(2)}) collective-permute-start(bf16[256,512]{1,0:T(8,128)(2,1)S(1)} %pad_maximum_fusion.refs_0_), channel_id=1, source_target_pairs={{0,16},{4,20},{8,24},{12,28},{16,0},{20,4},{24,8},{28,12},{1,17},{... | collective-permute-start | bytes 786440 | tf_op jit(solution)/shard_map/ppermute | solution.py:34
  6.7 11.8 %collective-permute-start.1 = (bf16[256,512]{1,0:T(8,128)(2,1)S(1)}, bf16[256,512]{1,0:T(8,128)(2,1)}, u32[]{:S(2)}, u32[]{:S(2)}) collective-permute-start(bf16[256,512]{1,0:T(8,128)(2,1)S(1)} %pad_maximum_fusion.refs_0_), channel_id=1, source_target_pairs={{0,8},{4,12},{8,0},{12,4},{16,24},{20,28},{24,16},{28,20},{1,9},{5... | collective-permute-start | bytes 786440 | tf_op jit(solution)/shard_map/ppermute | solution.py:34
  6.9 13.7 %collective-permute-start = (bf16[256,512]{1,0:T(8,128)(2,1)S(1)}, bf16[256,512]{1,0:T(8,128)(2,1)}, u32[]{:S(2)}, u32[]{:S(2)}) collective-permute-start(bf16[256,512]{1,0:T(8,128)(2,1)S(1)} %pad_maximum_fusion.refs_0_), channel_id=1, source_target_pairs={{0,4},{4,0},{8,12},{12,8},{16,20},{20,16},{24,28},{28,24},{1,5},{5... | collective-permute-start | bytes 786440 | tf_op jit(solution)/shard_map/ppermute | solution.py:34
  9.5 87.4 %collective-permute-start.27 = (bf16[640,2048]{1,0:T(8,128)(2,1)S(1)}, bf16[640,2048]{1,0:T(8,128)(2,1)}, u32[]{:S(2)}, u32[]{:S(2)}) collective-permute-start(bf16[640,2048]{1,0:T(8,128)(2,1)S(1)} %bitcast.19), channel_id=1, source_target_pairs={{0,4},{4,0},{8,12},{12,8},{16,20},{20,16},{24,28},{28,24},{1,5},{5... | collective-permute-start | bytes 7864328 | tf_op jit(solution)/shard_map/ppermute | solution.py:34
  10.1 14.0 %copy-start = (bf16[1,384,1280]{2,1,0:T(8,128)(2,1)S(1)}, bf16[1,384,1280]{2,1,0:T(8,128)(2,1)}, u32[]{:S(2)}) copy-start(bf16[1,384,1280]{2,1,0:T(8,128)(2,1)} %param.5) | copy-start | bytes 2949124
  10.1 14.0 %copy-start.1 = (bf16[1,384,1280]{2,1,0:T(8,128)(2,1)S(1)}, bf16[1,384,1280]{2,1,0:T(8,128)(2,1)}, u32[]{:S(2)}) copy-start(bf16[1,384,1280]{2,1,0:T(8,128)(2,1)} %param.7) | copy-start | bytes 2949124
  13.4 8.9 %collective-permute-start.6 = (bf16[256,512]{1,0:T(8,128)(2,1)S(1)}, bf16[256,512]{1,0:T(8,128)(2,1)S(1)}, u32[]{:S(2)}, u32[]{:S(2)}) collective-permute-start(bf16[256,512]{1,0:T(8,128)(2,1)S(1)} %collective-permute-done.5.refs_6_), channel_id=1, source_target_pairs={{0,4},{4,0},{8,12},{12,8},{16,20},{20,16},{24,28},{28,24},{1,5},{5... | collective-permute-start | bytes 786440 | tf_op jit(solution)/shard_map/ppermute | solution.py:34
  18.2 4.8 %collective-permute-start.4 = (bf16[256,512]{1,0:T(8,128)(2,1)S(1)}, bf16[256,512]{1,0:T(8,128)(2,1)S(1)}, u32[]{:S(2)}, u32[]{:S(2)}) collective-permute-start(bf16[256,512]{1,0:T(8,128)(2,1)S(1)} %collective-permute-done.3.refs_4_), channel_id=1, source_target_pairs={{0,4},{4,0},{8,12},{12,8},{16,20},{20,16},{24,28},{28,24},{1,5},{5... | collective-permute-start | bytes 786440 | tf_op jit(solution)/shard_map/ppermute | solution.py:34
  18.6 5.6 %collective-permute-start.2 = (bf16[256,512]{1,0:T(8,128)(2,1)}, bf16[256,512]{1,0:T(8,128)(2,1)S(1)}, u32[]{:S(2)}, u32[]{:S(2)}) collective-permute-start(bf16[256,512]{1,0:T(8,128)(2,1)} %collective-permute-done.1.refs_2_), channel_id=1, source_target_pairs={{0,4},{4,0},{8,12},{12,8},{16,20},{20,16},{24,28},{28,24},{1,5},{5... | collective-permute-start | bytes 786440 | tf_op jit(solution)/shard_map/ppermute | solution.py:34
  20.5 33.5 %collective-permute-start.11 = (bf16[256,1280]{1,0:T(8,128)(2,1)S(1)}, bf16[256,1280]{1,0:T(8,128)(2,1)S(1)}, u32[]{:S(2)}, u32[]{:S(2)}) collective-permute-start(bf16[256,1280]{1,0:T(8,128)(2,1)S(1)} %get-tuple-element.63), channel_id=1, source_target_pairs={{0,8},{4,12},{8,0},{12,4},{16,24},{20,28},{24,16},{28,20},{1,9},{5... | collective-permute-start | bytes 1966088 | tf_op jit(solution)/shard_map/ppermute | solution.py:34
  22.3 33.5 %collective-permute-start.12 = (bf16[256,1280]{1,0:T(8,128)(2,1)S(1)}, bf16[256,1280]{1,0:T(8,128)(2,1)S(1)}, u32[]{:S(2)}, u32[]{:S(2)}) collective-permute-start(bf16[256,1280]{1,0:T(8,128)(2,1)S(1)} %get-tuple-element.64), channel_id=1, source_target_pairs={{0,16},{4,20},{8,24},{12,28},{16,0},{20,4},{24,8},{28,12},{1,17},{... | collective-permute-start | bytes 1966088 | tf_op jit(solution)/shard_map/ppermute | solution.py:34
  23.0 33.5 %collective-permute-start.13 = (bf16[256,1280]{1,0:T(8,128)(2,1)S(1)}, bf16[256,1280]{1,0:T(8,128)(2,1)S(1)}, u32[]{:S(2)}, u32[]{:S(2)}) collective-permute-start(bf16[256,1280]{1,0:T(8,128)(2,1)S(1)} %get-tuple-element.65), channel_id=1, source_target_pairs={{0,24},{4,28},{8,16},{12,20},{16,8},{20,12},{24,0},{28,4},{1,25},{... | collective-permute-start | bytes 1966088 | tf_op jit(solution)/shard_map/ppermute | solution.py:34
  38.8 14.7 %collective-permute-start.7 = (bf16[4,256,256]{2,1,0:T(8,128)(2,1)S(1)}, bf16[4,256,256]{2,1,0:T(8,128)(2,1)S(1)}, u32[]{:S(2)}, u32[]{:S(2)}) collective-permute-start(bf16[4,256,256]{2,1,0:T(8,128)(2,1)S(1)} %get-tuple-element.57), channel_id=1, source_target_pairs={{0,4},{4,0},{8,12},{12,8},{16,20},{20,16},{24,28},{28,24},{1,5},{5... | collective-permute-start | bytes 1572872 | tf_op jit(solution)/shard_map/ppermute | solution.py:34
  53.5 4.2 %collective-permute-start.14 = (bf16[4,256,256]{2,1,0:T(8,128)(2,1)S(1)}, bf16[4,256,256]{2,1,0:T(8,128)(2,1)S(1)}, u32[]{:S(2)}, u32[]{:S(2)}) collective-permute-start(bf16[4,256,256]{2,1,0:T(8,128)(2,1)S(1)} %get-tuple-element.67), channel_id=1, source_target_pairs={{0,4},{4,0},{8,12},{12,8},{16,20},{20,16},{24,28},{28,24},{1,5},{5... | collective-permute-start | bytes 1572872 | tf_op jit(solution)/shard_map/ppermute | solution.py:34
  54.1 5.7 %collective-permute-start.8 = (bf16[256,256]{1,0:T(8,128)(2,1)S(1)}, bf16[256,256]{1,0:T(8,128)(2,1)S(1)}, u32[]{:S(2)}, u32[]{:S(2)}) collective-permute-start(bf16[256,256]{1,0:T(8,128)(2,1)S(1)} %get-tuple-element.59), channel_id=1, source_target_pairs={{0,8},{4,12},{8,0},{12,4},{16,24},{20,28},{24,16},{28,20},{1,9},{5... | collective-permute-start | bytes 393224 | tf_op jit(solution)/shard_map/ppermute | solution.py:34
  55.8 7.9 %collective-permute-start.9 = (bf16[256,256]{1,0:T(8,128)(2,1)S(1)}, bf16[256,256]{1,0:T(8,128)(2,1)S(1)}, u32[]{:S(2)}, u32[]{:S(2)}) collective-permute-start(bf16[256,256]{1,0:T(8,128)(2,1)S(1)} %get-tuple-element.60), channel_id=1, source_target_pairs={{0,16},{4,20},{8,24},{12,28},{16,0},{20,4},{24,8},{28,12},{1,17},{... | collective-permute-start | bytes 393224 | tf_op jit(solution)/shard_map/ppermute | solution.py:34
  56.5 8.5 %collective-permute-start.10 = (bf16[256,256]{1,0:T(8,128)(2,1)S(1)}, bf16[256,256]{1,0:T(8,128)(2,1)S(1)}, u32[]{:S(2)}, u32[]{:S(2)}) collective-permute-start(bf16[256,256]{1,0:T(8,128)(2,1)S(1)} %get-tuple-element.61), channel_id=1, source_target_pairs={{0,24},{4,28},{8,16},{12,20},{16,8},{20,12},{24,0},{28,4},{1,25},{... | collective-permute-start | bytes 393224 | tf_op jit(solution)/shard_map/ppermute | solution.py:34
  57.7 8.8 %collective-permute-start.15 = (bf16[256,256]{1,0:T(8,128)(2,1)S(1)}, bf16[256,256]{1,0:T(8,128)(2,1)S(1)}, u32[]{:S(2)}, u32[]{:S(2)}) collective-permute-start(bf16[256,256]{1,0:T(8,128)(2,1)S(1)} %get-tuple-element.69), channel_id=1, source_target_pairs={{0,8},{4,12},{8,0},{12,4},{16,24},{20,28},{24,16},{28,20},{1,9},{5... | collective-permute-start | bytes 393224 | tf_op jit(solution)/shard_map/ppermute | solution.py:34
  59.7 8.2 %collective-permute-start.16 = (bf16[256,256]{1,0:T(8,128)(2,1)S(1)}, bf16[256,256]{1,0:T(8,128)(2,1)S(1)}, u32[]{:S(2)}, u32[]{:S(2)}) collective-permute-start(bf16[256,256]{1,0:T(8,128)(2,1)S(1)} %get-tuple-element.70), channel_id=1, source_target_pairs={{0,16},{4,20},{8,24},{12,28},{16,0},{20,4},{24,8},{28,12},{1,17},{... | collective-permute-start | bytes 393224 | tf_op jit(solution)/shard_map/ppermute | solution.py:34
  63.7 5.9 %collective-permute-start.17 = (bf16[256,256]{1,0:T(8,128)(2,1)S(1)}, bf16[256,256]{1,0:T(8,128)(2,1)S(1)}, u32[]{:S(2)}, u32[]{:S(2)}) collective-permute-start(bf16[256,256]{1,0:T(8,128)(2,1)S(1)} %get-tuple-element.71), channel_id=1, source_target_pairs={{0,24},{4,28},{8,16},{12,20},{16,8},{20,12},{24,0},{28,4},{1,25},{... | collective-permute-start | bytes 393224 | tf_op jit(solution)/shard_map/ppermute | solution.py:34
  70.3 14.3 %collective-permute-start.26 = (bf16[256,512]{1,0:T(8,128)(2,1)S(1)}, bf16[256,512]{1,0:T(8,128)(2,1)S(1)}, u32[]{:S(2)}, u32[]{:S(2)}) collective-permute-start(bf16[256,512]{1,0:T(8,128)(2,1)S(1)} %get-tuple-element.94.refs_4_), channel_id=1, source_target_pairs={{0,24},{4,28},{8,16},{12,20},{16,8},{20,12},{24,0},{28,4},{1,25},{... | collective-permute-start | bytes 786440 | tf_op jit(solution)/shard_map/ppermute | solution.py:34
  71.7 14.2 %collective-permute-start.25 = (bf16[256,512]{1,0:T(8,128)(2,1)S(1)}, bf16[256,512]{1,0:T(8,128)(2,1)S(1)}, u32[]{:S(2)}, u32[]{:S(2)}) collective-permute-start(bf16[256,512]{1,0:T(8,128)(2,1)S(1)} %get-tuple-element.94.refs_4_), channel_id=1, source_target_pairs={{0,16},{4,20},{8,24},{12,28},{16,0},{20,4},{24,8},{28,12},{1,17},{... | collective-permute-start | bytes 786440 | tf_op jit(solution)/shard_map/ppermute | solution.py:34
  72.2 4.7 %collective-permute-start.18 = (bf16[64,512]{1,0:T(8,128)(2,1)S(1)}, bf16[64,512]{1,0:T(8,128)(2,1)S(1)}, u32[]{:S(2)}, u32[]{:S(2)}) collective-permute-start(bf16[64,512]{1,0:T(8,128)(2,1)S(1)} %get-tuple-element.73), channel_id=1, source_target_pairs={{0,1},{1,0},{2,3},{3,2},{4,5},{5,4},{6,7},{7,6},{8,9},{9,8},{10,11... | collective-permute-start | bytes 196616 | tf_op jit(solution)/shard_map/ppermute | solution.py:34
  73.8 6.6 %collective-permute-start.19 = (bf16[64,512]{1,0:T(8,128)(2,1)S(1)}, bf16[64,512]{1,0:T(8,128)(2,1)S(1)}, u32[]{:S(2)}, u32[]{:S(2)}) collective-permute-start(bf16[64,512]{1,0:T(8,128)(2,1)S(1)} %get-tuple-element.74), channel_id=1, source_target_pairs={{0,2},{1,3},{2,0},{3,1},{4,6},{5,7},{6,4},{7,5},{8,10},{9,11},{10,... | collective-permute-start | bytes 196616 | tf_op jit(solution)/shard_map/ppermute | solution.py:34
  76.9 6.2 %collective-permute-start.20 = (bf16[64,512]{1,0:T(8,128)(2,1)S(1)}, bf16[64,512]{1,0:T(8,128)(2,1)S(1)}, u32[]{:S(2)}, u32[]{:S(2)}) collective-permute-start(bf16[64,512]{1,0:T(8,128)(2,1)S(1)} %get-tuple-element.75), channel_id=1, source_target_pairs={{0,3},{1,2},{2,1},{3,0},{4,7},{5,6},{6,5},{7,4},{8,11},{9,10},{10,... | collective-permute-start | bytes 196616 | tf_op jit(solution)/shard_map/ppermute | solution.py:34
  80.3 9.2 %collective-permute-start.24 = (bf16[256,512]{1,0:T(8,128)(2,1)S(1)}, bf16[256,512]{1,0:T(8,128)(2,1)S(1)}, u32[]{:S(2)}, u32[]{:S(2)}) collective-permute-start(bf16[256,512]{1,0:T(8,128)(2,1)S(1)} %get-tuple-element.94.refs_4_), channel_id=1, source_target_pairs={{0,8},{4,12},{8,0},{12,4},{16,24},{20,28},{24,16},{28,20},{1,9},{5... | collective-permute-start | bytes 786440 | tf_op jit(solution)/shard_map/ppermute | solution.py:34
  83.1 11.6 %collective-permute-start.23 = (bf16[4,64,512]{2,1,0:T(8,128)(2,1)S(1)}, bf16[4,64,512]{2,1,0:T(8,128)(2,1)S(1)}, u32[]{:S(2)}, u32[]{:S(2)}) collective-permute-start(bf16[4,64,512]{2,1,0:T(8,128)(2,1)S(1)} %pad_maximum_fusion.1.refs_0_), channel_id=1, source_target_pairs={{0,24},{4,28},{8,16},{12,20},{16,8},{20,12},{24,0},{28,4},{1,25},{... | collective-permute-start | bytes 786440 | tf_op jit(solution)/shard_map/ppermute | solution.py:34
  84.6 10.1 %collective-permute-start.22 = (bf16[4,64,512]{2,1,0:T(8,128)(2,1)S(1)}, bf16[4,64,512]{2,1,0:T(8,128)(2,1)S(1)}, u32[]{:S(2)}, u32[]{:S(2)}) collective-permute-start(bf16[4,64,512]{2,1,0:T(8,128)(2,1)S(1)} %pad_maximum_fusion.1.refs_0_), channel_id=1, source_target_pairs={{0,16},{4,20},{8,24},{12,28},{16,0},{20,4},{24,8},{28,12},{1,17},{... | collective-permute-start | bytes 786440 | tf_op jit(solution)/shard_map/ppermute | solution.py:34
  85.9 11.0 %collective-permute-start.21 = (bf16[4,64,512]{2,1,0:T(8,128)(2,1)S(1)}, bf16[4,64,512]{2,1,0:T(8,128)(2,1)S(1)}, u32[]{:S(2)}, u32[]{:S(2)}) collective-permute-start(bf16[4,64,512]{2,1,0:T(8,128)(2,1)S(1)} %pad_maximum_fusion.1.refs_0_), channel_id=1, source_target_pairs={{0,8},{4,12},{8,0},{12,4},{16,24},{20,28},{24,16},{28,20},{1,9},{5... | collective-permute-start | bytes 786440 | tf_op jit(solution)/shard_map/ppermute | solution.py:34
  102.7 3.6 %collective-permute-start.31 = (f32[640,512]{1,0:T(8,128)S(1)}, f32[640,512]{1,0:T(8,128)S(1)}, u32[]{:S(2)}, u32[]{:S(2)}) collective-permute-start(f32[640,512]{1,0:T(8,128)S(1)} %get-tuple-element.99), channel_id=1, source_target_pairs={{0,4},{4,0},{8,12},{12,8},{16,20},{20,16},{24,28},{28,24},{1,5},{5... | collective-permute-start | bytes 3932168 | tf_op jit(solution)/shard_map/ppermute | solution.py:34
  102.8 7.1 %collective-permute-start.28 = (bf16[64,1280]{1,0:T(8,128)(2,1)S(1)}, bf16[64,1280]{1,0:T(8,128)(2,1)S(1)}, u32[]{:S(2)}, u32[]{:S(2)}) collective-permute-start(bf16[64,1280]{1,0:T(8,128)(2,1)S(1)} %get-tuple-element.87), channel_id=1, source_target_pairs={{0,8},{4,12},{8,0},{12,4},{16,24},{20,28},{24,16},{28,20},{1,9},{5... | collective-permute-start | bytes 491528 | tf_op jit(solution)/shard_map/ppermute | solution.py:34
  103.4 8.9 %collective-permute-start.29 = (bf16[64,1280]{1,0:T(8,128)(2,1)S(1)}, bf16[64,1280]{1,0:T(8,128)(2,1)S(1)}, u32[]{:S(2)}, u32[]{:S(2)}) collective-permute-start(bf16[64,1280]{1,0:T(8,128)(2,1)S(1)} %get-tuple-element.88), channel_id=1, source_target_pairs={{0,16},{4,20},{8,24},{12,28},{16,0},{20,4},{24,8},{28,12},{1,17},{... | collective-permute-start | bytes 491528 | tf_op jit(solution)/shard_map/ppermute | solution.py:34
  104.9 8.7 %collective-permute-start.30 = (bf16[64,1280]{1,0:T(8,128)(2,1)S(1)}, bf16[64,1280]{1,0:T(8,128)(2,1)S(1)}, u32[]{:S(2)}, u32[]{:S(2)}) collective-permute-start(bf16[64,1280]{1,0:T(8,128)(2,1)S(1)} %get-tuple-element.89), channel_id=1, source_target_pairs={{0,24},{4,28},{8,16},{12,20},{16,8},{20,12},{24,0},{28,4},{1,25},{... | collective-permute-start | bytes 491528 | tf_op jit(solution)/shard_map/ppermute | solution.py:34

commit v5 on v4

--- a/solution.py
+++ b/solution.py
@@ -278,11 +278,20 @@
 
 def weight_grad(place, columns, gathered):
     half = len(columns)
-    cols = columns[0].shape[1] // 2
-    shape = jax.ShapeDtypeStruct((cols, gathered[0].shape[1]), F32)
+    rows, cols = columns[1].shape
+    features = gathered[0].shape[1]
+    shape = jax.ShapeDtypeStruct((cols // 2, features), F32)
+    full = lambda *shape: pl.BlockSpec(shape, lambda i, s: (0, 0))
     return pl.pallas_call(
         functools.partial(weight_grad_kernel, half),
-        in_specs=[pl.BlockSpec(memory_space=pltpu.SMEM)] + [pl.BlockSpec(memory_space=pltpu.VMEM)] * (2 * half),
+        grid_spec=pltpu.PrefetchScalarGridSpec(
+            num_scalar_prefetch=1,
+            grid=(1,),
+            in_specs=[pl.BlockSpec((rows, cols), lambda i, s: (0, lax.div(s[0], 2)))]
+            + [full(rows, cols)] * (half - 1)
+            + [full(rows, features)] * half,
+            out_specs=[full(*shape.shape)] * 2,
+        ),
         out_shape=[shape, shape],
         compiler_params=params(),
         name="weight_grad",
@@ -394,10 +403,10 @@
     cols = 2 * inputs.shape[1] // n
     columns = [
         lax.dynamic_slice_in_dim(inputs, lax.bitwise_xor(me // 2, k) * cols, cols, axis=1)
-        for k in range(half)
+        for k in range(1, half)
     ]
     columns, near = lax.optimization_barrier((columns, near))
-    columns = across(columns)
+    columns = across([inputs, *columns])
     own_w = w_kv.reshape(w_kv.shape[0], -1)
     other_w = exchange(own_w, 1, "sec")
 

time: 115 us -> 117 us (1.017)
  waiting for transfers between devices: 32.6 us -> 34.1 us
    ppermute x32, waiting for transfers between devices: 32.6 us -> 34.1 us  [exchange(): lax.ppermute(x, axis, [(i, i ^ offset) for i in range(lax.axis_size(axis))])]
    unnamed x5 -> x7, local copies, waits for them, and re-layouts: 2.57 us -> 2.57 us
  transfers between devices with their start and end apart: 32 -> 32, of which waited for: 17 -> 18; matrix products, arithmetic and copies ran while one was open for 4% -> 4% of each run, Pallas kernels for 28% -> 28%
where the time goes in v5:
time: 117 us; the launch traced here: 116 us
  Pallas kernels  39.4 us (34%)
  starting transfers between devices  36.2 us (31%)
  waiting for transfers between devices  34.1 us (29%)
  local copies, waits for them, and re-layouts  5.78 us (5%)
    ppermute x32, starting transfers between devices, exchange(): lax.ppermute(x, axis, [(i, i ^ offset) for i in range(lax.axis_size(axis))])  36.2 us
    ppermute x32, waiting for transfers between devices, exchange(): lax.ppermute(x, axis, [(i, i ^ offset) for i in range(lax.axis_size(axis))])  34.1 us
    pallas_call x2, Pallas kernels, attend(): pl.pallas_call(functools.partial(attend_kernel, n, group, dq is not None)...  29.3 us
    pallas_call x1, Pallas kernels, input_grad(): pl.pallas_call(functools.partial(input_grad_kernel, here // (2 * HD), hal...  3.77 us
    unnamed x7, local copies, waits for them, and re-layouts  2.57 us
  transfers between devices with their start and end apart: 32, of which 18 were waited for; matrix products, arithmetic and copies ran while one was open for 4% of the time, Pallas kernels for 28%

profile of v5, /device:TPU:0, one launch (start us, length us, event | category | flops | bytes accessed | tf_op | source)
XLA Modules:
  0.0 116.4 jit_solution(2373687799746314090)
XLA Ops:
  0.6 1.5 %fusion = (bf16[256,1,128]{2,1,0:T(2,128)(2,1)S(1)}, bf16[256,1,128]{2,1,0:T(2,128)(2,1)S(1)}, bf16[256,1,128]{2,1,0:T(2,128)(2,1)S(1)}, bf16[256,1,128]{2,1,0:T(2,128)(2,1)S(1)}) fusion(bf16[256,2,256]{2,1,0:T(2,128)(2,1)} %param.6), kind=kLoop, calls=%fused_computation.10 | loop fusion | bytes 524288 | tf_op jit(solution)/shard_map/slice | solution.py:398
  2.3 4.0 %collective-permute-start.5 = (bf16[256,512]{1,0:T(8,128)(2,1)S(1)}, bf16[256,512]{1,0:T(8,128)(2,1)S(1)}, u32[]{:S(2)}, u32[]{:S(2)}) collective-permute-start(bf16[256,512]{1,0:T(8,128)(2,1)S(1)} %pad_maximum_fusion.refs_0_), channel_id=1, source_target_pairs={{0,24},{4,28},{8,16},{12,20},{16,8},{20,12},{24,0},{28,4},{1,25},{... | collective-permute-start | bytes 786440 | tf_op jit(solution)/shard_map/ppermute | solution.py:34
  6.9 2.6 %copy.17 = bf16[80,8,2,1024]{3,1,2,0:T(8,128)(2,1)S(1)} copy(bf16[80,8,2,1024]{3,2,1,0:T(2,128)(2,1)} %bitcast.26) | data formatting | bytes 5242880
  9.5 0.6 collective-permute-start.27
  10.1 3.3 %collective-permute-done.5.refs_6_ = bf16[256,512]{1,0:T(8,128)(2,1)S(1)} collective-permute-done((bf16[256,512]{1,0:T(8,128)(2,1)S(1)}, bf16[256,512]{1,0:T(8,128)(2,1)S(1)}, u32[]{:S(2)}, u32[]{:S(2)}) %collective-permute-start.5) | collective-permute-done | bytes 262176 | tf_op jit(solution)/shard_map/ppermute | solution.py:34
  13.4 4.7 %collective-permute-done.3.refs_4_ = bf16[256,512]{1,0:T(8,128)(2,1)S(1)} collective-permute-done((bf16[256,512]{1,0:T(8,128)(2,1)S(1)}, bf16[256,512]{1,0:T(8,128)(2,1)S(1)}, u32[]{:S(2)}, u32[]{:S(2)}) %collective-permute-start.3) | collective-permute-done | bytes 262176 | tf_op jit(solution)/shard_map/ppermute | solution.py:34
  18.7 1.6 %constant_dynamic-slice_fusion = (bf16[256,1280]{1,0:T(8,128)(2,1)S(1)}, bf16[256,1280]{1,0:T(8,128)(2,1)S(1)}, bf16[256,1280]{1,0:T(8,128)(2,1)S(1)}) fusion(bf16[256,5120]{1,0:T(8,128)(2,1)} %refs_0_.1, s32[]{:T(128)S(6)} %select_n.19, s32[]{:T(128)S(6)} %select_n.18, s32[]{:T(128)S(6)} %select_n.17), kind=kLoop, calls=%fused_computation.6 | loop fusion | bytes 3932172 | tf_op jit(solution)/shard_map/dynamic_slice | solution.py:405
  20.3 1.7 %collective-permute-start.11 = (bf16[256,1280]{1,0:T(8,128)(2,1)S(1)}, bf16[256,1280]{1,0:T(8,128)(2,1)S(1)}, u32[]{:S(2)}, u32[]{:S(2)}) collective-permute-start(bf16[256,1280]{1,0:T(8,128)(2,1)S(1)} %get-tuple-element.62), channel_id=1, source_target_pairs={{0,8},{4,12},{8,0},{12,4},{16,24},{20,28},{24,16},{28,20},{1,9},{5... | collective-permute-start | bytes 1966088 | tf_op jit(solution)/shard_map/ppermute | solution.py:34
  22.1 0.7 collective-permute-start.12
  22.8 1.1 collective-permute-start.13
  23.9 14.6 %attend.2 = (bf16[384,1280]{1,0:T(8,128)(2,1)}, f32[4,256,256]{2,1,0:T(8,128)S(1)}, bf16[4,256,256]{2,1,0:T(8,128)(2,1)S(1)}) custom-call(s32[2]{0:T(128)S(1)} %pad_add_fusion.place, bf16[256,512]{1,0:T(8,128)(2,1)S(1)} %pad_maximum_fusion.refs_0_, bf16[256,512]{1,0:T(8,128)(2,1)} %collective-permute-done.refs_1_, ...), custom_call_target="tpu_custom_call" | custom-call | flops 10066329600 | bytes 4194304 | tf_op jit(solution)/shard_map/attend/pallas_call | solution.py:186
  38.5 14.7 %attend.3 = (bf16[384,1280]{1,0:T(8,128)(2,1)}, f32[4,256,256]{2,1,0:T(8,128)S(1)}, bf16[4,256,256]{2,1,0:T(8,128)(2,1)S(1)}) custom-call(s32[2]{0:T(128)S(1)} %pad_add_fusion.place, bf16[256,512]{1,0:T(8,128)(2,1)S(1)} %pad_maximum_fusion.refs_0_, bf16[256,512]{1,0:T(8,128)(2,1)} %collective-permute-done.refs_1_, ...), custom_call_target="tpu_custom_call", output_to_operand_aliasing={{0}: (11, {})} | custom-call | flops 10066329600 | bytes 4194304 | tf_op jit(solution)/shard_map/attend/pallas_call | solution.py:186
  53.2 0.5 collective-permute-start.7
  53.7 1.4 %collective-permute-done.14.got_ref = bf16[4,256,256]{2,1,0:T(8,128)(2,1)S(1)} collective-permute-done((bf16[4,256,256]{2,1,0:T(8,128)(2,1)S(1)}, bf16[4,256,256]{2,1,0:T(8,128)(2,1)S(1)}, u32[]{:S(2)}, u32[]{:S(2)}) %collective-permute-start.14) | collective-permute-done | bytes 524320 | tf_op jit(solution)/shard_map/ppermute | solution.py:34
  55.2 1.7 %collective-permute-start.15 = (bf16[256,256]{1,0:T(8,128)(2,1)S(1)}, bf16[256,256]{1,0:T(8,128)(2,1)S(1)}, u32[]{:S(2)}, u32[]{:S(2)}) collective-permute-start(bf16[256,256]{1,0:T(8,128)(2,1)S(1)} %get-tuple-element.68), channel_id=1, source_target_pairs={{0,8},{4,12},{8,0},{12,4},{16,24},{20,28},{24,16},{28,20},{1,9},{5... | collective-permute-start | bytes 393224 | tf_op jit(solution)/shard_map/ppermute | solution.py:34
  56.9 0.7 collective-permute-start.16
  57.6 1.1 collective-permute-start.17
  58.9 1.7 %collective-permute-start.8 = (bf16[256,256]{1,0:T(8,128)(2,1)S(1)}, bf16[256,256]{1,0:T(8,128)(2,1)S(1)}, u32[]{:S(2)}, u32[]{:S(2)}) collective-permute-start(bf16[256,256]{1,0:T(8,128)(2,1)S(1)} %get-tuple-element.58), channel_id=1, source_target_pairs={{0,8},{4,12},{8,0},{12,4},{16,24},{20,28},{24,16},{28,20},{1,9},{5... | collective-permute-start | bytes 393224 | tf_op jit(solution)/shard_map/ppermute | solution.py:34
  61.0 2.3 %collective-permute-start.9 = (bf16[256,256]{1,0:T(8,128)(2,1)S(1)}, bf16[256,256]{1,0:T(8,128)(2,1)S(1)}, u32[]{:S(2)}, u32[]{:S(2)}) collective-permute-start(bf16[256,256]{1,0:T(8,128)(2,1)S(1)} %get-tuple-element.59), channel_id=1, source_target_pairs={{0,16},{4,20},{8,24},{12,28},{16,0},{20,4},{24,8},{28,12},{1,17},{... | collective-permute-start | bytes 393224 | tf_op jit(solution)/shard_map/ppermute | solution.py:34
  63.3 1.5 %collective-permute-done.16.refs_6_ = bf16[256,256]{1,0:T(8,128)(2,1)S(1)} collective-permute-done((bf16[256,256]{1,0:T(8,128)(2,1)S(1)}, bf16[256,256]{1,0:T(8,128)(2,1)S(1)}, u32[]{:S(2)}, u32[]{:S(2)}) %collective-permute-start.16) | collective-permute-done | bytes 131104 | tf_op jit(solution)/shard_map/ppermute | solution.py:34
  64.8 1.4 %collective-permute-start.10 = (bf16[256,256]{1,0:T(8,128)(2,1)S(1)}, bf16[256,256]{1,0:T(8,128)(2,1)S(1)}, u32[]{:S(2)}, u32[]{:S(2)}) collective-permute-start(bf16[256,256]{1,0:T(8,128)(2,1)S(1)} %get-tuple-element.60), channel_id=1, source_target_pairs={{0,24},{4,28},{8,16},{12,20},{16,8},{20,12},{24,0},{28,4},{1,25},{... | collective-permute-start | bytes 393224 | tf_op jit(solution)/shard_map/ppermute | solution.py:34
  66.2 1.4 %collective-permute-done.8.refs_1_ = bf16[256,256]{1,0:T(8,128)(2,1)S(1)} collective-permute-done((bf16[256,256]{1,0:T(8,128)(2,1)S(1)}, bf16[256,256]{1,0:T(8,128)(2,1)S(1)}, u32[]{:S(2)}, u32[]{:S(2)}) %collective-permute-start.8) | collective-permute-done | bytes 131104 | tf_op jit(solution)/shard_map/ppermute | solution.py:34
  67.7 1.5 %collective-permute-done.9.refs_2_ = bf16[256,256]{1,0:T(8,128)(2,1)S(1)} collective-permute-done((bf16[256,256]{1,0:T(8,128)(2,1)S(1)}, bf16[256,256]{1,0:T(8,128)(2,1)S(1)}, u32[]{:S(2)}, u32[]{:S(2)}) %collective-permute-start.9) | collective-permute-done | bytes 131104 | tf_op jit(solution)/shard_map/ppermute | solution.py:34
  69.2 1.5 %collective-permute-done.10.refs_3_ = bf16[256,256]{1,0:T(8,128)(2,1)S(1)} collective-permute-done((bf16[256,256]{1,0:T(8,128)(2,1)S(1)}, bf16[256,256]{1,0:T(8,128)(2,1)S(1)}, u32[]{:S(2)}, u32[]{:S(2)}) %collective-permute-start.10) | collective-permute-done | bytes 131104 | tf_op jit(solution)/shard_map/ppermute | solution.py:34
  70.7 0.7 owner_sum.1
  71.4 1.5 %collective-permute-start.26 = (bf16[256,512]{1,0:T(8,128)(2,1)S(1)}, bf16[256,512]{1,0:T(8,128)(2,1)S(1)}, u32[]{:S(2)}, u32[]{:S(2)}) collective-permute-start(bf16[256,512]{1,0:T(8,128)(2,1)S(1)} %get-tuple-element.92.refs_4_), channel_id=1, source_target_pairs={{0,24},{4,28},{8,16},{12,20},{16,8},{20,12},{24,0},{28,4},{1,25},{... | collective-permute-start | bytes 786440 | tf_op jit(solution)/shard_map/ppermute | solution.py:34
  73.3 1.7 %collective-permute-start.18 = (bf16[64,512]{1,0:T(8,128)(2,1)S(1)}, bf16[64,512]{1,0:T(8,128)(2,1)S(1)}, u32[]{:S(2)}, u32[]{:S(2)}) collective-permute-start(bf16[64,512]{1,0:T(8,128)(2,1)S(1)} %get-tuple-element.72), channel_id=1, source_target_pairs={{0,1},{1,0},{2,3},{3,2},{4,5},{5,4},{6,7},{7,6},{8,9},{9,8},{10,11... | collective-permute-start | bytes 196616 | tf_op jit(solution)/shard_map/ppermute | solution.py:34
  75.0 2.6 %collective-permute-start.19 = (bf16[64,512]{1,0:T(8,128)(2,1)S(1)}, bf16[64,512]{1,0:T(8,128)(2,1)S(1)}, u32[]{:S(2)}, u32[]{:S(2)}) collective-permute-start(bf16[64,512]{1,0:T(8,128)(2,1)S(1)} %get-tuple-element.73), channel_id=1, source_target_pairs={{0,2},{1,3},{2,0},{3,1},{4,6},{5,7},{6,4},{7,5},{8,10},{9,11},{10,... | collective-permute-start | bytes 196616 | tf_op jit(solution)/shard_map/ppermute | solution.py:34
  77.6 0.6 collective-permute-done.18
  78.2 3.1 %collective-permute-start.20 = (bf16[64,512]{1,0:T(8,128)(2,1)S(1)}, bf16[64,512]{1,0:T(8,128)(2,1)S(1)}, u32[]{:S(2)}, u32[]{:S(2)}) collective-permute-start(bf16[64,512]{1,0:T(8,128)(2,1)S(1)} %get-tuple-element.74), channel_id=1, source_target_pairs={{0,3},{1,2},{2,1},{3,0},{4,7},{5,6},{6,5},{7,4},{8,11},{9,10},{10,... | collective-permute-start | bytes 196616 | tf_op jit(solution)/shard_map/ppermute | solution.py:34
  81.7 1.2 %collective-permute-start.24 = (bf16[256,512]{1,0:T(8,128)(2,1)S(1)}, bf16[256,512]{1,0:T(8,128)(2,1)S(1)}, u32[]{:S(2)}, u32[]{:S(2)}) collective-permute-start(bf16[256,512]{1,0:T(8,128)(2,1)S(1)} %get-tuple-element.92.refs_4_), channel_id=1, source_target_pairs={{0,8},{4,12},{8,0},{12,4},{16,24},{20,28},{24,16},{28,20},{1,9},{5... | collective-permute-start | bytes 786440 | tf_op jit(solution)/shard_map/ppermute | solution.py:34
  82.9 1.4 %collective-permute-done.20 = bf16[64,512]{1,0:T(8,128)(2,1)S(1)} collective-permute-done((bf16[64,512]{1,0:T(8,128)(2,1)S(1)}, bf16[64,512]{1,0:T(8,128)(2,1)S(1)}, u32[]{:S(2)}, u32[]{:S(2)}) %collective-permute-start.20) | collective-permute-done | bytes 65568 | tf_op jit(solution)/shard_map/ppermute | solution.py:34
  84.3 1.7 %collective-permute-start.23 = (bf16[4,64,512]{2,1,0:T(8,128)(2,1)S(1)}, bf16[4,64,512]{2,1,0:T(8,128)(2,1)S(1)}, u32[]{:S(2)}, u32[]{:S(2)}) collective-permute-start(bf16[4,64,512]{2,1,0:T(8,128)(2,1)S(1)} %pad_maximum_fusion.1.refs_0_), channel_id=1, source_target_pairs={{0,24},{4,28},{8,16},{12,20},{16,8},{20,12},{24,0},{28,4},{1,25},{... | collective-permute-start | bytes 786440 | tf_op jit(solution)/shard_map/ppermute | solution.py:34
  86.0 0.9 collective-permute-start.22
  86.9 0.9 collective-permute-start.21
  87.9 3.0 %collective-permute-done.24.refs_5_ = bf16[256,512]{1,0:T(8,128)(2,1)S(1)} collective-permute-done((bf16[256,512]{1,0:T(8,128)(2,1)S(1)}, bf16[256,512]{1,0:T(8,128)(2,1)S(1)}, u32[]{:S(2)}, u32[]{:S(2)}) %collective-permute-start.24) | collective-permute-done | bytes 262176 | tf_op jit(solution)/shard_map/ppermute | solution.py:34
  90.9 5.0 %collective-permute-done.23.refs_3_ = bf16[4,64,512]{2,1,0:T(8,128)(2,1)S(1)} collective-permute-done((bf16[4,64,512]{2,1,0:T(8,128)(2,1)S(1)}, bf16[4,64,512]{2,1,0:T(8,128)(2,1)S(1)}, u32[]{:S(2)}, u32[]{:S(2)}) %collective-permute-start.23) | collective-permute-done | bytes 262176 | tf_op jit(solution)/shard_map/ppermute | solution.py:34
  95.9 2.2 %collective-permute-done.21.refs_1_ = bf16[4,64,512]{2,1,0:T(8,128)(2,1)S(1)} collective-permute-done((bf16[4,64,512]{2,1,0:T(8,128)(2,1)S(1)}, bf16[4,64,512]{2,1,0:T(8,128)(2,1)S(1)}, u32[]{:S(2)}, u32[]{:S(2)}) %collective-permute-start.21) | collective-permute-done | bytes 262176 | tf_op jit(solution)/shard_map/ppermute | solution.py:34
  98.2 3.8 %input_grad.1 = (bf16[64,1280]{1,0:T(8,128)(2,1)S(1)}, bf16[64,1280]{1,0:T(8,128)(2,1)S(1)}, bf16[64,1280]{1,0:T(8,128)(2,1)S(1)}, bf16[64,1280]{1,0:T(8,128)(2,1)S(1)}) custom-call(s32[2]{0:T(128)S(1)} %pad_add_fusion.place, bf16[4,64,512]{2,1,0:T(8,128)(2,1)S(1)} %pad_maximum_fusion.1.refs_0_, bf16[4,64,512]{2,1,0:T(8,128)(2,1)S(1)} %collective-permute-done.21.refs_1_, ...), custom_call_target="tpu_custom_call" | custom-call | tf_op jit(solution)/shard_map/input_grad/pallas_call | solution.py:346
  101.9 2.1 %weight_grad.1 = (f32[640,512]{1,0:T(8,128)S(1)}, f32[640,512]{1,0:T(8,128)S(1)}) custom-call(s32[2]{0:T(128)S(1)} %pad_add_fusion.place, bf16[256,5120]{1,0:T(8,128)(2,1)S(1)} %copy-done, bf16[256,1280]{1,0:T(8,128)(2,1)S(1)} %collective-permute-done.11.refs_1_, bf16[256,1280]{1,0:T(8,128)(2,1)S(1)} %collective-permute-done.12.refs_2_, ...), custom_call_target="tpu_custom_call" | custom-call | tf_op jit(solution)/shard_map/weight_grad/pallas_call | solution.py:285
  104.1 0.5 collective-permute-start.28
  104.7 1.6 %collective-permute-start.29 = (bf16[64,1280]{1,0:T(8,128)(2,1)S(1)}, bf16[64,1280]{1,0:T(8,128)(2,1)S(1)}, u32[]{:S(2)}, u32[]{:S(2)}) collective-permute-start(bf16[64,1280]{1,0:T(8,128)(2,1)S(1)} %get-tuple-element.87), channel_id=1, source_target_pairs={{0,16},{4,20},{8,24},{12,28},{16,0},{20,4},{24,8},{28,12},{1,17},{... | collective-permute-start | bytes 491528 | tf_op jit(solution)/shard_map/ppermute | solution.py:34
  106.3 1.4 %collective-permute-start.30 = (bf16[64,1280]{1,0:T(8,128)(2,1)S(1)}, bf16[64,1280]{1,0:T(8,128)(2,1)S(1)}, u32[]{:S(2)}, u32[]{:S(2)}) collective-permute-start(bf16[64,1280]{1,0:T(8,128)(2,1)S(1)} %get-tuple-element.88), channel_id=1, source_target_pairs={{0,24},{4,28},{8,16},{12,20},{16,8},{20,12},{24,0},{28,4},{1,25},{... | collective-permute-start | bytes 491528 | tf_op jit(solution)/shard_map/ppermute | solution.py:34
  107.7 1.8 %weight_sum.1 = f32[640,2,256]{2,1,0:T(2,128)} custom-call(f32[640,512]{1,0:T(8,128)S(1)} %get-tuple-element.96.keep_ref, f32[640,512]{1,0:T(8,128)S(1)} %collective-permute-done.31.got_ref), custom_call_target="tpu_custom_call" | custom-call | tf_op jit(solution)/shard_map/weight_sum/pallas_call | solution.py:311
  109.5 1.7 %collective-permute-done.28.refs_1_ = bf16[64,1280]{1,0:T(8,128)(2,1)S(1)} collective-permute-done((bf16[64,1280]{1,0:T(8,128)(2,1)S(1)}, bf16[64,1280]{1,0:T(8,128)(2,1)S(1)}, u32[]{:S(2)}, u32[]{:S(2)}) %collective-permute-start.28) | collective-permute-done | bytes 163872 | tf_op jit(solution)/shard_map/ppermute | solution.py:34
  111.2 2.4 %collective-permute-done.29.refs_2_ = bf16[64,1280]{1,0:T(8,128)(2,1)S(1)} collective-permute-done((bf16[64,1280]{1,0:T(8,128)(2,1)S(1)}, bf16[64,1280]{1,0:T(8,128)(2,1)S(1)}, u32[]{:S(2)}, u32[]{:S(2)}) %collective-permute-start.29) | collective-permute-done | bytes 163872 | tf_op jit(solution)/shard_map/ppermute | solution.py:34
  113.6 1.3 %collective-permute-done.30.refs_3_ = bf16[64,1280]{1,0:T(8,128)(2,1)S(1)} collective-permute-done((bf16[64,1280]{1,0:T(8,128)(2,1)S(1)}, bf16[64,1280]{1,0:T(8,128)(2,1)S(1)}, u32[]{:S(2)}, u32[]{:S(2)}) %collective-permute-start.30) | collective-permute-done | bytes 163872 | tf_op jit(solution)/shard_map/ppermute | solution.py:34
  114.9 1.4 %lay_rows.1 = bf16[64,5120]{1,0:T(8,128)(2,1)} custom-call(s32[2]{0:T(128)S(1)} %pad_add_fusion.place, bf16[64,1280]{1,0:T(8,128)(2,1)S(1)} %get-tuple-element.98.refs_0_, bf16[64,1280]{1,0:T(8,128)(2,1)S(1)} %collective-permute-done.28.refs_1_, bf16[64,1280]{1,0:T(8,128)(2,1)S(1)} %collective-permute-done.29.refs_2_, ...), custom_call_target="tpu_custom_call" | custom-call | tf_op jit(solution)/shard_map/lay_rows/pallas_call | solution.py:373
  (39 shorter events, 2.9 us)
Async XLA Ops:
  2.3 11.1 %collective-permute-start.5 = (bf16[256,512]{1,0:T(8,128)(2,1)S(1)}, bf16[256,512]{1,0:T(8,128)(2,1)S(1)}, u32[]{:S(2)}, u32[]{:S(2)}) collective-permute-start(bf16[256,512]{1,0:T(8,128)(2,1)S(1)} %pad_maximum_fusion.refs_0_), channel_id=1, source_target_pairs={{0,24},{4,28},{8,16},{12,20},{16,8},{20,12},{24,0},{28,4},{1,25},{... | collective-permute-start | bytes 786440 | tf_op jit(solution)/shard_map/ppermute | solution.py:34
  6.2 11.9 %collective-permute-start.3 = (bf16[256,512]{1,0:T(8,128)(2,1)S(1)}, bf16[256,512]{1,0:T(8,128)(2,1)S(1)}, u32[]{:S(2)}, u32[]{:S(2)}) collective-permute-start(bf16[256,512]{1,0:T(8,128)(2,1)S(1)} %pad_maximum_fusion.refs_0_), channel_id=1, source_target_pairs={{0,16},{4,20},{8,24},{12,28},{16,0},{20,4},{24,8},{28,12},{1,17},{... | collective-permute-start | bytes 786440 | tf_op jit(solution)/shard_map/ppermute | solution.py:34
  6.7 11.8 %collective-permute-start.1 = (bf16[256,512]{1,0:T(8,128)(2,1)S(1)}, bf16[256,512]{1,0:T(8,128)(2,1)}, u32[]{:S(2)}, u32[]{:S(2)}) collective-permute-start(bf16[256,512]{1,0:T(8,128)(2,1)S(1)} %pad_maximum_fusion.refs_0_), channel_id=1, source_target_pairs={{0,8},{4,12},{8,0},{12,4},{16,24},{20,28},{24,16},{28,20},{1,9},{5... | collective-permute-start | bytes 786440 | tf_op jit(solution)/shard_map/ppermute | solution.py:34
  6.9 13.4 %collective-permute-start = (bf16[256,512]{1,0:T(8,128)(2,1)S(1)}, bf16[256,512]{1,0:T(8,128)(2,1)}, u32[]{:S(2)}, u32[]{:S(2)}) collective-permute-start(bf16[256,512]{1,0:T(8,128)(2,1)S(1)} %pad_maximum_fusion.refs_0_), channel_id=1, source_target_pairs={{0,4},{4,0},{8,12},{12,8},{16,20},{20,16},{24,28},{28,24},{1,5},{5... | collective-permute-start | bytes 786440 | tf_op jit(solution)/shard_map/ppermute | solution.py:34
  9.5 88.7 %collective-permute-start.27 = (bf16[640,2048]{1,0:T(8,128)(2,1)S(1)}, bf16[640,2048]{1,0:T(8,128)(2,1)}, u32[]{:S(2)}, u32[]{:S(2)}) collective-permute-start(bf16[640,2048]{1,0:T(8,128)(2,1)S(1)} %bitcast.19), channel_id=1, source_target_pairs={{0,4},{4,0},{8,12},{12,8},{16,20},{20,16},{24,28},{28,24},{1,5},{5... | collective-permute-start | bytes 7864328 | tf_op jit(solution)/shard_map/ppermute | solution.py:34
  10.0 13.9 %copy-start.1 = (bf16[1,384,1280]{2,1,0:T(8,128)(2,1)S(1)}, bf16[1,384,1280]{2,1,0:T(8,128)(2,1)}, u32[]{:S(2)}) copy-start(bf16[1,384,1280]{2,1,0:T(8,128)(2,1)} %param.5) | copy-start | bytes 2949124
  10.0 13.9 %copy-start.2 = (bf16[1,384,1280]{2,1,0:T(8,128)(2,1)S(1)}, bf16[1,384,1280]{2,1,0:T(8,128)(2,1)}, u32[]{:S(2)}) copy-start(bf16[1,384,1280]{2,1,0:T(8,128)(2,1)} %param.7) | copy-start | bytes 2949124
  13.4 8.6 %collective-permute-start.6 = (bf16[256,512]{1,0:T(8,128)(2,1)S(1)}, bf16[256,512]{1,0:T(8,128)(2,1)S(1)}, u32[]{:S(2)}, u32[]{:S(2)}) collective-permute-start(bf16[256,512]{1,0:T(8,128)(2,1)S(1)} %collective-permute-done.5.refs_6_), channel_id=1, source_target_pairs={{0,4},{4,0},{8,12},{12,8},{16,20},{20,16},{24,28},{28,24},{1,5},{5... | collective-permute-start | bytes 786440 | tf_op jit(solution)/shard_map/ppermute | solution.py:34
  18.2 4.6 %collective-permute-start.4 = (bf16[256,512]{1,0:T(8,128)(2,1)S(1)}, bf16[256,512]{1,0:T(8,128)(2,1)S(1)}, u32[]{:S(2)}, u32[]{:S(2)}) collective-permute-start(bf16[256,512]{1,0:T(8,128)(2,1)S(1)} %collective-permute-done.3.refs_4_), channel_id=1, source_target_pairs={{0,4},{4,0},{8,12},{12,8},{16,20},{20,16},{24,28},{28,24},{1,5},{5... | collective-permute-start | bytes 786440 | tf_op jit(solution)/shard_map/ppermute | solution.py:34
  18.6 5.3 %collective-permute-start.2 = (bf16[256,512]{1,0:T(8,128)(2,1)}, bf16[256,512]{1,0:T(8,128)(2,1)S(1)}, u32[]{:S(2)}, u32[]{:S(2)}) collective-permute-start(bf16[256,512]{1,0:T(8,128)(2,1)} %collective-permute-done.1.refs_2_), channel_id=1, source_target_pairs={{0,4},{4,0},{8,12},{12,8},{16,20},{20,16},{24,28},{28,24},{1,5},{5... | collective-permute-start | bytes 786440 | tf_op jit(solution)/shard_map/ppermute | solution.py:34
  20.3 32.9 %collective-permute-start.11 = (bf16[256,1280]{1,0:T(8,128)(2,1)S(1)}, bf16[256,1280]{1,0:T(8,128)(2,1)S(1)}, u32[]{:S(2)}, u32[]{:S(2)}) collective-permute-start(bf16[256,1280]{1,0:T(8,128)(2,1)S(1)} %get-tuple-element.62), channel_id=1, source_target_pairs={{0,8},{4,12},{8,0},{12,4},{16,24},{20,28},{24,16},{28,20},{1,9},{5... | collective-permute-start | bytes 1966088 | tf_op jit(solution)/shard_map/ppermute | solution.py:34
  22.1 31.7 %collective-permute-start.12 = (bf16[256,1280]{1,0:T(8,128)(2,1)S(1)}, bf16[256,1280]{1,0:T(8,128)(2,1)S(1)}, u32[]{:S(2)}, u32[]{:S(2)}) collective-permute-start(bf16[256,1280]{1,0:T(8,128)(2,1)S(1)} %get-tuple-element.63), channel_id=1, source_target_pairs={{0,16},{4,20},{8,24},{12,28},{16,0},{20,4},{24,8},{28,12},{1,17},{... | collective-permute-start | bytes 1966088 | tf_op jit(solution)/shard_map/ppermute | solution.py:34
  22.8 31.0 %collective-permute-start.13 = (bf16[256,1280]{1,0:T(8,128)(2,1)S(1)}, bf16[256,1280]{1,0:T(8,128)(2,1)S(1)}, u32[]{:S(2)}, u32[]{:S(2)}) collective-permute-start(bf16[256,1280]{1,0:T(8,128)(2,1)S(1)} %get-tuple-element.64), channel_id=1, source_target_pairs={{0,24},{4,28},{8,16},{12,20},{16,8},{20,12},{24,0},{28,4},{1,25},{... | collective-permute-start | bytes 1966088 | tf_op jit(solution)/shard_map/ppermute | solution.py:34
  53.2 1.9 %collective-permute-start.14 = (bf16[4,256,256]{2,1,0:T(8,128)(2,1)S(1)}, bf16[4,256,256]{2,1,0:T(8,128)(2,1)S(1)}, u32[]{:S(2)}, u32[]{:S(2)}) collective-permute-start(bf16[4,256,256]{2,1,0:T(8,128)(2,1)S(1)} %get-tuple-element.66), channel_id=1, source_target_pairs={{0,4},{4,0},{8,12},{12,8},{16,20},{20,16},{24,28},{28,24},{1,5},{5... | collective-permute-start | bytes 1572872 | tf_op jit(solution)/shard_map/ppermute | solution.py:34
  53.2 5.6 %collective-permute-start.7 = (bf16[4,256,256]{2,1,0:T(8,128)(2,1)S(1)}, bf16[4,256,256]{2,1,0:T(8,128)(2,1)S(1)}, u32[]{:S(2)}, u32[]{:S(2)}) collective-permute-start(bf16[4,256,256]{2,1,0:T(8,128)(2,1)S(1)} %get-tuple-element.56), channel_id=1, source_target_pairs={{0,4},{4,0},{8,12},{12,8},{16,20},{20,16},{24,28},{28,24},{1,5},{5... | collective-permute-start | bytes 1572872 | tf_op jit(solution)/shard_map/ppermute | solution.py:34
  55.2 5.8 %collective-permute-start.15 = (bf16[256,256]{1,0:T(8,128)(2,1)S(1)}, bf16[256,256]{1,0:T(8,128)(2,1)S(1)}, u32[]{:S(2)}, u32[]{:S(2)}) collective-permute-start(bf16[256,256]{1,0:T(8,128)(2,1)S(1)} %get-tuple-element.68), channel_id=1, source_target_pairs={{0,8},{4,12},{8,0},{12,4},{16,24},{20,28},{24,16},{28,20},{1,9},{5... | collective-permute-start | bytes 393224 | tf_op jit(solution)/shard_map/ppermute | solution.py:34
  56.9 7.9 %collective-permute-start.16 = (bf16[256,256]{1,0:T(8,128)(2,1)S(1)}, bf16[256,256]{1,0:T(8,128)(2,1)S(1)}, u32[]{:S(2)}, u32[]{:S(2)}) collective-permute-start(bf16[256,256]{1,0:T(8,128)(2,1)S(1)} %get-tuple-element.69), channel_id=1, source_target_pairs={{0,16},{4,20},{8,24},{12,28},{16,0},{20,4},{24,8},{28,12},{1,17},{... | collective-permute-start | bytes 393224 | tf_op jit(solution)/shard_map/ppermute | solution.py:34
  57.6 8.6 %collective-permute-start.17 = (bf16[256,256]{1,0:T(8,128)(2,1)S(1)}, bf16[256,256]{1,0:T(8,128)(2,1)S(1)}, u32[]{:S(2)}, u32[]{:S(2)}) collective-permute-start(bf16[256,256]{1,0:T(8,128)(2,1)S(1)} %get-tuple-element.70), channel_id=1, source_target_pairs={{0,24},{4,28},{8,16},{12,20},{16,8},{20,12},{24,0},{28,4},{1,25},{... | collective-permute-start | bytes 393224 | tf_op jit(solution)/shard_map/ppermute | solution.py:34
  58.9 8.8 %collective-permute-start.8 = (bf16[256,256]{1,0:T(8,128)(2,1)S(1)}, bf16[256,256]{1,0:T(8,128)(2,1)S(1)}, u32[]{:S(2)}, u32[]{:S(2)}) collective-permute-start(bf16[256,256]{1,0:T(8,128)(2,1)S(1)} %get-tuple-element.58), channel_id=1, source_target_pairs={{0,8},{4,12},{8,0},{12,4},{16,24},{20,28},{24,16},{28,20},{1,9},{5... | collective-permute-start | bytes 393224 | tf_op jit(solution)/shard_map/ppermute | solution.py:34
  61.0 8.2 %collective-permute-start.9 = (bf16[256,256]{1,0:T(8,128)(2,1)S(1)}, bf16[256,256]{1,0:T(8,128)(2,1)S(1)}, u32[]{:S(2)}, u32[]{:S(2)}) collective-permute-start(bf16[256,256]{1,0:T(8,128)(2,1)S(1)} %get-tuple-element.59), channel_id=1, source_target_pairs={{0,16},{4,20},{8,24},{12,28},{16,0},{20,4},{24,8},{28,12},{1,17},{... | collective-permute-start | bytes 393224 | tf_op jit(solution)/shard_map/ppermute | solution.py:34
  64.8 5.9 %collective-permute-start.10 = (bf16[256,256]{1,0:T(8,128)(2,1)S(1)}, bf16[256,256]{1,0:T(8,128)(2,1)S(1)}, u32[]{:S(2)}, u32[]{:S(2)}) collective-permute-start(bf16[256,256]{1,0:T(8,128)(2,1)S(1)} %get-tuple-element.60), channel_id=1, source_target_pairs={{0,24},{4,28},{8,16},{12,20},{16,8},{20,12},{24,0},{28,4},{1,25},{... | collective-permute-start | bytes 393224 | tf_op jit(solution)/shard_map/ppermute | solution.py:34
  71.4 14.6 %collective-permute-start.26 = (bf16[256,512]{1,0:T(8,128)(2,1)S(1)}, bf16[256,512]{1,0:T(8,128)(2,1)S(1)}, u32[]{:S(2)}, u32[]{:S(2)}) collective-permute-start(bf16[256,512]{1,0:T(8,128)(2,1)S(1)} %get-tuple-element.92.refs_4_), channel_id=1, source_target_pairs={{0,24},{4,28},{8,16},{12,20},{16,8},{20,12},{24,0},{28,4},{1,25},{... | collective-permute-start | bytes 786440 | tf_op jit(solution)/shard_map/ppermute | solution.py:34
  72.9 14.0 %collective-permute-start.25 = (bf16[256,512]{1,0:T(8,128)(2,1)S(1)}, bf16[256,512]{1,0:T(8,128)(2,1)S(1)}, u32[]{:S(2)}, u32[]{:S(2)}) collective-permute-start(bf16[256,512]{1,0:T(8,128)(2,1)S(1)} %get-tuple-element.92.refs_4_), channel_id=1, source_target_pairs={{0,16},{4,20},{8,24},{12,28},{16,0},{20,4},{24,8},{28,12},{1,17},{... | collective-permute-start | bytes 786440 | tf_op jit(solution)/shard_map/ppermute | solution.py:34
  73.3 4.9 %collective-permute-start.18 = (bf16[64,512]{1,0:T(8,128)(2,1)S(1)}, bf16[64,512]{1,0:T(8,128)(2,1)S(1)}, u32[]{:S(2)}, u32[]{:S(2)}) collective-permute-start(bf16[64,512]{1,0:T(8,128)(2,1)S(1)} %get-tuple-element.72), channel_id=1, source_target_pairs={{0,1},{1,0},{2,3},{3,2},{4,5},{5,4},{6,7},{7,6},{8,9},{9,8},{10,11... | collective-permute-start | bytes 196616 | tf_op jit(solution)/shard_map/ppermute | solution.py:34
  75.0 6.7 %collective-permute-start.19 = (bf16[64,512]{1,0:T(8,128)(2,1)S(1)}, bf16[64,512]{1,0:T(8,128)(2,1)S(1)}, u32[]{:S(2)}, u32[]{:S(2)}) collective-permute-start(bf16[64,512]{1,0:T(8,128)(2,1)S(1)} %get-tuple-element.73), channel_id=1, source_target_pairs={{0,2},{1,3},{2,0},{3,1},{4,6},{5,7},{6,4},{7,5},{8,10},{9,11},{10,... | collective-permute-start | bytes 196616 | tf_op jit(solution)/shard_map/ppermute | solution.py:34
  78.2 6.1 %collective-permute-start.20 = (bf16[64,512]{1,0:T(8,128)(2,1)S(1)}, bf16[64,512]{1,0:T(8,128)(2,1)S(1)}, u32[]{:S(2)}, u32[]{:S(2)}) collective-permute-start(bf16[64,512]{1,0:T(8,128)(2,1)S(1)} %get-tuple-element.74), channel_id=1, source_target_pairs={{0,3},{1,2},{2,1},{3,0},{4,7},{5,6},{6,5},{7,4},{8,11},{9,10},{10,... | collective-permute-start | bytes 196616 | tf_op jit(solution)/shard_map/ppermute | solution.py:34
  81.7 9.2 %collective-permute-start.24 = (bf16[256,512]{1,0:T(8,128)(2,1)S(1)}, bf16[256,512]{1,0:T(8,128)(2,1)S(1)}, u32[]{:S(2)}, u32[]{:S(2)}) collective-permute-start(bf16[256,512]{1,0:T(8,128)(2,1)S(1)} %get-tuple-element.92.refs_4_), channel_id=1, source_target_pairs={{0,8},{4,12},{8,0},{12,4},{16,24},{20,28},{24,16},{28,20},{1,9},{5... | collective-permute-start | bytes 786440 | tf_op jit(solution)/shard_map/ppermute | solution.py:34
  84.3 17.6 %copy-start = (bf16[256,5120]{1,0:T(8,128)(2,1)S(1)}, bf16[256,5120]{1,0:T(8,128)(2,1)}, u32[]{:S(2)}) copy-start(bf16[256,5120]{1,0:T(8,128)(2,1)} %refs_0_.1) | copy-start | bytes 7864324
  84.3 11.6 %collective-permute-start.23 = (bf16[4,64,512]{2,1,0:T(8,128)(2,1)S(1)}, bf16[4,64,512]{2,1,0:T(8,128)(2,1)S(1)}, u32[]{:S(2)}, u32[]{:S(2)}) collective-permute-start(bf16[4,64,512]{2,1,0:T(8,128)(2,1)S(1)} %pad_maximum_fusion.1.refs_0_), channel_id=1, source_target_pairs={{0,24},{4,28},{8,16},{12,20},{16,8},{20,12},{24,0},{28,4},{1,25},{... | collective-permute-start | bytes 786440 | tf_op jit(solution)/shard_map/ppermute | solution.py:34
  86.0 9.9 %collective-permute-start.22 = (bf16[4,64,512]{2,1,0:T(8,128)(2,1)S(1)}, bf16[4,64,512]{2,1,0:T(8,128)(2,1)S(1)}, u32[]{:S(2)}, u32[]{:S(2)}) collective-permute-start(bf16[4,64,512]{2,1,0:T(8,128)(2,1)S(1)} %pad_maximum_fusion.1.refs_0_), channel_id=1, source_target_pairs={{0,16},{4,20},{8,24},{12,28},{16,0},{20,4},{24,8},{28,12},{1,17},{... | collective-permute-start | bytes 786440 | tf_op jit(solution)/shard_map/ppermute | solution.py:34
  86.9 11.2 %collective-permute-start.21 = (bf16[4,64,512]{2,1,0:T(8,128)(2,1)S(1)}, bf16[4,64,512]{2,1,0:T(8,128)(2,1)S(1)}, u32[]{:S(2)}, u32[]{:S(2)}) collective-permute-start(bf16[4,64,512]{2,1,0:T(8,128)(2,1)S(1)} %pad_maximum_fusion.1.refs_0_), channel_id=1, source_target_pairs={{0,8},{4,12},{8,0},{12,4},{16,24},{20,28},{24,16},{28,20},{1,9},{5... | collective-permute-start | bytes 786440 | tf_op jit(solution)/shard_map/ppermute | solution.py:34
  104.1 3.6 %collective-permute-start.31 = (f32[640,512]{1,0:T(8,128)S(1)}, f32[640,512]{1,0:T(8,128)S(1)}, u32[]{:S(2)}, u32[]{:S(2)}) collective-permute-start(f32[640,512]{1,0:T(8,128)S(1)} %get-tuple-element.97), channel_id=1, source_target_pairs={{0,4},{4,0},{8,12},{12,8},{16,20},{20,16},{24,28},{28,24},{1,5},{5... | collective-permute-start | bytes 3932168 | tf_op jit(solution)/shard_map/ppermute | solution.py:34
  104.1 7.1 %collective-permute-start.28 = (bf16[64,1280]{1,0:T(8,128)(2,1)S(1)}, bf16[64,1280]{1,0:T(8,128)(2,1)S(1)}, u32[]{:S(2)}, u32[]{:S(2)}) collective-permute-start(bf16[64,1280]{1,0:T(8,128)(2,1)S(1)} %get-tuple-element.86), channel_id=1, source_target_pairs={{0,8},{4,12},{8,0},{12,4},{16,24},{20,28},{24,16},{28,20},{1,9},{5... | collective-permute-start | bytes 491528 | tf_op jit(solution)/shard_map/ppermute | solution.py:34
  104.7 8.9 %collective-permute-start.29 = (bf16[64,1280]{1,0:T(8,128)(2,1)S(1)}, bf16[64,1280]{1,0:T(8,128)(2,1)S(1)}, u32[]{:S(2)}, u32[]{:S(2)}) collective-permute-start(bf16[64,1280]{1,0:T(8,128)(2,1)S(1)} %get-tuple-element.87), channel_id=1, source_target_pairs={{0,16},{4,20},{8,24},{12,28},{16,0},{20,4},{24,8},{28,12},{1,17},{... | collective-permute-start | bytes 491528 | tf_op jit(solution)/shard_map/ppermute | solution.py:34
  106.3 8.6 %collective-permute-start.30 = (bf16[64,1280]{1,0:T(8,128)(2,1)S(1)}, bf16[64,1280]{1,0:T(8,128)(2,1)S(1)}, u32[]{:S(2)}, u32[]{:S(2)}) collective-permute-start(bf16[64,1280]{1,0:T(8,128)(2,1)S(1)} %get-tuple-element.88), channel_id=1, source_target_pairs={{0,24},{4,28},{8,16},{12,20},{16,8},{20,12},{24,0},{28,4},{1,25},{... | collective-permute-start | bytes 491528 | tf_op jit(solution)/shard_map/ppermute | solution.py:34
